TPU v7x, 256 devices: a whole 4x4x8 slice. The times are simulated.
256 devices in a mesh: chan: 32 (over z, y), tm: 8 (over x, core).
Axes of the slice: x: 4, y: 4, z: 8, core: 2. Of those that a mesh axis runs over, the one named last changes fastest.
Arguments:
- intensity: bfloat16 [2, 16384, 4096], P(None, 'chan', 'tm'), may hold values from -6 to 6
- channel_scale: float32 [16384], P('chan'), may hold values from 0.5 to 2
- box_widths: int32 [6], replicated, may hold values from 1 to 64, as said below
Outputs:
- snr: float32 [2, 6, 2048, 4096], P(None, None, 'chan', 'tm')
Inputs may be any that keep to these rules, and one draw needn't show every extreme that they name: `box_widths`: distinct and increasing; the first is 1 and the last is 2 ** 6.
All inputs are finite; a program needn't handle non-finite values.
Results may differ from a plain program's by a relative error of at most 0.0003.
Values may be sent and summed in bfloat16 or wider, within the bound.
No kernel may reach another device: no remote copies, remote signals or barrier semaphores. Data moves between devices by JAX's collectives and lax.ppermute only.
A program may use at most 64 MiB of HBM per device.

v0:
```python
import jax
import jax.numpy as jnp
from jax import lax
from jax.experimental import pallas as pl
from jax.experimental.pallas import tpu as pltpu
from jax.sharding import PartitionSpec as P

BEAMS = 2
CHANS = 512
SPAN = 512
PARTS = 32
SEGMENTS = 8
ROWS = 64
WIDE = SPAN + 128
NBOX = 6
LANES = 128
REACH = 5


def split3(x):
    first = x.astype(jnp.bfloat16)
    rest = x - first.astype(jnp.float32)
    second = rest.astype(jnp.bfloat16)
    third = (rest - second.astype(jnp.float32)).astype(jnp.bfloat16)
    return first, second, third


def roll(x, shift):
    return x if isinstance(shift, int) and shift == 0 else pltpu.roll(x, shift, 1)


def merge_groups(groups):
    merged = []
    for upper, lower in zip(groups[0::2], groups[1::2]):
        trials = []
        for e in range(len(upper)):
            early = roll(upper[e], e)
            trials += [lower[e] + early, lower[e] + roll(early, 1)]
        merged.append(trials)
    return merged


def put(ref, start, stride, rows):
    for c in range(rows.shape[1] // LANES):
        ref[c, pl.ds(start, 8, stride=stride), :] = rows[:, c * LANES : (c + 1) * LANES]


def take(ref, start, count, first, last):
    chunks = [ref[c, pl.ds(start, count), :] for c in range(first, last)]
    return jnp.concatenate(chunks, axis=1)


def merge_rows(groups, one, two):
    tiles = WIDE // LANES
    while len(groups) > 1:
        groups = merge_groups(groups)
    for e in range(8):
        put(one, e, 8, groups[0][e])
    source, target = one, two
    trials = 8
    while trials < ROWS:
        for base in range(0, ROWS, 2 * trials):
            for a in range(0, trials, 8):
                upper = take(source, base + a, 8, 0, tiles)
                lower = take(source, base + trials + a, 8, 0, tiles)
                early = pltpu.roll(upper, a, 1, stride=1, stride_axis=0)
                late = pltpu.roll(early, 1, 1)
                put(target, base + 2 * a, 2, lower + early)
                put(target, base + 2 * a + 1, 2, lower + late)
        source, target = target, source
        trials *= 2
    return source


def local_kernel(q_ref, scale_ref, x_ref, o0, o1, o2, o3, o4, one, two, delayed):
    q = q_ref[0]
    row = lax.broadcasted_iota(jnp.int32, (ROWS, CHANS), 0)
    col = lax.broadcasted_iota(jnp.int32, (ROWS, CHANS), 1)
    member = (row & 7) * 8 + (row >> 3) == col >> 3
    weights = jnp.where(member, scale_ref[...], 0.0)
    x = x_ref[0]
    base = None
    for part in split3(weights):
        term = jnp.dot(part, x, preferred_element_type=jnp.float32)
        base = term if base is None else base + term
    blank = jnp.zeros((8, LANES), jnp.float32)
    groups = [
        [jnp.concatenate([base[8 * g : 8 * g + 8], blank], axis=1)] for g in range(8)
    ]
    plane = merge_rows(groups, one, two)
    delayed[...] = jnp.zeros_like(delayed)
    extent = WIDE + 2 * LANES
    pair = lax.broadcasted_iota(jnp.int32, (8, extent), 0) >> 1
    more = jnp.zeros((8, 2 * LANES), jnp.float32)
    for a in range(8):
        rows = jnp.concatenate(
            [take(plane, 8 * a, 8, 0, WIDE // LANES), more], axis=1
        )
        rows = jnp.where(pair & 1 != 0, pltpu.roll(rows, 2 * q, 1), rows)
        rows = jnp.where(pair & 2 != 0, pltpu.roll(rows, 4 * q, 1), rows)
        delay = 8 * q * a
        rows = pltpu.roll(rows, delay & (LANES - 1), 1)
        start = pl.multiple_of(delay - (delay & (LANES - 1)), LANES)
        delayed[pl.ds(8 * a, 8), pl.ds(start, extent)] = rows
    for k, out in enumerate((o0, o1, o2, o3, o4)):
        first = 16 * max(k - 1, 0)
        out[0] = delayed[pl.ds(first, ROWS - first), pl.ds(SPAN * k, SPAN)]


def local_plane(x, scale, q):
    counts = [ROWS - 16 * max(k - 1, 0) for k in range(REACH)]
    return pl.pallas_call(
        local_kernel,
        grid=(BEAMS,),
        in_specs=[
            pl.BlockSpec(memory_space=pltpu.SMEM),
            pl.BlockSpec((1, CHANS), lambda b: (0, 0)),
            pl.BlockSpec((1, CHANS, SPAN), lambda b: (b, 0, 0)),
        ],
        out_specs=[pl.BlockSpec((1, n, SPAN), lambda b: (b, 0, 0)) for n in counts],
        out_shape=[
            jax.ShapeDtypeStruct((BEAMS, n, SPAN), jnp.float32) for n in counts
        ],
        scratch_shapes=[
            pltpu.VMEM((WIDE // LANES, ROWS, LANES), jnp.float32),
            pltpu.VMEM((WIDE // LANES, ROWS, LANES), jnp.float32),
            pltpu.VMEM((ROWS, REACH * SPAN), jnp.float32),
        ],
        compiler_params=pltpu.CompilerParams(vmem_limit_bytes=24 << 20),
        name="local_plane",
    )(q, scale, x)


def gather_kernel(o0, r1, r2, r3, r4, out, held):
    for b in range(BEAMS):
        for a in range(0, ROWS, 16):
            total = o0[b, pl.ds(a, 16), :] + r1[b, pl.ds(a, 16), :]
            for k, received in ((2, r2), (3, r3), (4, r4)):
                first = 16 * (k - 1)
                if a >= first:
                    total = total + received[b, pl.ds(a - first, 16), :]
            for c in range(SPAN // LANES):
                held[c, pl.ds(a, 16), :] = total[:, c * LANES : (c + 1) * LANES]
        for c in range(SPAN // LANES):
            for i in range(2):
                out[pl.ds(b * 8 + c * 2 + i, PARTS, stride=16), :] = held[
                    c, pl.ds(i, PARTS, stride=2), :
                ]


def gather_shifted(pieces):
    return pl.pallas_call(
        gather_kernel,
        out_shape=jax.ShapeDtypeStruct((PARTS * 16, LANES), jnp.float32),
        scratch_shapes=[pltpu.VMEM((SPAN // LANES, ROWS, LANES), jnp.float32)],
        compiler_params=pltpu.CompilerParams(vmem_limit_bytes=24 << 20),
        name="gather_shifted",
    )(*pieces)


def final_kernel(x_ref, main, tail, one, two):
    blank = jnp.zeros((8, LANES), jnp.float32)
    lane = lax.broadcasted_iota(jnp.int32, (ROWS, LANES), 1)
    for b in range(BEAMS):
        groups = []
        for g in range(4):
            trials = []
            for e in range(2):
                chunks = [
                    x_ref[pl.ds(g * 16 + b * 8 + c * 2 + e, 8, stride=64), :]
                    for c in range(SPAN // LANES)
                ]
                trials.append(jnp.concatenate(chunks + [blank], axis=1))
            groups.append(trials)
        plane = merge_rows(groups, one, two)
        main[b] = take(plane, 0, ROWS, 0, SPAN // LANES)
        tail[b] = jnp.where(
            lane < LANES // 2,
            plane[SPAN // LANES],
            plane[SPAN // LANES - 1],
        )


def final_plane(x):
    return pl.pallas_call(
        final_kernel,
        out_shape=[
            jax.ShapeDtypeStruct((BEAMS, ROWS, SPAN), jnp.float32),
            jax.ShapeDtypeStruct((BEAMS, ROWS, LANES), jnp.float32),
        ],
        scratch_shapes=[
            pltpu.VMEM((WIDE // LANES, ROWS, LANES), jnp.float32),
            pltpu.VMEM((WIDE // LANES, ROWS, LANES), jnp.float32),
        ],
        compiler_params=pltpu.CompilerParams(vmem_limit_bytes=24 << 20),
        name="final_plane",
    )(x)


def boxcar_kernel(widths, main, tail, out, bands):
    @pl.when(pl.program_id(0) == 0)
    def _():
        u = lax.broadcasted_iota(jnp.int32, (2 * LANES, LANES), 0)
        t = lax.broadcasted_iota(jnp.int32, (2 * LANES, LANES), 1)
        ago = t + LANES - u
        for k in range(NBOX):
            inside = jnp.logical_and(ago >= 0, ago < widths[k])
            bands[:, pl.ds(k * LANES, LANES)] = jnp.where(inside, 1.0, 0.0).astype(
                jnp.bfloat16
            )

    lane = lax.broadcasted_iota(jnp.int32, (ROWS, LANES), 1)
    edge = tail[0]
    chunks = [jnp.where(lane >= LANES // 2, edge, 0.0)]
    for c in range(SPAN // LANES):
        chunks.append(main[0, :, pl.ds(c * LANES, LANES)])
    chunks[1] = chunks[1] + jnp.where(lane < LANES // 2, edge, 0.0)
    parts = [split3(chunk) for chunk in chunks]
    norms = [
        lax.rsqrt(
            jnp.full((ROWS, LANES), widths[k] * (CHANS * PARTS), jnp.int32).astype(
                jnp.float32
            )
        )
        for k in range(NBOX)
    ]
    for c in range(SPAN // LANES):
        total = None
        for before, here in zip(parts[c], parts[c + 1]):
            window = jnp.concatenate([before, here], axis=1)
            term = jnp.dot(window, bands[...], preferred_element_type=jnp.float32)
            total = term if total is None else total + term
        for k in range(NBOX):
            out[0, k, :, pl.ds(c * LANES, LANES)] = (
                total[:, k * LANES : (k + 1) * LANES] * norms[k]
            )


def boxcars(main, tail, widths):
    return pl.pallas_call(
        boxcar_kernel,
        grid=(BEAMS,),
        in_specs=[
            pl.BlockSpec(memory_space=pltpu.SMEM),
            pl.BlockSpec((1, ROWS, SPAN), lambda b: (b, 0, 0)),
            pl.BlockSpec((1, ROWS, LANES), lambda b: (b, 0, 0)),
        ],
        out_specs=pl.BlockSpec((1, NBOX, ROWS, SPAN), lambda b: (b, 0, 0, 0)),
        out_shape=jax.ShapeDtypeStruct((BEAMS, NBOX, ROWS, SPAN), jnp.float32),
        scratch_shapes=[pltpu.VMEM((2 * LANES, NBOX * LANES), jnp.bfloat16)],
        compiler_params=pltpu.CompilerParams(vmem_limit_bytes=24 << 20),
        name="boxcars",
    )(widths, main, tail)


def later(block, distance):
    route = [(i, i + distance) for i in range(SEGMENTS - distance)]
    return lax.ppermute(block, "tm", route)


def per_device(intensity, channel_scale, box_widths):
    q = (PARTS - 1 - lax.axis_index("chan")).astype(jnp.int32).reshape(1)
    pieces = list(local_plane(intensity, channel_scale.reshape(1, CHANS), q))
    for k in range(REACH - 1, 0, -1):
        pieces[k] = later(pieces[k], k)
    lined = gather_shifted(pieces)
    lined = lax.all_to_all(lined, "chan", 0, 0, tiled=True)
    main, tail = final_plane(lined)
    return boxcars(main, later(tail, 1), box_widths)


def solution(mesh):
    in_specs = (P(None, "chan", "tm"), P("chan"), P())
    out_specs = P(None, None, "chan", "tm")
    return jax.shard_map(
        per_device, mesh=mesh, in_specs=in_specs, out_specs=out_specs, check_vma=False
    )
```

profile of v0, /device:TPU:4, one launch (start us, length us, event | category | flops | bytes accessed | tf_op | source)
XLA Modules:
  0.0 55.7 jit_solution(4189645155366127420)
XLA Ops:
  0.0 0.0 copy-start.2
  0.0 0.0 copy-start
  0.0 1.2 %copy-done = bf16[2,512,512]{2,1,0:T(8,128)(2,1)S(1)} copy-done((bf16[2,512,512]{2,1,0:T(8,128)(2,1)S(1)}, bf16[2,512,512]{2,1,0:T(8,128)(2,1)}, u32[]{:S(2)}) %copy-start) | copy-done | bytes 1048600
  1.2 0.0 copy-start.1
  1.2 0.7 %copy-done.1 = f32[512]{0:T(512)S(1)} copy-done((f32[512]{0:T(512)S(1)}, f32[512]{0:T(512)}, u32[]{:S(2)}) %copy-start.1) | copy-done | bytes 2072
  1.9 3.1 %local_plane.1 = (f32[2,64,512]{2,1,0:T(8,128)S(1)}, f32[2,64,512]{2,1,0:T(8,128)S(1)}, f32[2,48,512]{2,1,0:T(8,128)S(1)}, f32[2,32,512]{2,1,0:T(8,128)S(1)}, f32[2,16,512]{2,1,0:T(8,128)S(1)}) custom-call(s32[1]{0:T(128)} %bitcast.q_ref, f32[1,512]{1,0:T(1,128)S(1)} %bitcast.6, bf16[2,512,512]{2,1,0:T(8,128)(2,1)S(1)} %copy-done), custom_call_target="tpu_custom_call" | custom-call | tf_op jit(solution)/shard_map/local_plane/pallas_call | solution.py:112
  5.1 1.9 %collective-permute-start = (f32[2,64,512]{2,1,0:T(8,128)S(1)}, f32[2,64,512]{2,1,0:T(8,128)S(1)}, u32[]{:S(2)}, u32[]{:S(2)}) collective-permute-start(f32[2,64,512]{2,1,0:T(8,128)S(1)} %get-tuple-element.13), channel_id=1, source_target_pairs={{0,1},{1,2},{2,3},{3,4},{4,5},{5,6},{6,7},{8,9},{9,10},{10,11},{11... | collective-permute-start | bytes 786440 | tf_op jit(solution)/shard_map/ppermute | solution.py:258
  7.0 3.1 %collective-permute-start.1 = (f32[2,48,512]{2,1,0:T(8,128)S(1)}, f32[2,48,512]{2,1,0:T(8,128)S(1)}, u32[]{:S(2)}, u32[]{:S(2)}) collective-permute-start(f32[2,48,512]{2,1,0:T(8,128)S(1)} %get-tuple-element.14), channel_id=1, source_target_pairs={{0,2},{1,3},{2,4},{3,5},{4,6},{5,7},{8,10},{9,11},{10,12},{11,13},... | collective-permute-start | bytes 589832 | tf_op jit(solution)/shard_map/ppermute | solution.py:258
  10.1 1.9 %collective-permute-start.2 = (f32[2,32,512]{2,1,0:T(8,128)S(1)}, f32[2,32,512]{2,1,0:T(8,128)S(1)}, u32[]{:S(2)}, u32[]{:S(2)}) collective-permute-start(f32[2,32,512]{2,1,0:T(8,128)S(1)} %get-tuple-element.15), channel_id=1, source_target_pairs={{0,3},{1,4},{2,5},{3,6},{4,7},{8,11},{9,12},{10,13},{11,14},{12,15... | collective-permute-start | bytes 393224 | tf_op jit(solution)/shard_map/ppermute | solution.py:258
  12.0 1.3 %collective-permute-start.3 = (f32[2,16,512]{2,1,0:T(8,128)S(1)}, f32[2,16,512]{2,1,0:T(8,128)S(1)}, u32[]{:S(2)}, u32[]{:S(2)}) collective-permute-start(f32[2,16,512]{2,1,0:T(8,128)S(1)} %get-tuple-element.16), channel_id=1, source_target_pairs={{0,4},{1,5},{2,6},{3,7},{8,12},{9,13},{10,14},{11,15},{16,20},{17,... | collective-permute-start | bytes 196616 | tf_op jit(solution)/shard_map/ppermute | solution.py:258
  13.3 7.5 %collective-permute-done.3.r4 = f32[2,16,512]{2,1,0:T(8,128)S(1)} collective-permute-done((f32[2,16,512]{2,1,0:T(8,128)S(1)}, f32[2,16,512]{2,1,0:T(8,128)S(1)}, u32[]{:S(2)}, u32[]{:S(2)}) %collective-permute-start.3) | collective-permute-done | bytes 65568 | tf_op jit(solution)/shard_map/ppermute | solution.py:258
  20.9 0.0 collective-permute-done.2.r3
  20.9 0.0 collective-permute-done.1.r2
  20.9 0.0 collective-permute-done.r1
  20.9 0.2 gather_shifted.1
  21.0 24.5 %all_to_all.11 = f32[32,16,128]{2,1,0:T(8,128)S(1)} all-to-all(f32[32,16,128]{2,1,0:T(8,128)S(1)} %bitcast.5), channel_id=1, replica_groups=mesh['chan'=32,'tm'=8] {'chan'}, dimensions={0} | all-to-all | bytes 524288 | tf_op jit(solution)/shard_map/all_to_all | solution.py:267
  45.6 1.1 %final_plane.1 = (f32[2,64,512]{2,1,0:T(8,128)S(1)}, f32[2,64,128]{2,1,0:T(8,128)S(1)}) custom-call(f32[512,128]{1,0:T(8,128)S(1)} %bitcast.4), custom_call_target="tpu_custom_call" | custom-call | tf_op jit(solution)/shard_map/final_plane/pallas_call | solution.py:185
  46.7 1.9 %collective-permute-start.4 = (f32[2,64,128]{2,1,0:T(8,128)S(1)}, f32[2,64,128]{2,1,0:T(8,128)S(1)}, u32[]{:S(2)}, u32[]{:S(2)}) collective-permute-start(f32[2,64,128]{2,1,0:T(8,128)S(1)} %get-tuple-element.18), channel_id=1, source_target_pairs={{0,1},{1,2},{2,3},{3,4},{4,5},{5,6},{6,7},{8,9},{9,10},{10,11},{11... | collective-permute-start | bytes 196616 | tf_op jit(solution)/shard_map/ppermute | solution.py:258
  48.6 3.7 %collective-permute-done.4.tail = f32[2,64,128]{2,1,0:T(8,128)S(1)} collective-permute-done((f32[2,64,128]{2,1,0:T(8,128)S(1)}, f32[2,64,128]{2,1,0:T(8,128)S(1)}, u32[]{:S(2)}, u32[]{:S(2)}) %collective-permute-start.4) | collective-permute-done | bytes 65568 | tf_op jit(solution)/shard_map/ppermute | solution.py:258
  52.3 0.0 copy-done.2
  52.3 3.4 %boxcars.1 = f32[2,6,64,512]{3,2,1,0:T(8,128)} custom-call(s32[6]{0:T(128)S(1)} %copy-done.2, f32[2,64,512]{2,1,0:T(8,128)S(1)} %get-tuple-element.17.main, f32[2,64,128]{2,1,0:T(8,128)S(1)} %collective-permute-done.4.tail), custom_call_target="tpu_custom_call" | custom-call | tf_op jit(solution)/shard_map/boxcars/pallas_call | solution.py:240
Async XLA Ops:
  0.0 52.3 %copy-start.2 = (s32[6]{0:T(128)S(1)}, s32[6]{0:T(128)}, u32[]{:S(2)}) copy-start(s32[6]{0:T(128)} %widths.1) | copy-start | bytes 76
  0.0 1.2 %copy-start = (bf16[2,512,512]{2,1,0:T(8,128)(2,1)S(1)}, bf16[2,512,512]{2,1,0:T(8,128)(2,1)}, u32[]{:S(2)}) copy-start(bf16[2,512,512]{2,1,0:T(8,128)(2,1)} %x_ref.1) | copy-start | bytes 3145732
  1.2 0.7 %copy-start.1 = (f32[512]{0:T(512)S(1)}, f32[512]{0:T(512)}, u32[]{:S(2)}) copy-start(f32[512]{0:T(512)} %param.4) | copy-start | bytes 6148
  5.1 15.8 %collective-permute-start = (f32[2,64,512]{2,1,0:T(8,128)S(1)}, f32[2,64,512]{2,1,0:T(8,128)S(1)}, u32[]{:S(2)}, u32[]{:S(2)}) collective-permute-start(f32[2,64,512]{2,1,0:T(8,128)S(1)} %get-tuple-element.13), channel_id=1, source_target_pairs={{0,1},{1,2},{2,3},{3,4},{4,5},{5,6},{6,7},{8,9},{9,10},{10,11},{11... | collective-permute-start | bytes 786440 | tf_op jit(solution)/shard_map/ppermute | solution.py:258
  7.0 13.9 %collective-permute-start.1 = (f32[2,48,512]{2,1,0:T(8,128)S(1)}, f32[2,48,512]{2,1,0:T(8,128)S(1)}, u32[]{:S(2)}, u32[]{:S(2)}) collective-permute-start(f32[2,48,512]{2,1,0:T(8,128)S(1)} %get-tuple-element.14), channel_id=1, source_target_pairs={{0,2},{1,3},{2,4},{3,5},{4,6},{5,7},{8,10},{9,11},{10,12},{11,13},... | collective-permute-start | bytes 589832 | tf_op jit(solution)/shard_map/ppermute | solution.py:258
  10.1 10.8 %collective-permute-start.2 = (f32[2,32,512]{2,1,0:T(8,128)S(1)}, f32[2,32,512]{2,1,0:T(8,128)S(1)}, u32[]{:S(2)}, u32[]{:S(2)}) collective-permute-start(f32[2,32,512]{2,1,0:T(8,128)S(1)} %get-tuple-element.15), channel_id=1, source_target_pairs={{0,3},{1,4},{2,5},{3,6},{4,7},{8,11},{9,12},{10,13},{11,14},{12,15... | collective-permute-start | bytes 393224 | tf_op jit(solution)/shard_map/ppermute | solution.py:258
  12.0 8.8 %collective-permute-start.3 = (f32[2,16,512]{2,1,0:T(8,128)S(1)}, f32[2,16,512]{2,1,0:T(8,128)S(1)}, u32[]{:S(2)}, u32[]{:S(2)}) collective-permute-start(f32[2,16,512]{2,1,0:T(8,128)S(1)} %get-tuple-element.16), channel_id=1, source_target_pairs={{0,4},{1,5},{2,6},{3,7},{8,12},{9,13},{10,14},{11,15},{16,20},{17,... | collective-permute-start | bytes 196616 | tf_op jit(solution)/shard_map/ppermute | solution.py:258
  46.7 5.6 %collective-permute-start.4 = (f32[2,64,128]{2,1,0:T(8,128)S(1)}, f32[2,64,128]{2,1,0:T(8,128)S(1)}, u32[]{:S(2)}, u32[]{:S(2)}) collective-permute-start(f32[2,64,128]{2,1,0:T(8,128)S(1)} %get-tuple-element.18), channel_id=1, source_target_pairs={{0,1},{1,2},{2,3},{3,4},{4,5},{5,6},{6,7},{8,9},{9,10},{10,11},{11... | collective-permute-start | bytes 196616 | tf_op jit(solution)/shard_map/ppermute | solution.py:258
where the time goes:
time: 56 us; the launch traced here: 55.7 us
  blocking collectives  24.5 us (44%)
  waiting for transfers between devices  11.2 us (20%)
  starting transfers between devices  10.2 us (18%)
  Pallas kernels  7.83 us (14%)
  local copies, waits for them, and re-layouts  1.92 us (3%)
    all_to_all x1, blocking collectives, per_device(): lined = lax.all_to_all(lined, 'chan', 0, 0, tiled=True)  24.5 us
    ppermute x5, waiting for transfers between devices, later(): return lax.ppermute(block, 'tm', route)  11.2 us
    ppermute x5, starting transfers between devices, later(): return lax.ppermute(block, 'tm', route)  10.2 us
    pallas_call x1, Pallas kernels, boxcars(): pl.pallas_call(boxcar_kernel, grid=(BEAMS,), in_specs=[pl.BlockSpec(memor...  3.41 us
    pallas_call x1, Pallas kernels, local_plane(): pl.pallas_call(local_kernel, grid=(BEAMS,), in_specs=[pl.BlockSpec(memory...  3.14 us
    unnamed x6, local copies, waits for them, and re-layouts  1.92 us
    pallas_call x1, Pallas kernels, final_plane(): pl.pallas_call(final_kernel, out_shape=[jax.ShapeDtypeStruct((BEAMS, ROWS...  1.13 us
  transfers between devices with their start and end apart: 5, of which 2 were waited for; matrix products, arithmetic and copies ran while one was open for 0% of the time, Pallas kernels for 0%

commit v1 on v0

--- a/solution.py
+++ b/solution.py
@@ -17,12 +17,10 @@
 REACH = 5
 
 
-def split3(x):
+def split(x):
     first = x.astype(jnp.bfloat16)
-    rest = x - first.astype(jnp.float32)
-    second = rest.astype(jnp.bfloat16)
-    third = (rest - second.astype(jnp.float32)).astype(jnp.bfloat16)
-    return first, second, third
+    second = (x - first.astype(jnp.float32)).astype(jnp.bfloat16)
+    return first, second
 
 
 def roll(x, shift):
@@ -72,63 +70,86 @@
     return source
 
 
-def local_kernel(q_ref, scale_ref, x_ref, o0, o1, o2, o3, o4, one, two, delayed):
+def local_kernel(
+    q_ref, scale_hbm, x_hbm, o0, o1, o2, o3, o4, scale, x, one, two, delayed, sems
+):
+    half = CHANS // 2
+    fetch_scale = pltpu.make_async_copy(scale_hbm, scale, sems.at[2 * BEAMS])
+    fetch_scale.start()
+    fetches = []
+    for b in range(BEAMS):
+        for h in range(2):
+            piece = pl.ds(h * half, half)
+            fetches.append(
+                pltpu.make_async_copy(
+                    x_hbm.at[b, piece], x.at[b, piece], sems.at[2 * b + h]
+                )
+            )
+            fetches[-1].start()
     q = q_ref[0]
     row = lax.broadcasted_iota(jnp.int32, (ROWS, CHANS), 0)
     col = lax.broadcasted_iota(jnp.int32, (ROWS, CHANS), 1)
     member = (row & 7) * 8 + (row >> 3) == col >> 3
-    weights = jnp.where(member, scale_ref[...], 0.0)
-    x = x_ref[0]
-    base = None
-    for part in split3(weights):
-        term = jnp.dot(part, x, preferred_element_type=jnp.float32)
-        base = term if base is None else base + term
+    fetch_scale.wait()
+    weights = jnp.where(member, scale[...], 0.0)
+    weights = jnp.concatenate(split(weights), axis=0)
     blank = jnp.zeros((8, LANES), jnp.float32)
-    groups = [
-        [jnp.concatenate([base[8 * g : 8 * g + 8], blank], axis=1)] for g in range(8)
-    ]
-    plane = merge_rows(groups, one, two)
-    delayed[...] = jnp.zeros_like(delayed)
     extent = WIDE + 2 * LANES
     pair = lax.broadcasted_iota(jnp.int32, (8, extent), 0) >> 1
     more = jnp.zeros((8, 2 * LANES), jnp.float32)
-    for a in range(8):
-        rows = jnp.concatenate(
-            [take(plane, 8 * a, 8, 0, WIDE // LANES), more], axis=1
-        )
-        rows = jnp.where(pair & 1 != 0, pltpu.roll(rows, 2 * q, 1), rows)
-        rows = jnp.where(pair & 2 != 0, pltpu.roll(rows, 4 * q, 1), rows)
-        delay = 8 * q * a
-        rows = pltpu.roll(rows, delay & (LANES - 1), 1)
-        start = pl.multiple_of(delay - (delay & (LANES - 1)), LANES)
-        delayed[pl.ds(8 * a, 8), pl.ds(start, extent)] = rows
-    for k, out in enumerate((o0, o1, o2, o3, o4)):
-        first = 16 * max(k - 1, 0)
-        out[0] = delayed[pl.ds(first, ROWS - first), pl.ds(SPAN * k, SPAN)]
+    delayed[...] = jnp.zeros_like(delayed)
+    for b in range(BEAMS):
+        fetches[2 * b].wait()
+        fetches[2 * b + 1].wait()
+        base = jnp.dot(weights, x[b], preferred_element_type=jnp.float32)
+        base = base[:ROWS] + base[ROWS:]
+        groups = [
+            [jnp.concatenate([base[8 * g : 8 * g + 8], blank], axis=1)]
+            for g in range(8)
+        ]
+        plane = merge_rows(groups, one, two)
+        for a in range(8):
+            rows = jnp.concatenate(
+                [take(plane, 8 * a, 8, 0, WIDE // LANES), more], axis=1
+            )
+            rows = jnp.where(pair & 1 != 0, pltpu.roll(rows, 2 * q, 1), rows)
+            rows = jnp.where(pair & 2 != 0, pltpu.roll(rows, 4 * q, 1), rows)
+            delay = 8 * q * a
+            rows = pltpu.roll(rows, delay & (LANES - 1), 1)
+            start = pl.multiple_of(delay - (delay & (LANES - 1)), LANES)
+            delayed[b, pl.ds(8 * a, 8), pl.ds(start, extent)] = rows
+        for k, out in enumerate((o0, o1, o2, o3, o4)):
+            first = 16 * max(k - 1, 0)
+            out[b] = delayed[b, pl.ds(first, ROWS - first), pl.ds(SPAN * k, SPAN)]
 
 
 def local_plane(x, scale, q):
     counts = [ROWS - 16 * max(k - 1, 0) for k in range(REACH)]
     return pl.pallas_call(
         local_kernel,
-        grid=(BEAMS,),
         in_specs=[
             pl.BlockSpec(memory_space=pltpu.SMEM),
-            pl.BlockSpec((1, CHANS), lambda b: (0, 0)),
-            pl.BlockSpec((1, CHANS, SPAN), lambda b: (b, 0, 0)),
-        ],
-        out_specs=[pl.BlockSpec((1, n, SPAN), lambda b: (b, 0, 0)) for n in counts],
+            pl.BlockSpec(memory_space=pltpu.HBM),
+            pl.BlockSpec(memory_space=pltpu.HBM),
+        ],
         out_shape=[
             jax.ShapeDtypeStruct((BEAMS, n, SPAN), jnp.float32) for n in counts
         ],
         scratch_shapes=[
+            pltpu.VMEM((1, CHANS), jnp.float32),
+            pltpu.VMEM((BEAMS, CHANS, SPAN), jnp.bfloat16),
             pltpu.VMEM((WIDE // LANES, ROWS, LANES), jnp.float32),
             pltpu.VMEM((WIDE // LANES, ROWS, LANES), jnp.float32),
-            pltpu.VMEM((ROWS, REACH * SPAN), jnp.float32),
+            pltpu.VMEM((BEAMS, ROWS, REACH * SPAN), jnp.float32),
+            pltpu.SemaphoreType.DMA((2 * BEAMS + 1,)),
         ],
         compiler_params=pltpu.CompilerParams(vmem_limit_bytes=24 << 20),
         name="local_plane",
-    )(q, scale, x)
+    )(
+        q,
+        pltpu.with_memory_space_constraint(scale, pltpu.HBM),
+        pltpu.with_memory_space_constraint(x, pltpu.HBM),
+    )
 
 
 def gather_kernel(o0, r1, r2, r3, r4, out, held):
@@ -197,60 +218,118 @@
     )(x)
 
 
-def boxcar_kernel(widths, main, tail, out, bands):
-    @pl.when(pl.program_id(0) == 0)
-    def _():
-        u = lax.broadcasted_iota(jnp.int32, (2 * LANES, LANES), 0)
-        t = lax.broadcasted_iota(jnp.int32, (2 * LANES, LANES), 1)
-        ago = t + LANES - u
+def boxcar_bands(widths):
+    u = lax.broadcasted_iota(jnp.int32, (2 * LANES, LANES), 0)
+    t = lax.broadcasted_iota(jnp.int32, (2 * LANES, LANES), 1)
+    ago = t + LANES - u
+    bands = []
+    for k in range(NBOX):
+        inside = jnp.logical_and(ago >= 0, ago < widths[k])
+        bands.append(jnp.where(inside, 1.0, 0.0).astype(jnp.bfloat16))
+    return jnp.concatenate(bands, axis=1)
+
+
+def boxcar_norms(widths):
+    norms = []
+    for k in range(NBOX):
+        square = jnp.full((1, LANES), widths[k] * (CHANS * PARTS), jnp.int32)
+        norms.append(lax.rsqrt(square.astype(jnp.float32)))
+    return jnp.concatenate(norms, axis=1)
+
+
+def boxcar_tile(before, here, bands, norms, held, c):
+    window = jnp.concatenate([before, here], axis=1)
+    sums = jnp.dot(window, bands, preferred_element_type=jnp.float32)
+    rows = BEAMS * ROWS
+    sums = (sums[:rows] + sums[rows:]) * norms
+    for b in range(BEAMS):
         for k in range(NBOX):
-            inside = jnp.logical_and(ago >= 0, ago < widths[k])
-            bands[:, pl.ds(k * LANES, LANES)] = jnp.where(inside, 1.0, 0.0).astype(
-                jnp.bfloat16
-            )
-
-    lane = lax.broadcasted_iota(jnp.int32, (ROWS, LANES), 1)
-    edge = tail[0]
-    chunks = [jnp.where(lane >= LANES // 2, edge, 0.0)]
+            held[b, k, :, pl.ds(c * LANES, LANES)] = sums[
+                b * ROWS : (b + 1) * ROWS, k * LANES : (k + 1) * LANES
+            ]
+
+
+def later_kernel(widths, main, out, held, sems):
+    bands = boxcar_bands(widths)
+    norms = boxcar_norms(widths)
+    parts = []
     for c in range(SPAN // LANES):
-        chunks.append(main[0, :, pl.ds(c * LANES, LANES)])
-    chunks[1] = chunks[1] + jnp.where(lane < LANES // 2, edge, 0.0)
-    parts = [split3(chunk) for chunk in chunks]
-    norms = [
-        lax.rsqrt(
-            jnp.full((ROWS, LANES), widths[k] * (CHANS * PARTS), jnp.int32).astype(
-                jnp.float32
+        tile = main[:, :, pl.ds(c * LANES, LANES)].reshape(BEAMS * ROWS, LANES)
+        parts.append(jnp.concatenate(split(tile), axis=0))
+    copies = []
+    for c in range(1, SPAN // LANES):
+        boxcar_tile(parts[c - 1], parts[c], bands, norms, held, c - 1)
+        copies.append(
+            pltpu.make_async_copy(
+                held.at[:, :, :, pl.ds((c - 1) * LANES, LANES)],
+                out.at[:, :, :, pl.ds(c * LANES, LANES)],
+                sems.at[c - 1],
             )
         )
-        for k in range(NBOX)
-    ]
-    for c in range(SPAN // LANES):
-        total = None
-        for before, here in zip(parts[c], parts[c + 1]):
-            window = jnp.concatenate([before, here], axis=1)
-            term = jnp.dot(window, bands[...], preferred_element_type=jnp.float32)
-            total = term if total is None else total + term
-        for k in range(NBOX):
-            out[0, k, :, pl.ds(c * LANES, LANES)] = (
-                total[:, k * LANES : (k + 1) * LANES] * norms[k]
-            )
-
-
-def boxcars(main, tail, widths):
-    return pl.pallas_call(
-        boxcar_kernel,
-        grid=(BEAMS,),
+        copies[-1].start()
+    for copy in copies:
+        copy.wait()
+
+
+def first_kernel(widths, main, tail, rest, out, held, sem):
+    del rest
+    lane = lax.broadcasted_iota(jnp.int32, (BEAMS * ROWS, LANES), 1)
+    edge = tail[...].reshape(BEAMS * ROWS, LANES)
+    before = jnp.where(lane >= LANES // 2, edge, 0.0)
+    here = main[:, :, pl.ds(0, LANES)].reshape(BEAMS * ROWS, LANES)
+    here = here + jnp.where(lane < LANES // 2, edge, 0.0)
+    before = jnp.concatenate(split(before), axis=0)
+    here = jnp.concatenate(split(here), axis=0)
+    boxcar_tile(before, here, boxcar_bands(widths), boxcar_norms(widths), held, 0)
+    copy = pltpu.make_async_copy(held, out.at[:, :, :, pl.ds(0, LANES)], sem)
+    copy.start()
+    copy.wait()
+
+
+OUT = jax.ShapeDtypeStruct((BEAMS, NBOX, ROWS, SPAN), jnp.float32)
+
+
+def boxcars_later(main, widths):
+    lanes = SPAN - LANES
+    return pl.pallas_call(
+        later_kernel,
         in_specs=[
             pl.BlockSpec(memory_space=pltpu.SMEM),
-            pl.BlockSpec((1, ROWS, SPAN), lambda b: (b, 0, 0)),
-            pl.BlockSpec((1, ROWS, LANES), lambda b: (b, 0, 0)),
-        ],
-        out_specs=pl.BlockSpec((1, NBOX, ROWS, SPAN), lambda b: (b, 0, 0, 0)),
-        out_shape=jax.ShapeDtypeStruct((BEAMS, NBOX, ROWS, SPAN), jnp.float32),
-        scratch_shapes=[pltpu.VMEM((2 * LANES, NBOX * LANES), jnp.bfloat16)],
-        compiler_params=pltpu.CompilerParams(vmem_limit_bytes=24 << 20),
-        name="boxcars",
-    )(widths, main, tail)
+            pl.BlockSpec(memory_space=pltpu.VMEM),
+        ],
+        out_specs=pl.BlockSpec(memory_space=pltpu.HBM),
+        out_shape=OUT,
+        scratch_shapes=[
+            pltpu.VMEM((BEAMS, NBOX, ROWS, lanes), jnp.float32),
+            pltpu.SemaphoreType.DMA((lanes // LANES,)),
+        ],
+        compiler_params=pltpu.CompilerParams(vmem_limit_bytes=24 << 20),
+        cost_estimate=pl.CostEstimate(
+            flops=2 * 256 * 256 * 768 * 3, bytes_accessed=2 << 20, transcendentals=0
+        ),
+        name="boxcars_later",
+    )(widths, main)
+
+
+def boxcars_first(main, tail, rest, widths):
+    return pl.pallas_call(
+        first_kernel,
+        in_specs=[
+            pl.BlockSpec(memory_space=pltpu.SMEM),
+            pl.BlockSpec(memory_space=pltpu.VMEM),
+            pl.BlockSpec(memory_space=pltpu.VMEM),
+            pl.BlockSpec(memory_space=pltpu.HBM),
+        ],
+        out_specs=pl.BlockSpec(memory_space=pltpu.HBM),
+        out_shape=OUT,
+        input_output_aliases={3: 0},
+        scratch_shapes=[
+            pltpu.VMEM((BEAMS, NBOX, ROWS, LANES), jnp.float32),
+            pltpu.SemaphoreType.DMA,
+        ],
+        compiler_params=pltpu.CompilerParams(vmem_limit_bytes=24 << 20),
+        name="boxcars_first",
+    )(widths, main, tail, rest)
 
 
 def later(block, distance):
@@ -266,7 +345,9 @@
     lined = gather_shifted(pieces)
     lined = lax.all_to_all(lined, "chan", 0, 0, tiled=True)
     main, tail = final_plane(lined)
-    return boxcars(main, later(tail, 1), box_widths)
+    tail = later(tail, 1)
+    rest = boxcars_later(main, box_widths)
+    return boxcars_first(main, tail, rest, box_widths)
 
 
 def solution(mesh):

time: 56 us -> 53 us (0.946)
  local copies, waits for them, and re-layouts: 1.92 us -> 0.01 us
  waiting for transfers between devices: 11.2 us -> 9.31 us
  Pallas kernels: 7.83 us -> 8.67 us
    unnamed x6 -> x2, local copies, waits for them, and re-layouts: 1.92 us -> 0.01 us
    ppermute x5, waiting for transfers between devices: 11.2 us -> 9.31 us  [later(): return lax.ppermute(block, 'tm', route)]
    pallas_call x2 -> x3, Pallas kernels: 6.55 us -> 7.4 us  [the longest x1 3.95 us: local_plane(): pl.pallas_call(local_kernel, in_specs=[pl.BlockSpec(memory_space=pltpu.SM...]
  transfers between devices with their start and end apart: 5 -> 5, of which waited for: 2 -> 2; matrix products, arithmetic and copies ran while one was open for 0% -> 0% of each run, Pallas kernels for 0% -> 4%
where the time goes in v1:
time: 53 us; the launch traced here: 52.8 us
  blocking collectives  24.5 us (46%)
  starting transfers between devices  10.2 us (19%)
  waiting for transfers between devices  9.31 us (18%)
  Pallas kernels  8.67 us (16%)
    all_to_all x1, blocking collectives, per_device(): lined = lax.all_to_all(lined, 'chan', 0, 0, tiled=True)  24.5 us
    ppermute x5, starting transfers between devices, later(): return lax.ppermute(block, 'tm', route)  10.2 us
    ppermute x5, waiting for transfers between devices, later(): return lax.ppermute(block, 'tm', route)  9.31 us
    pallas_call x1, Pallas kernels, local_plane(): pl.pallas_call(local_kernel, in_specs=[pl.BlockSpec(memory_space=pltpu.SM...  3.95 us
    pallas_call x1, Pallas kernels, boxcars_later(): pl.pallas_call(later_kernel, in_specs=[pl.BlockSpec(memory_space=pltpu.SM...  1.86 us
    pallas_call x1, Pallas kernels, boxcars_first(): pl.pallas_call(first_kernel, in_specs=[pl.BlockSpec(memory_space=pltpu.SM...  1.58 us
    pallas_call x1, Pallas kernels, final_plane(): pl.pallas_call(final_kernel, out_shape=[jax.ShapeDtypeStruct((BEAMS, ROWS...  1.13 us
  transfers between devices with their start and end apart: 5, of which 2 were waited for; matrix products, arithmetic and copies ran while one was open for 0% of the time, Pallas kernels for 4%

profile of v1, /device:TPU:4, one launch (start us, length us, event | category | flops | bytes accessed | tf_op | source)
XLA Modules:
  0.0 52.8 jit_solution(1846656013885555420)
XLA Ops:
  0.0 0.0 copy-start
  0.0 4.0 %local_plane.1 = (f32[2,64,512]{2,1,0:T(8,128)S(1)}, f32[2,64,512]{2,1,0:T(8,128)S(1)}, f32[2,48,512]{2,1,0:T(8,128)S(1)}, f32[2,32,512]{2,1,0:T(8,128)S(1)}, f32[2,16,512]{2,1,0:T(8,128)S(1)}) custom-call(s32[1]{0:T(128)} %bitcast.q_ref, f32[1,512]{1,0:T(1,128)} %bitcast.6, bf16[2,512,512]{2,1,0:T(8,128)(2,1)} %x_hbm.1), custom_call_target="tpu_custom_call" | custom-call | tf_op jit(solution)/shard_map/local_plane/pallas_call | solution.py:128
  4.0 1.9 %collective-permute-start = (f32[2,64,512]{2,1,0:T(8,128)S(1)}, f32[2,64,512]{2,1,0:T(8,128)S(1)}, u32[]{:S(2)}, u32[]{:S(2)}) collective-permute-start(f32[2,64,512]{2,1,0:T(8,128)S(1)} %get-tuple-element.13), channel_id=1, source_target_pairs={{0,1},{1,2},{2,3},{3,4},{4,5},{5,6},{6,7},{8,9},{9,10},{10,11},{11... | collective-permute-start | bytes 786440 | tf_op jit(solution)/shard_map/ppermute | solution.py:337
  5.9 3.1 %collective-permute-start.1 = (f32[2,48,512]{2,1,0:T(8,128)S(1)}, f32[2,48,512]{2,1,0:T(8,128)S(1)}, u32[]{:S(2)}, u32[]{:S(2)}) collective-permute-start(f32[2,48,512]{2,1,0:T(8,128)S(1)} %get-tuple-element.14), channel_id=1, source_target_pairs={{0,2},{1,3},{2,4},{3,5},{4,6},{5,7},{8,10},{9,11},{10,12},{11,13},... | collective-permute-start | bytes 589832 | tf_op jit(solution)/shard_map/ppermute | solution.py:337
  9.0 1.9 %collective-permute-start.2 = (f32[2,32,512]{2,1,0:T(8,128)S(1)}, f32[2,32,512]{2,1,0:T(8,128)S(1)}, u32[]{:S(2)}, u32[]{:S(2)}) collective-permute-start(f32[2,32,512]{2,1,0:T(8,128)S(1)} %get-tuple-element.15), channel_id=1, source_target_pairs={{0,3},{1,4},{2,5},{3,6},{4,7},{8,11},{9,12},{10,13},{11,14},{12,15... | collective-permute-start | bytes 393224 | tf_op jit(solution)/shard_map/ppermute | solution.py:337
  10.9 1.3 %collective-permute-start.3 = (f32[2,16,512]{2,1,0:T(8,128)S(1)}, f32[2,16,512]{2,1,0:T(8,128)S(1)}, u32[]{:S(2)}, u32[]{:S(2)}) collective-permute-start(f32[2,16,512]{2,1,0:T(8,128)S(1)} %get-tuple-element.16), channel_id=1, source_target_pairs={{0,4},{1,5},{2,6},{3,7},{8,12},{9,13},{10,14},{11,15},{16,20},{17,... | collective-permute-start | bytes 196616 | tf_op jit(solution)/shard_map/ppermute | solution.py:337
  12.2 7.5 %collective-permute-done.3.r4 = f32[2,16,512]{2,1,0:T(8,128)S(1)} collective-permute-done((f32[2,16,512]{2,1,0:T(8,128)S(1)}, f32[2,16,512]{2,1,0:T(8,128)S(1)}, u32[]{:S(2)}, u32[]{:S(2)}) %collective-permute-start.3) | collective-permute-done | bytes 65568 | tf_op jit(solution)/shard_map/ppermute | solution.py:337
  19.8 0.0 collective-permute-done.2.r3
  19.8 0.0 collective-permute-done.1.r2
  19.8 0.0 collective-permute-done.r1
  19.8 0.1 gather_shifted.1
  19.9 24.5 %all_to_all.11 = f32[32,16,128]{2,1,0:T(8,128)S(1)} all-to-all(f32[32,16,128]{2,1,0:T(8,128)S(1)} %bitcast.5), channel_id=1, replica_groups=mesh['chan'=32,'tm'=8] {'chan'}, dimensions={0} | all-to-all | bytes 524288 | tf_op jit(solution)/shard_map/all_to_all | solution.py:346
  44.5 1.1 %final_plane.1 = (f32[2,64,512]{2,1,0:T(8,128)S(1)}, f32[2,64,128]{2,1,0:T(8,128)S(1)}) custom-call(f32[512,128]{1,0:T(8,128)S(1)} %bitcast.4), custom_call_target="tpu_custom_call" | custom-call | tf_op jit(solution)/shard_map/final_plane/pallas_call | solution.py:206
  45.6 1.9 %collective-permute-start.4 = (f32[2,64,128]{2,1,0:T(8,128)S(1)}, f32[2,64,128]{2,1,0:T(8,128)S(1)}, u32[]{:S(2)}, u32[]{:S(2)}) collective-permute-start(f32[2,64,128]{2,1,0:T(8,128)S(1)} %get-tuple-element.18), channel_id=1, source_target_pairs={{0,1},{1,2},{2,3},{3,4},{4,5},{5,6},{6,7},{8,9},{9,10},{10,11},{11... | collective-permute-start | bytes 196616 | tf_op jit(solution)/shard_map/ppermute | solution.py:337
  47.5 0.0 copy-done
  47.5 1.9 %boxcars_later.1.rest = f32[2,6,64,512]{3,2,1,0:T(8,128)} custom-call(s32[6]{0:T(128)S(1)} %copy-done, f32[2,64,512]{2,1,0:T(8,128)S(1)} %get-tuple-element.17.main), custom_call_target="tpu_custom_call" | custom-call | flops 301989888 | bytes 2097152 | tf_op jit(solution)/shard_map/boxcars_later/pallas_call | solution.py:294
  49.4 1.8 %collective-permute-done.4.tail = f32[2,64,128]{2,1,0:T(8,128)S(1)} collective-permute-done((f32[2,64,128]{2,1,0:T(8,128)S(1)}, f32[2,64,128]{2,1,0:T(8,128)S(1)}, u32[]{:S(2)}, u32[]{:S(2)}) %collective-permute-start.4) | collective-permute-done | bytes 65568 | tf_op jit(solution)/shard_map/ppermute | solution.py:337
  51.2 1.6 %boxcars_first.1 = f32[2,6,64,512]{3,2,1,0:T(8,128)} custom-call(s32[6]{0:T(128)S(1)} %copy-done, f32[2,64,512]{2,1,0:T(8,128)S(1)} %get-tuple-element.17.main, f32[2,64,128]{2,1,0:T(8,128)S(1)} %collective-permute-done.4.tail, f32[2,6,64,512]{3,2,1,0:T(8,128)} %boxcars_later.1.rest), custom_call_target="tpu_custom_call", output_to_operand_aliasing={{}: (3, {})} | custom-call | tf_op jit(solution)/shard_map/boxcars_first/pallas_call | solution.py:315
Async XLA Ops:
  0.0 47.5 %copy-start = (s32[6]{0:T(128)S(1)}, s32[6]{0:T(128)}, u32[]{:S(2)}) copy-start(s32[6]{0:T(128)} %widths.3) | copy-start | bytes 76
  4.0 15.8 %collective-permute-start = (f32[2,64,512]{2,1,0:T(8,128)S(1)}, f32[2,64,512]{2,1,0:T(8,128)S(1)}, u32[]{:S(2)}, u32[]{:S(2)}) collective-permute-start(f32[2,64,512]{2,1,0:T(8,128)S(1)} %get-tuple-element.13), channel_id=1, source_target_pairs={{0,1},{1,2},{2,3},{3,4},{4,5},{5,6},{6,7},{8,9},{9,10},{10,11},{11... | collective-permute-start | bytes 786440 | tf_op jit(solution)/shard_map/ppermute | solution.py:337
  5.9 13.9 %collective-permute-start.1 = (f32[2,48,512]{2,1,0:T(8,128)S(1)}, f32[2,48,512]{2,1,0:T(8,128)S(1)}, u32[]{:S(2)}, u32[]{:S(2)}) collective-permute-start(f32[2,48,512]{2,1,0:T(8,128)S(1)} %get-tuple-element.14), channel_id=1, source_target_pairs={{0,2},{1,3},{2,4},{3,5},{4,6},{5,7},{8,10},{9,11},{10,12},{11,13},... | collective-permute-start | bytes 589832 | tf_op jit(solution)/shard_map/ppermute | solution.py:337
  9.0 10.8 %collective-permute-start.2 = (f32[2,32,512]{2,1,0:T(8,128)S(1)}, f32[2,32,512]{2,1,0:T(8,128)S(1)}, u32[]{:S(2)}, u32[]{:S(2)}) collective-permute-start(f32[2,32,512]{2,1,0:T(8,128)S(1)} %get-tuple-element.15), channel_id=1, source_target_pairs={{0,3},{1,4},{2,5},{3,6},{4,7},{8,11},{9,12},{10,13},{11,14},{12,15... | collective-permute-start | bytes 393224 | tf_op jit(solution)/shard_map/ppermute | solution.py:337
  10.9 8.8 %collective-permute-start.3 = (f32[2,16,512]{2,1,0:T(8,128)S(1)}, f32[2,16,512]{2,1,0:T(8,128)S(1)}, u32[]{:S(2)}, u32[]{:S(2)}) collective-permute-start(f32[2,16,512]{2,1,0:T(8,128)S(1)} %get-tuple-element.16), channel_id=1, source_target_pairs={{0,4},{1,5},{2,6},{3,7},{8,12},{9,13},{10,14},{11,15},{16,20},{17,... | collective-permute-start | bytes 196616 | tf_op jit(solution)/shard_map/ppermute | solution.py:337
  45.6 5.6 %collective-permute-start.4 = (f32[2,64,128]{2,1,0:T(8,128)S(1)}, f32[2,64,128]{2,1,0:T(8,128)S(1)}, u32[]{:S(2)}, u32[]{:S(2)}) collective-permute-start(f32[2,64,128]{2,1,0:T(8,128)S(1)} %get-tuple-element.18), channel_id=1, source_target_pairs={{0,1},{1,2},{2,3},{3,4},{4,5},{5,6},{6,7},{8,9},{9,10},{10,11},{11... | collective-permute-start | bytes 196616 | tf_op jit(solution)/shard_map/ppermute | solution.py:337

commit v2 on v1

--- a/solution.py
+++ b/solution.py
@@ -333,8 +333,14 @@
 
 
 def later(block, distance):
-    route = [(i, i + distance) for i in range(SEGMENTS - distance)]
-    return lax.ppermute(block, "tm", route)
+    route = []
+    for part in range(PARTS):
+        longest = (PARTS - 1 - part) * (ROWS - 2) + ROWS - 1
+        if longest + SPAN > distance * SPAN:
+            for i in range(SEGMENTS - distance):
+                sender = part * SEGMENTS + i
+                route.append((sender, sender + distance))
+    return lax.ppermute(block, ("chan", "tm"), route)
 
 
 def per_device(intensity, channel_scale, box_widths):

time: 53 us -> 49.6 us (0.936)
  the two profiles are of different devices: /device:TPU:4 before, /device:TPU:1 now
where the time goes in v2:
time: 49.6 us; the launch traced here: 49.4 us
  blocking collectives  19 us (38%)
  starting transfers between devices  17.7 us (36%)
  Pallas kernels  8.68 us (18%)
  waiting for transfers between devices  3.85 us (8%)
    all_to_all x1, blocking collectives, per_device(): lined = lax.all_to_all(lined, 'chan', 0, 0, tiled=True)  19 us
    ppermute x5, starting transfers between devices, later(): return lax.ppermute(block, ('chan', 'tm'), route)  17.7 us
    pallas_call x1, Pallas kernels, local_plane(): pl.pallas_call(local_kernel, in_specs=[pl.BlockSpec(memory_space=pltpu.SM...  3.95 us
    ppermute x5, waiting for transfers between devices, later(): return lax.ppermute(block, ('chan', 'tm'), route)  3.85 us
    pallas_call x1, Pallas kernels, boxcars_later(): pl.pallas_call(later_kernel, in_specs=[pl.BlockSpec(memory_space=pltpu.SM...  1.87 us
    pallas_call x1, Pallas kernels, boxcars_first(): pl.pallas_call(first_kernel, in_specs=[pl.BlockSpec(memory_space=pltpu.SM...  1.59 us
    pallas_call x1, Pallas kernels, final_plane(): pl.pallas_call(final_kernel, out_shape=[jax.ShapeDtypeStruct((BEAMS, ROWS...  1.13 us
  transfers between devices with their start and end apart: 5, of which 1 were waited for; matrix products, arithmetic and copies ran while one was open for 0% of the time, Pallas kernels for 4%

profile of v2, /device:TPU:1, one launch (start us, length us, event | category | flops | bytes accessed | tf_op | source)
XLA Modules:
  0.0 49.4 jit_solution(17726384081974348836)
XLA Ops:
  0.0 0.0 copy-start
  0.0 4.0 %local_plane.1 = (f32[2,64,512]{2,1,0:T(8,128)S(1)}, f32[2,64,512]{2,1,0:T(8,128)S(1)}, f32[2,48,512]{2,1,0:T(8,128)S(1)}, f32[2,32,512]{2,1,0:T(8,128)S(1)}, f32[2,16,512]{2,1,0:T(8,128)S(1)}) custom-call(s32[1]{0:T(128)} %bitcast.q_ref, f32[1,512]{1,0:T(1,128)} %bitcast.6, bf16[2,512,512]{2,1,0:T(8,128)(2,1)} %x_hbm.1), custom_call_target="tpu_custom_call" | custom-call | tf_op jit(solution)/shard_map/local_plane/pallas_call | solution.py:128
  4.0 4.5 %collective-permute-start = (f32[2,64,512]{2,1,0:T(8,128)S(1)}, f32[2,64,512]{2,1,0:T(8,128)S(1)}, u32[]{:S(2)}, u32[]{:S(2)}) collective-permute-start(f32[2,64,512]{2,1,0:T(8,128)S(1)} %get-tuple-element.13), channel_id=1, source_target_pairs={{0,1},{1,2},{2,3},{3,4},{4,5},{5,6},{6,7},{8,9},{9,10},{10,11},{11... | collective-permute-start | bytes 786440 | tf_op jit(solution)/shard_map/ppermute | solution.py:343
  8.5 3.1 %collective-permute-start.1 = (f32[2,48,512]{2,1,0:T(8,128)S(1)}, f32[2,48,512]{2,1,0:T(8,128)S(1)}, u32[]{:S(2)}, u32[]{:S(2)}) collective-permute-start(f32[2,48,512]{2,1,0:T(8,128)S(1)} %get-tuple-element.14), channel_id=1, source_target_pairs={{0,2},{1,3},{2,4},{3,5},{4,6},{5,7},{8,10},{9,11},{10,12},{11,13},... | collective-permute-start | bytes 589832 | tf_op jit(solution)/shard_map/ppermute | solution.py:343
  11.6 3.4 %collective-permute-start.2 = (f32[2,32,512]{2,1,0:T(8,128)S(1)}, f32[2,32,512]{2,1,0:T(8,128)S(1)}, u32[]{:S(2)}, u32[]{:S(2)}) collective-permute-start(f32[2,32,512]{2,1,0:T(8,128)S(1)} %get-tuple-element.15), channel_id=1, source_target_pairs={{0,3},{1,4},{2,5},{3,6},{4,7},{8,11},{9,12},{10,13},{11,14},{12,15... | collective-permute-start | bytes 393224 | tf_op jit(solution)/shard_map/ppermute | solution.py:343
  15.1 1.3 %collective-permute-start.3 = (f32[2,16,512]{2,1,0:T(8,128)S(1)}, f32[2,16,512]{2,1,0:T(8,128)S(1)}, u32[]{:S(2)}, u32[]{:S(2)}) collective-permute-start(f32[2,16,512]{2,1,0:T(8,128)S(1)} %get-tuple-element.16), channel_id=1, source_target_pairs={{0,4},{1,5},{2,6},{3,7},{8,12},{9,13},{10,14},{11,15},{16,20},{17,... | collective-permute-start | bytes 196616 | tf_op jit(solution)/shard_map/ppermute | solution.py:343
  16.4 3.8 %collective-permute-done.3.r4 = f32[2,16,512]{2,1,0:T(8,128)S(1)} collective-permute-done((f32[2,16,512]{2,1,0:T(8,128)S(1)}, f32[2,16,512]{2,1,0:T(8,128)S(1)}, u32[]{:S(2)}, u32[]{:S(2)}) %collective-permute-start.3) | collective-permute-done | bytes 65568 | tf_op jit(solution)/shard_map/ppermute | solution.py:343
  20.2 0.0 collective-permute-done.2.r3
  20.2 0.0 collective-permute-done.1.r2
  20.2 0.0 collective-permute-done.r1
  20.2 0.1 gather_shifted.1
  20.4 19.0 %all_to_all.11 = f32[32,16,128]{2,1,0:T(8,128)S(1)} all-to-all(f32[32,16,128]{2,1,0:T(8,128)S(1)} %bitcast.5), channel_id=1, replica_groups=mesh['chan'=32,'tm'=8] {'chan'}, dimensions={0} | all-to-all | bytes 524288 | tf_op jit(solution)/shard_map/all_to_all | solution.py:352
  39.4 1.1 %final_plane.1 = (f32[2,64,512]{2,1,0:T(8,128)S(1)}, f32[2,64,128]{2,1,0:T(8,128)S(1)}) custom-call(f32[512,128]{1,0:T(8,128)S(1)} %bitcast.4), custom_call_target="tpu_custom_call" | custom-call | tf_op jit(solution)/shard_map/final_plane/pallas_call | solution.py:206
  40.5 5.4 %collective-permute-start.4 = (f32[2,64,128]{2,1,0:T(8,128)S(1)}, f32[2,64,128]{2,1,0:T(8,128)S(1)}, u32[]{:S(2)}, u32[]{:S(2)}) collective-permute-start(f32[2,64,128]{2,1,0:T(8,128)S(1)} %get-tuple-element.18), channel_id=1, source_target_pairs={{0,1},{1,2},{2,3},{3,4},{4,5},{5,6},{6,7},{8,9},{9,10},{10,11},{11... | collective-permute-start | bytes 196616 | tf_op jit(solution)/shard_map/ppermute | solution.py:343
  45.9 0.0 copy-done
  45.9 1.9 %boxcars_later.1.rest = f32[2,6,64,512]{3,2,1,0:T(8,128)} custom-call(s32[6]{0:T(128)S(1)} %copy-done, f32[2,64,512]{2,1,0:T(8,128)S(1)} %get-tuple-element.17.main), custom_call_target="tpu_custom_call" | custom-call | flops 301989888 | bytes 2097152 | tf_op jit(solution)/shard_map/boxcars_later/pallas_call | solution.py:294
  47.8 0.0 collective-permute-done.4.tail
  47.8 1.6 %boxcars_first.1 = f32[2,6,64,512]{3,2,1,0:T(8,128)} custom-call(s32[6]{0:T(128)S(1)} %copy-done, f32[2,64,512]{2,1,0:T(8,128)S(1)} %get-tuple-element.17.main, f32[2,64,128]{2,1,0:T(8,128)S(1)} %collective-permute-done.4.tail, f32[2,6,64,512]{3,2,1,0:T(8,128)} %boxcars_later.1.rest), custom_call_target="tpu_custom_call", output_to_operand_aliasing={{}: (3, {})} | custom-call | tf_op jit(solution)/shard_map/boxcars_first/pallas_call | solution.py:315
Async XLA Ops:
  0.0 45.9 %copy-start = (s32[6]{0:T(128)S(1)}, s32[6]{0:T(128)}, u32[]{:S(2)}) copy-start(s32[6]{0:T(128)} %widths.3) | copy-start | bytes 76
  4.0 16.2 %collective-permute-start = (f32[2,64,512]{2,1,0:T(8,128)S(1)}, f32[2,64,512]{2,1,0:T(8,128)S(1)}, u32[]{:S(2)}, u32[]{:S(2)}) collective-permute-start(f32[2,64,512]{2,1,0:T(8,128)S(1)} %get-tuple-element.13), channel_id=1, source_target_pairs={{0,1},{1,2},{2,3},{3,4},{4,5},{5,6},{6,7},{8,9},{9,10},{10,11},{11... | collective-permute-start | bytes 786440 | tf_op jit(solution)/shard_map/ppermute | solution.py:343
  8.5 11.7 %collective-permute-start.1 = (f32[2,48,512]{2,1,0:T(8,128)S(1)}, f32[2,48,512]{2,1,0:T(8,128)S(1)}, u32[]{:S(2)}, u32[]{:S(2)}) collective-permute-start(f32[2,48,512]{2,1,0:T(8,128)S(1)} %get-tuple-element.14), channel_id=1, source_target_pairs={{0,2},{1,3},{2,4},{3,5},{4,6},{5,7},{8,10},{9,11},{10,12},{11,13},... | collective-permute-start | bytes 589832 | tf_op jit(solution)/shard_map/ppermute | solution.py:343
  11.6 8.6 %collective-permute-start.2 = (f32[2,32,512]{2,1,0:T(8,128)S(1)}, f32[2,32,512]{2,1,0:T(8,128)S(1)}, u32[]{:S(2)}, u32[]{:S(2)}) collective-permute-start(f32[2,32,512]{2,1,0:T(8,128)S(1)} %get-tuple-element.15), channel_id=1, source_target_pairs={{0,3},{1,4},{2,5},{3,6},{4,7},{8,11},{9,12},{10,13},{11,14},{12,15... | collective-permute-start | bytes 393224 | tf_op jit(solution)/shard_map/ppermute | solution.py:343
  15.1 5.1 %collective-permute-start.3 = (f32[2,16,512]{2,1,0:T(8,128)S(1)}, f32[2,16,512]{2,1,0:T(8,128)S(1)}, u32[]{:S(2)}, u32[]{:S(2)}) collective-permute-start(f32[2,16,512]{2,1,0:T(8,128)S(1)} %get-tuple-element.16), channel_id=1, source_target_pairs={{0,4},{1,5},{2,6},{3,7},{8,12},{9,13},{10,14},{11,15},{16,20},{17,... | collective-permute-start | bytes 196616 | tf_op jit(solution)/shard_map/ppermute | solution.py:343
  40.5 7.3 %collective-permute-start.4 = (f32[2,64,128]{2,1,0:T(8,128)S(1)}, f32[2,64,128]{2,1,0:T(8,128)S(1)}, u32[]{:S(2)}, u32[]{:S(2)}) collective-permute-start(f32[2,64,128]{2,1,0:T(8,128)S(1)} %get-tuple-element.18), channel_id=1, source_target_pairs={{0,1},{1,2},{2,3},{3,4},{4,5},{5,6},{6,7},{8,9},{9,10},{10,11},{11... | collective-permute-start | bytes 196616 | tf_op jit(solution)/shard_map/ppermute | solution.py:343

commit v3 on v2

--- a/solution.py
+++ b/solution.py
@@ -1,5 +1,6 @@
 import jax
 import jax.numpy as jnp
+import numpy as np
 from jax import lax
 from jax.experimental import pallas as pl
 from jax.experimental.pallas import tpu as pltpu
@@ -15,6 +16,43 @@
 NBOX = 6
 LANES = 128
 REACH = 5
+TILES = 16
+UNITS = 6
+PER = SPAN // LANES
+
+
+def packing():
+    tail = [sum(((i >> level) + 1) // 2 for level in range(6)) for i in range(ROWS)]
+    units = {}
+    for q in range(PARTS):
+        for a in range(TILES):
+            delay = 4 * q * a
+            ends = [
+                delay % LANES + 2 * q * (r // 2) + SPAN + tail[4 * a + r] for r in range(4)
+            ]
+            units[q, a] = (delay // LANES, -(-max(ends) // LANES))
+    counts = np.zeros((PARTS, REACH), np.int32)
+    for (q, a), (first, number) in units.items():
+        for h in range(first, first + number):
+            counts[q, h // PER] += 1
+    sizes = [int(n) for n in counts.max(axis=0)]
+    starts = [sum(sizes[:k]) for k in range(REACH)]
+    spare = sum(sizes)
+    table = np.full((PARTS, 2, LANES), spare, np.int32)
+    for q in range(PARTS):
+        free = list(starts)
+        for a in range(TILES):
+            first, number = units[q, a]
+            for i in range(number):
+                h = first + i
+                table[q, 0, a * UNITS + i] = free[h // PER]
+                place = (a * PER + h % PER) * 2 + (i >= PER)
+                table[q, 1, place] = free[h // PER]
+                free[h // PER] += 1
+    return sizes, starts, spare, table, counts
+
+
+SIZES, STARTS, SPARE, TABLE, COUNTS = packing()
 
 
 def split(x):
@@ -71,11 +109,29 @@
 
 
 def local_kernel(
-    q_ref, scale_hbm, x_hbm, o0, o1, o2, o3, o4, scale, x, one, two, delayed, sems
+    q_ref,
+    table_hbm,
+    scale_hbm,
+    x_hbm,
+    o0,
+    o1,
+    o2,
+    o3,
+    o4,
+    slots,
+    scale,
+    x,
+    one,
+    two,
+    packed,
+    sems,
 ):
     half = CHANS // 2
+    q = q_ref[0]
     fetch_scale = pltpu.make_async_copy(scale_hbm, scale, sems.at[2 * BEAMS])
     fetch_scale.start()
+    fetch_slots = pltpu.make_async_copy(table_hbm.at[q], slots, sems.at[2 * BEAMS + 1])
+    fetch_slots.start()
     fetches = []
     for b in range(BEAMS):
         for h in range(2):
@@ -86,7 +142,6 @@
                 )
             )
             fetches[-1].start()
-    q = q_ref[0]
     row = lax.broadcasted_iota(jnp.int32, (ROWS, CHANS), 0)
     col = lax.broadcasted_iota(jnp.int32, (ROWS, CHANS), 1)
     member = (row & 7) * 8 + (row >> 3) == col >> 3
@@ -94,10 +149,6 @@
     weights = jnp.where(member, scale[...], 0.0)
     weights = jnp.concatenate(split(weights), axis=0)
     blank = jnp.zeros((8, LANES), jnp.float32)
-    extent = WIDE + 2 * LANES
-    pair = lax.broadcasted_iota(jnp.int32, (8, extent), 0) >> 1
-    more = jnp.zeros((8, 2 * LANES), jnp.float32)
-    delayed[...] = jnp.zeros_like(delayed)
     for b in range(BEAMS):
         fetches[2 * b].wait()
         fetches[2 * b + 1].wait()
@@ -107,76 +158,91 @@
             [jnp.concatenate([base[8 * g : 8 * g + 8], blank], axis=1)]
             for g in range(8)
         ]
-        plane = merge_rows(groups, one, two)
-        for a in range(8):
-            rows = jnp.concatenate(
-                [take(plane, 8 * a, 8, 0, WIDE // LANES), more], axis=1
-            )
-            rows = jnp.where(pair & 1 != 0, pltpu.roll(rows, 2 * q, 1), rows)
-            rows = jnp.where(pair & 2 != 0, pltpu.roll(rows, 4 * q, 1), rows)
-            delay = 8 * q * a
-            rows = pltpu.roll(rows, delay & (LANES - 1), 1)
-            start = pl.multiple_of(delay - (delay & (LANES - 1)), LANES)
-            delayed[b, pl.ds(8 * a, 8), pl.ds(start, extent)] = rows
-        for k, out in enumerate((o0, o1, o2, o3, o4)):
-            first = 16 * max(k - 1, 0)
-            out[b] = delayed[b, pl.ds(first, ROWS - first), pl.ds(SPAN * k, SPAN)]
+        merge_rows(groups, one, two.at[b])
+    fetch_slots.wait()
+    odd = lax.broadcasted_iota(jnp.int32, (8, UNITS * LANES), 0) & 2 != 0
+    for a in range(TILES):
+        rows = [take(two.at[b], 4 * a, 4, 0, WIDE // LANES) for b in range(BEAMS)]
+        rows = jnp.concatenate([jnp.concatenate(rows, axis=0), blank], axis=1)
+        rows = jnp.where(odd, pltpu.roll(rows, 2 * q, 1), rows)
+        rows = pltpu.roll(rows, (4 * q * a) & (LANES - 1), 1)
+        for i in range(UNITS):
+            packed[slots[0, a * UNITS + i]] = rows[:, i * LANES : (i + 1) * LANES]
+    for k, out in enumerate((o0, o1, o2, o3, o4)):
+        out[...] = packed[pl.ds(STARTS[k], SIZES[k])]
 
 
 def local_plane(x, scale, q):
-    counts = [ROWS - 16 * max(k - 1, 0) for k in range(REACH)]
     return pl.pallas_call(
         local_kernel,
         in_specs=[
             pl.BlockSpec(memory_space=pltpu.SMEM),
             pl.BlockSpec(memory_space=pltpu.HBM),
             pl.BlockSpec(memory_space=pltpu.HBM),
-        ],
-        out_shape=[
-            jax.ShapeDtypeStruct((BEAMS, n, SPAN), jnp.float32) for n in counts
-        ],
+            pl.BlockSpec(memory_space=pltpu.HBM),
+        ],
+        out_shape=[jax.ShapeDtypeStruct((n, 8, LANES), jnp.float32) for n in SIZES],
         scratch_shapes=[
+            pltpu.SMEM((2, LANES), jnp.int32),
             pltpu.VMEM((1, CHANS), jnp.float32),
             pltpu.VMEM((BEAMS, CHANS, SPAN), jnp.bfloat16),
             pltpu.VMEM((WIDE // LANES, ROWS, LANES), jnp.float32),
-            pltpu.VMEM((WIDE // LANES, ROWS, LANES), jnp.float32),
-            pltpu.VMEM((BEAMS, ROWS, REACH * SPAN), jnp.float32),
-            pltpu.SemaphoreType.DMA((2 * BEAMS + 1,)),
+            pltpu.VMEM((BEAMS, WIDE // LANES, ROWS, LANES), jnp.float32),
+            pltpu.VMEM((SPARE + 1, 8, LANES), jnp.float32),
+            pltpu.SemaphoreType.DMA((2 * BEAMS + 2,)),
         ],
         compiler_params=pltpu.CompilerParams(vmem_limit_bytes=24 << 20),
         name="local_plane",
     )(
         q,
+        pltpu.with_memory_space_constraint(TABLE, pltpu.HBM),
         pltpu.with_memory_space_constraint(scale, pltpu.HBM),
         pltpu.with_memory_space_constraint(x, pltpu.HBM),
     )
 
 
-def gather_kernel(o0, r1, r2, r3, r4, out, held):
-    for b in range(BEAMS):
-        for a in range(0, ROWS, 16):
-            total = o0[b, pl.ds(a, 16), :] + r1[b, pl.ds(a, 16), :]
-            for k, received in ((2, r2), (3, r3), (4, r4)):
-                first = 16 * (k - 1)
-                if a >= first:
-                    total = total + received[b, pl.ds(a - first, 16), :]
-            for c in range(SPAN // LANES):
-                held[c, pl.ds(a, 16), :] = total[:, c * LANES : (c + 1) * LANES]
-        for c in range(SPAN // LANES):
-            for i in range(2):
-                out[pl.ds(b * 8 + c * 2 + i, PARTS, stride=16), :] = held[
-                    c, pl.ds(i, PARTS, stride=2), :
-                ]
-
-
-def gather_shifted(pieces):
+def gather_kernel(
+    q_ref, table_hbm, o0, r1, r2, r3, r4, out, slots, packed, held, sem
+):
+    fetch_slots = pltpu.make_async_copy(table_hbm.at[q_ref[0]], slots, sem)
+    fetch_slots.start()
+    for k, piece in enumerate((o0, r1, r2, r3, r4)):
+        packed[pl.ds(STARTS[k], SIZES[k])] = piece[...]
+    packed[SPARE] = jnp.zeros((8, LANES), jnp.float32)
+    fetch_slots.wait()
+    for a in range(TILES):
+        for c in range(PER):
+            place = (a * PER + c) * 2
+            held[c, pl.ds(8 * a, 8), :] = (
+                packed[slots[1, place]] + packed[slots[1, place + 1]]
+            )
+    for c in range(PER):
+        for r in range(8):
+            b, m, i = r >> 2, r >> 1 & 1, r & 1
+            out[pl.ds(m * 16 + b * 8 + c * 2 + i, TILES, stride=32), :] = held[
+                c, pl.ds(r, TILES, stride=8), :
+            ]
+
+
+def gather_shifted(pieces, q):
+    vmem = pl.BlockSpec(memory_space=pltpu.VMEM)
     return pl.pallas_call(
         gather_kernel,
+        in_specs=[
+            pl.BlockSpec(memory_space=pltpu.SMEM),
+            pl.BlockSpec(memory_space=pltpu.HBM),
+        ]
+        + [vmem] * REACH,
         out_shape=jax.ShapeDtypeStruct((PARTS * 16, LANES), jnp.float32),
-        scratch_shapes=[pltpu.VMEM((SPAN // LANES, ROWS, LANES), jnp.float32)],
+        scratch_shapes=[
+            pltpu.SMEM((2, LANES), jnp.int32),
+            pltpu.VMEM((SPARE + 1, 8, LANES), jnp.float32),
+            pltpu.VMEM((PER, 8 * TILES, LANES), jnp.float32),
+            pltpu.SemaphoreType.DMA,
+        ],
         compiler_params=pltpu.CompilerParams(vmem_limit_bytes=24 << 20),
         name="gather_shifted",
-    )(*pieces)
+    )(q, pltpu.with_memory_space_constraint(TABLE, pltpu.HBM), *pieces)
 
 
 def final_kernel(x_ref, main, tail, one, two):
@@ -335,8 +401,7 @@
 def later(block, distance):
     route = []
     for part in range(PARTS):
-        longest = (PARTS - 1 - part) * (ROWS - 2) + ROWS - 1
-        if longest + SPAN > distance * SPAN:
+        if COUNTS[PARTS - 1 - part, distance]:
             for i in range(SEGMENTS - distance):
                 sender = part * SEGMENTS + i
                 route.append((sender, sender + distance))
@@ -348,7 +413,7 @@
     pieces = list(local_plane(intensity, channel_scale.reshape(1, CHANS), q))
     for k in range(REACH - 1, 0, -1):
         pieces[k] = later(pieces[k], k)
-    lined = gather_shifted(pieces)
+    lined = gather_shifted(pieces, q)
     lined = lax.all_to_all(lined, "chan", 0, 0, tiled=True)
     main, tail = final_plane(lined)
     tail = later(tail, 1)

time: 49.6 us -> 48.5 us (0.978)
  waiting for transfers between devices: 3.85 us -> 1.61 us
  blocking collectives: 19 us -> 19.7 us
  Pallas kernels: 8.68 us -> 9.19 us
    ppermute x5, waiting for transfers between devices: 3.85 us -> 1.61 us  [later(): return lax.ppermute(block, ('chan', 'tm'), route)]
    pallas_call x1, Pallas kernels: 0.14 us -> 0.99 us  [gather_shifted(): pl.pallas_call(gather_kernel, in_specs=[pl.BlockSpec(memory_space=pltpu.S...]
    all_to_all x1, blocking collectives: 19 us -> 19.7 us  [per_device(): lined = lax.all_to_all(lined, 'chan', 0, 0, tiled=True)]
where the time goes in v3:
time: 48.5 us; the launch traced here: 48.3 us
  blocking collectives  19.7 us (41%)
  starting transfers between devices  17.7 us (36%)
  Pallas kernels  9.19 us (19%)
  waiting for transfers between devices  1.61 us (3%)
    all_to_all x1, blocking collectives, per_device(): lined = lax.all_to_all(lined, 'chan', 0, 0, tiled=True)  19.7 us
    ppermute x5, starting transfers between devices, later(): return lax.ppermute(block, ('chan', 'tm'), route)  17.7 us
    pallas_call x1, Pallas kernels, local_plane(): pl.pallas_call(local_kernel, in_specs=[pl.BlockSpec(memory_space=pltpu.SM...  3.62 us
    pallas_call x1, Pallas kernels, boxcars_later(): pl.pallas_call(later_kernel, in_specs=[pl.BlockSpec(memory_space=pltpu.SM...  1.86 us
    ppermute x5, waiting for transfers between devices, later(): return lax.ppermute(block, ('chan', 'tm'), route)  1.61 us
    pallas_call x1, Pallas kernels, boxcars_first(): pl.pallas_call(first_kernel, in_specs=[pl.BlockSpec(memory_space=pltpu.SM...  1.59 us
    pallas_call x1, Pallas kernels, final_plane(): pl.pallas_call(final_kernel, out_shape=[jax.ShapeDtypeStruct((BEAMS, ROWS...  1.13 us
    pallas_call x1, Pallas kernels, gather_shifted(): pl.pallas_call(gather_kernel, in_specs=[pl.BlockSpec(memory_space=pltpu.S...  0.99 us
  transfers between devices with their start and end apart: 5, of which 1 were waited for; matrix products, arithmetic and copies ran while one was open for 0% of the time, Pallas kernels for 4%

profile of v3, /device:TPU:1, one launch (start us, length us, event | category | flops | bytes accessed | tf_op | source)
XLA Modules:
  0.0 48.3 jit_solution(11791324588093977772)
XLA Ops:
  0.0 0.0 copy-start
  0.0 3.6 %local_plane.1 = (f32[64,8,128]{2,1,0:T(8,128)S(1)}, f32[48,8,128]{2,1,0:T(8,128)S(1)}, f32[30,8,128]{2,1,0:T(8,128)S(1)}, f32[23,8,128]{2,1,0:T(8,128)S(1)}, f32[10,8,128]{2,1,0:T(8,128)S(1)}) custom-call(s32[1]{0:T(128)} %bitcast.q_ref, s32[32,2,128]{2,1,0:T(2,128)} %constant.10.clone.table_hbm, f32[1,512]{1,0:T(1,128)} %bitcast.6, bf16[2,512,512]{2,1,0:T(8,128)(2,1)} %x_hbm.1), custom_call_target="tpu_custom_call" | custom-call | tf_op jit(solution)/shard_map/local_plane/pallas_call | solution.py:176
  3.6 4.5 %collective-permute-start = (f32[48,8,128]{2,1,0:T(8,128)S(1)}, f32[48,8,128]{2,1,0:T(8,128)S(1)}, u32[]{:S(2)}, u32[]{:S(2)}) collective-permute-start(f32[48,8,128]{2,1,0:T(8,128)S(1)} %get-tuple-element.13), channel_id=1, source_target_pairs={{0,1},{1,2},{2,3},{3,4},{4,5},{5,6},{6,7},{8,9},{9,10},{10,11},{11... | collective-permute-start | bytes 589832 | tf_op jit(solution)/shard_map/ppermute | solution.py:408
  8.1 3.1 %collective-permute-start.1 = (f32[30,8,128]{2,1,0:T(8,128)S(1)}, f32[30,8,128]{2,1,0:T(8,128)S(1)}, u32[]{:S(2)}, u32[]{:S(2)}) collective-permute-start(f32[30,8,128]{2,1,0:T(8,128)S(1)} %get-tuple-element.14), channel_id=1, source_target_pairs={{0,2},{1,3},{2,4},{3,5},{4,6},{5,7},{8,10},{9,11},{10,12},{11,13},... | collective-permute-start | bytes 368648 | tf_op jit(solution)/shard_map/ppermute | solution.py:408
  11.3 3.4 %collective-permute-start.2 = (f32[23,8,128]{2,1,0:T(8,128)S(1)}, f32[23,8,128]{2,1,0:T(8,128)S(1)}, u32[]{:S(2)}, u32[]{:S(2)}) collective-permute-start(f32[23,8,128]{2,1,0:T(8,128)S(1)} %get-tuple-element.15), channel_id=1, source_target_pairs={{0,3},{1,4},{2,5},{3,6},{4,7},{8,11},{9,12},{10,13},{11,14},{12,15... | collective-permute-start | bytes 282632 | tf_op jit(solution)/shard_map/ppermute | solution.py:408
  14.7 1.3 %collective-permute-start.3 = (f32[10,8,128]{2,1,0:T(8,128)S(1)}, f32[10,8,128]{2,1,0:T(8,128)S(1)}, u32[]{:S(2)}, u32[]{:S(2)}) collective-permute-start(f32[10,8,128]{2,1,0:T(8,128)S(1)} %get-tuple-element.16), channel_id=1, source_target_pairs={{0,4},{1,5},{2,6},{3,7},{8,12},{9,13},{10,14},{11,15},{16,20},{17,... | collective-permute-start | bytes 122888 | tf_op jit(solution)/shard_map/ppermute | solution.py:408
  16.0 1.6 %collective-permute-done.3.r4 = f32[10,8,128]{2,1,0:T(8,128)S(1)} collective-permute-done((f32[10,8,128]{2,1,0:T(8,128)S(1)}, f32[10,8,128]{2,1,0:T(8,128)S(1)}, u32[]{:S(2)}, u32[]{:S(2)}) %collective-permute-start.3) | collective-permute-done | bytes 40992 | tf_op jit(solution)/shard_map/ppermute | solution.py:408
  17.6 0.0 collective-permute-done.2.r3
  17.6 0.0 collective-permute-done.1.r2
  17.6 0.0 collective-permute-done.r1
  17.6 1.0 %gather_shifted.1 = f32[512,128]{1,0:T(8,128)S(1)} custom-call(s32[1]{0:T(128)} %bitcast.q_ref, s32[32,2,128]{2,1,0:T(2,128)} %constant.10.clone.table_hbm, f32[64,8,128]{2,1,0:T(8,128)S(1)} %get-tuple-element.12.o0, f32[48,8,128]{2,1,0:T(8,128)S(1)} %collective-permute-done.r1, f32[30,8,128]{2,1,0:T(8,128)S(1)} %collective-permute-done.1.r2, ...), custom_call_target="tpu_custom_call" | custom-call | tf_op jit(solution)/shard_map/gather_shifted/pallas_call | solution.py:229
  18.6 19.7 %all_to_all.11 = f32[32,16,128]{2,1,0:T(8,128)S(1)} all-to-all(f32[32,16,128]{2,1,0:T(8,128)S(1)} %bitcast.4), channel_id=1, replica_groups=mesh['chan'=32,'tm'=8] {'chan'}, dimensions={0} | all-to-all | bytes 524288 | tf_op jit(solution)/shard_map/all_to_all | solution.py:417
  38.4 1.1 %final_plane.1 = (f32[2,64,512]{2,1,0:T(8,128)S(1)}, f32[2,64,128]{2,1,0:T(8,128)S(1)}) custom-call(f32[512,128]{1,0:T(8,128)S(1)} %bitcast.5), custom_call_target="tpu_custom_call" | custom-call | tf_op jit(solution)/shard_map/final_plane/pallas_call | solution.py:272
  39.5 5.3 %collective-permute-start.4 = (f32[2,64,128]{2,1,0:T(8,128)S(1)}, f32[2,64,128]{2,1,0:T(8,128)S(1)}, u32[]{:S(2)}, u32[]{:S(2)}) collective-permute-start(f32[2,64,128]{2,1,0:T(8,128)S(1)} %get-tuple-element.18), channel_id=1, source_target_pairs={{0,1},{1,2},{2,3},{3,4},{4,5},{5,6},{6,7},{8,9},{9,10},{10,11},{11... | collective-permute-start | bytes 196616 | tf_op jit(solution)/shard_map/ppermute | solution.py:408
  44.8 0.0 copy-done
  44.8 1.9 %boxcars_later.1.rest = f32[2,6,64,512]{3,2,1,0:T(8,128)} custom-call(s32[6]{0:T(128)S(1)} %copy-done, f32[2,64,512]{2,1,0:T(8,128)S(1)} %get-tuple-element.17.main), custom_call_target="tpu_custom_call" | custom-call | flops 301989888 | bytes 2097152 | tf_op jit(solution)/shard_map/boxcars_later/pallas_call | solution.py:360
  46.7 0.0 collective-permute-done.4.tail
  46.7 1.6 %boxcars_first.1 = f32[2,6,64,512]{3,2,1,0:T(8,128)} custom-call(s32[6]{0:T(128)S(1)} %copy-done, f32[2,64,512]{2,1,0:T(8,128)S(1)} %get-tuple-element.17.main, f32[2,64,128]{2,1,0:T(8,128)S(1)} %collective-permute-done.4.tail, f32[2,6,64,512]{3,2,1,0:T(8,128)} %boxcars_later.1.rest), custom_call_target="tpu_custom_call", output_to_operand_aliasing={{}: (3, {})} | custom-call | tf_op jit(solution)/shard_map/boxcars_first/pallas_call | solution.py:381
Async XLA Ops:
  0.0 44.8 %copy-start = (s32[6]{0:T(128)S(1)}, s32[6]{0:T(128)}, u32[]{:S(2)}) copy-start(s32[6]{0:T(128)} %widths.3) | copy-start | bytes 76
  3.6 14.0 %collective-permute-start = (f32[48,8,128]{2,1,0:T(8,128)S(1)}, f32[48,8,128]{2,1,0:T(8,128)S(1)}, u32[]{:S(2)}, u32[]{:S(2)}) collective-permute-start(f32[48,8,128]{2,1,0:T(8,128)S(1)} %get-tuple-element.13), channel_id=1, source_target_pairs={{0,1},{1,2},{2,3},{3,4},{4,5},{5,6},{6,7},{8,9},{9,10},{10,11},{11... | collective-permute-start | bytes 589832 | tf_op jit(solution)/shard_map/ppermute | solution.py:408
  8.1 9.5 %collective-permute-start.1 = (f32[30,8,128]{2,1,0:T(8,128)S(1)}, f32[30,8,128]{2,1,0:T(8,128)S(1)}, u32[]{:S(2)}, u32[]{:S(2)}) collective-permute-start(f32[30,8,128]{2,1,0:T(8,128)S(1)} %get-tuple-element.14), channel_id=1, source_target_pairs={{0,2},{1,3},{2,4},{3,5},{4,6},{5,7},{8,10},{9,11},{10,12},{11,13},... | collective-permute-start | bytes 368648 | tf_op jit(solution)/shard_map/ppermute | solution.py:408
  11.3 6.4 %collective-permute-start.2 = (f32[23,8,128]{2,1,0:T(8,128)S(1)}, f32[23,8,128]{2,1,0:T(8,128)S(1)}, u32[]{:S(2)}, u32[]{:S(2)}) collective-permute-start(f32[23,8,128]{2,1,0:T(8,128)S(1)} %get-tuple-element.15), channel_id=1, source_target_pairs={{0,3},{1,4},{2,5},{3,6},{4,7},{8,11},{9,12},{10,13},{11,14},{12,15... | collective-permute-start | bytes 282632 | tf_op jit(solution)/shard_map/ppermute | solution.py:408
  14.7 2.9 %collective-permute-start.3 = (f32[10,8,128]{2,1,0:T(8,128)S(1)}, f32[10,8,128]{2,1,0:T(8,128)S(1)}, u32[]{:S(2)}, u32[]{:S(2)}) collective-permute-start(f32[10,8,128]{2,1,0:T(8,128)S(1)} %get-tuple-element.16), channel_id=1, source_target_pairs={{0,4},{1,5},{2,6},{3,7},{8,12},{9,13},{10,14},{11,15},{16,20},{17,... | collective-permute-start | bytes 122888 | tf_op jit(solution)/shard_map/ppermute | solution.py:408
  39.5 7.2 %collective-permute-start.4 = (f32[2,64,128]{2,1,0:T(8,128)S(1)}, f32[2,64,128]{2,1,0:T(8,128)S(1)}, u32[]{:S(2)}, u32[]{:S(2)}) collective-permute-start(f32[2,64,128]{2,1,0:T(8,128)S(1)} %get-tuple-element.18), channel_id=1, source_target_pairs={{0,1},{1,2},{2,3},{3,4},{4,5},{5,6},{6,7},{8,9},{9,10},{10,11},{11... | collective-permute-start | bytes 196616 | tf_op jit(solution)/shard_map/ppermute | solution.py:408

commit v4 on v3

--- a/solution.py
+++ b/solution.py
@@ -35,7 +35,17 @@
     for (q, a), (first, number) in units.items():
         for h in range(first, first + number):
             counts[q, h // PER] += 1
-    sizes = [int(n) for n in counts.max(axis=0)]
+    buffers = np.tile(np.arange(REACH), (PARTS, 1))
+    last = REACH - 1
+    few = (counts[:, last] == 0) & (counts[:, last - 1] <= counts[:, last].max())
+    buffers[few, last - 1] = last
+    sizes = [0] * REACH
+    distances = np.zeros((PARTS, REACH), np.int32)
+    for q in range(PARTS):
+        for k in range(REACH):
+            if counts[q, k]:
+                sizes[buffers[q, k]] = max(sizes[buffers[q, k]], int(counts[q, k]))
+                distances[q, buffers[q, k]] = k
     starts = [sum(sizes[:k]) for k in range(REACH)]
     spare = sum(sizes)
     table = np.full((PARTS, 2, LANES), spare, np.int32)
@@ -45,14 +55,15 @@
             first, number = units[q, a]
             for i in range(number):
                 h = first + i
-                table[q, 0, a * UNITS + i] = free[h // PER]
+                k = buffers[q, h // PER]
+                table[q, 0, a * UNITS + i] = free[k]
                 place = (a * PER + h % PER) * 2 + (i >= PER)
-                table[q, 1, place] = free[h // PER]
-                free[h // PER] += 1
-    return sizes, starts, spare, table, counts
-
-
-SIZES, STARTS, SPARE, TABLE, COUNTS = packing()
+                table[q, 1, place] = free[k]
+                free[k] += 1
+    return sizes, starts, spare, table, distances
+
+
+SIZES, STARTS, SPARE, TABLE, DISTANCES = packing()
 
 
 def split(x):
@@ -70,8 +81,7 @@
     for upper, lower in zip(groups[0::2], groups[1::2]):
         trials = []
         for e in range(len(upper)):
-            early = roll(upper[e], e)
-            trials += [lower[e] + early, lower[e] + roll(early, 1)]
+            trials += [lower[e] + roll(upper[e], e), lower[e] + roll(upper[e], e + 1)]
         merged.append(trials)
     return merged
 
@@ -100,7 +110,7 @@
                 upper = take(source, base + a, 8, 0, tiles)
                 lower = take(source, base + trials + a, 8, 0, tiles)
                 early = pltpu.roll(upper, a, 1, stride=1, stride_axis=0)
-                late = pltpu.roll(early, 1, 1)
+                late = pltpu.roll(upper, a + 1, 1, stride=1, stride_axis=0)
                 put(target, base + 2 * a, 2, lower + early)
                 put(target, base + 2 * a + 1, 2, lower + late)
         source, target = target, source
@@ -158,7 +168,7 @@
             [jnp.concatenate([base[8 * g : 8 * g + 8], blank], axis=1)]
             for g in range(8)
         ]
-        merge_rows(groups, one, two.at[b])
+        merge_rows(groups, one.at[b], two.at[b])
     fetch_slots.wait()
     odd = lax.broadcasted_iota(jnp.int32, (8, UNITS * LANES), 0) & 2 != 0
     for a in range(TILES):
@@ -186,7 +196,7 @@
             pltpu.SMEM((2, LANES), jnp.int32),
             pltpu.VMEM((1, CHANS), jnp.float32),
             pltpu.VMEM((BEAMS, CHANS, SPAN), jnp.bfloat16),
-            pltpu.VMEM((WIDE // LANES, ROWS, LANES), jnp.float32),
+            pltpu.VMEM((BEAMS, WIDE // LANES, ROWS, LANES), jnp.float32),
             pltpu.VMEM((BEAMS, WIDE // LANES, ROWS, LANES), jnp.float32),
             pltpu.VMEM((SPARE + 1, 8, LANES), jnp.float32),
             pltpu.SemaphoreType.DMA((2 * BEAMS + 2,)),
@@ -201,10 +211,8 @@
     )
 
 
-def gather_kernel(
-    q_ref, table_hbm, o0, r1, r2, r3, r4, out, slots, packed, held, sem
-):
-    fetch_slots = pltpu.make_async_copy(table_hbm.at[q_ref[0]], slots, sem)
+def gather_kernel(q_ref, table, o0, r1, r2, r3, r4, out, slots, packed, held, sem):
+    fetch_slots = pltpu.make_async_copy(table.at[q_ref[0]], slots, sem)
     fetch_slots.start()
     for k, piece in enumerate((o0, r1, r2, r3, r4)):
         packed[pl.ds(STARTS[k], SIZES[k])] = piece[...]
@@ -230,9 +238,8 @@
         gather_kernel,
         in_specs=[
             pl.BlockSpec(memory_space=pltpu.SMEM),
-            pl.BlockSpec(memory_space=pltpu.HBM),
         ]
-        + [vmem] * REACH,
+        + [vmem] * (1 + REACH),
         out_shape=jax.ShapeDtypeStruct((PARTS * 16, LANES), jnp.float32),
         scratch_shapes=[
             pltpu.SMEM((2, LANES), jnp.int32),
@@ -242,7 +249,7 @@
         ],
         compiler_params=pltpu.CompilerParams(vmem_limit_bytes=24 << 20),
         name="gather_shifted",
-    )(q, pltpu.with_memory_space_constraint(TABLE, pltpu.HBM), *pieces)
+    )(q, TABLE, *pieces)
 
 
 def final_kernel(x_ref, main, tail, one, two):
@@ -259,7 +266,7 @@
                 ]
                 trials.append(jnp.concatenate(chunks + [blank], axis=1))
             groups.append(trials)
-        plane = merge_rows(groups, one, two)
+        plane = merge_rows(groups, one.at[b], two.at[b])
         main[b] = take(plane, 0, ROWS, 0, SPAN // LANES)
         tail[b] = jnp.where(
             lane < LANES // 2,
@@ -276,8 +283,8 @@
             jax.ShapeDtypeStruct((BEAMS, ROWS, LANES), jnp.float32),
         ],
         scratch_shapes=[
-            pltpu.VMEM((WIDE // LANES, ROWS, LANES), jnp.float32),
-            pltpu.VMEM((WIDE // LANES, ROWS, LANES), jnp.float32),
+            pltpu.VMEM((BEAMS, WIDE // LANES, ROWS, LANES), jnp.float32),
+            pltpu.VMEM((BEAMS, WIDE // LANES, ROWS, LANES), jnp.float32),
         ],
         compiler_params=pltpu.CompilerParams(vmem_limit_bytes=24 << 20),
         name="final_plane",
@@ -315,9 +322,11 @@
             ]
 
 
-def later_kernel(widths, main, out, held, sems):
+def later_kernel(widths, main, out, bands_out, norms_out, held, sems):
     bands = boxcar_bands(widths)
     norms = boxcar_norms(widths)
+    bands_out[...] = bands
+    norms_out[...] = norms
     parts = []
     for c in range(SPAN // LANES):
         tile = main[:, :, pl.ds(c * LANES, LANES)].reshape(BEAMS * ROWS, LANES)
@@ -337,7 +346,7 @@
         copy.wait()
 
 
-def first_kernel(widths, main, tail, rest, out, held, sem):
+def first_kernel(main, tail, bands, norms, rest, out, held, sem):
     del rest
     lane = lax.broadcasted_iota(jnp.int32, (BEAMS * ROWS, LANES), 1)
     edge = tail[...].reshape(BEAMS * ROWS, LANES)
@@ -346,7 +355,7 @@
     here = here + jnp.where(lane < LANES // 2, edge, 0.0)
     before = jnp.concatenate(split(before), axis=0)
     here = jnp.concatenate(split(here), axis=0)
-    boxcar_tile(before, here, boxcar_bands(widths), boxcar_norms(widths), held, 0)
+    boxcar_tile(before, here, bands[...], norms[...], held, 0)
     copy = pltpu.make_async_copy(held, out.at[:, :, :, pl.ds(0, LANES)], sem)
     copy.start()
     copy.wait()
@@ -363,8 +372,16 @@
             pl.BlockSpec(memory_space=pltpu.SMEM),
             pl.BlockSpec(memory_space=pltpu.VMEM),
         ],
-        out_specs=pl.BlockSpec(memory_space=pltpu.HBM),
-        out_shape=OUT,
+        out_specs=[
+            pl.BlockSpec(memory_space=pltpu.HBM),
+            pl.BlockSpec(memory_space=pltpu.VMEM),
+            pl.BlockSpec(memory_space=pltpu.VMEM),
+        ],
+        out_shape=[
+            OUT,
+            jax.ShapeDtypeStruct((2 * LANES, NBOX * LANES), jnp.bfloat16),
+            jax.ShapeDtypeStruct((1, NBOX * LANES), jnp.float32),
+        ],
         scratch_shapes=[
             pltpu.VMEM((BEAMS, NBOX, ROWS, lanes), jnp.float32),
             pltpu.SemaphoreType.DMA((lanes // LANES,)),
@@ -377,31 +394,28 @@
     )(widths, main)
 
 
-def boxcars_first(main, tail, rest, widths):
+def boxcars_first(main, tail, bands, norms, rest):
     return pl.pallas_call(
         first_kernel,
-        in_specs=[
-            pl.BlockSpec(memory_space=pltpu.SMEM),
-            pl.BlockSpec(memory_space=pltpu.VMEM),
-            pl.BlockSpec(memory_space=pltpu.VMEM),
-            pl.BlockSpec(memory_space=pltpu.HBM),
-        ],
+        in_specs=[pl.BlockSpec(memory_space=pltpu.VMEM)] * 4
+        + [pl.BlockSpec(memory_space=pltpu.HBM)],
         out_specs=pl.BlockSpec(memory_space=pltpu.HBM),
         out_shape=OUT,
-        input_output_aliases={3: 0},
+        input_output_aliases={4: 0},
         scratch_shapes=[
             pltpu.VMEM((BEAMS, NBOX, ROWS, LANES), jnp.float32),
             pltpu.SemaphoreType.DMA,
         ],
         compiler_params=pltpu.CompilerParams(vmem_limit_bytes=24 << 20),
         name="boxcars_first",
-    )(widths, main, tail, rest)
-
-
-def later(block, distance):
+    )(main, tail, bands, norms, rest)
+
+
+def later(block, buffer):
     route = []
     for part in range(PARTS):
-        if COUNTS[PARTS - 1 - part, distance]:
+        distance = int(DISTANCES[PARTS - 1 - part, buffer])
+        if distance:
             for i in range(SEGMENTS - distance):
                 sender = part * SEGMENTS + i
                 route.append((sender, sender + distance))
@@ -417,8 +431,8 @@
     lined = lax.all_to_all(lined, "chan", 0, 0, tiled=True)
     main, tail = final_plane(lined)
     tail = later(tail, 1)
-    rest = boxcars_later(main, box_widths)
-    return boxcars_first(main, tail, rest, box_widths)
+    rest, bands, norms = boxcars_later(main, box_widths)
+    return boxcars_first(main, tail, bands, norms, rest)
 
 
 def solution(mesh):

time: 48.5 us -> 47.8 us (0.986)
  Pallas kernels: 9.19 us -> 7.45 us
  local copies, waits for them, and re-layouts: 0.01 us -> 0.76 us
  starting transfers between devices: 17.7 us -> 18.3 us
    unnamed x2 -> x4, local copies, waits for them, and re-layouts: 0.01 us -> 0.76 us
    pallas_call x1, Pallas kernels: 3.62 us -> 2.96 us  [local_plane(): pl.pallas_call(local_kernel, in_specs=[pl.BlockSpec(memory_space=pltpu.SM...]
    ppermute x5, starting transfers between devices: 17.7 us -> 18.3 us  [later(): return lax.ppermute(block, ('chan', 'tm'), route)]
    pallas_call x1, Pallas kernels: 1.59 us -> 1.03 us  [boxcars_first(): pl.pallas_call(first_kernel, in_specs=[pl.BlockSpec(memory_space=pltpu.VM...]
where the time goes in v4:
time: 47.8 us; the launch traced here: 47.5 us
  blocking collectives  19.3 us (40%)
  starting transfers between devices  18.3 us (38%)
  Pallas kernels  7.45 us (16%)
  waiting for transfers between devices  1.61 us (3%)
  local copies, waits for them, and re-layouts  0.76 us (2%)
    all_to_all x1, blocking collectives, per_device(): lined = lax.all_to_all(lined, 'chan', 0, 0, tiled=True)  19.3 us
    ppermute x5, starting transfers between devices, later(): return lax.ppermute(block, ('chan', 'tm'), route)  18.3 us
    pallas_call x1, Pallas kernels, local_plane(): pl.pallas_call(local_kernel, in_specs=[pl.BlockSpec(memory_space=pltpu.SM...  2.96 us
    pallas_call x1, Pallas kernels, boxcars_later(): pl.pallas_call(later_kernel, in_specs=[pl.BlockSpec(memory_space=pltpu.SM...  1.91 us
    ppermute x5, waiting for transfers between devices, later(): return lax.ppermute(block, ('chan', 'tm'), route)  1.61 us
    pallas_call x1, Pallas kernels, boxcars_first(): pl.pallas_call(first_kernel, in_specs=[pl.BlockSpec(memory_space=pltpu.VM...  1.03 us
  transfers between devices with their start and end apart: 5, of which 1 were waited for; matrix products, arithmetic and copies ran while one was open for 0% of the time, Pallas kernels for 4%

profile of v4, /device:TPU:1, one launch (start us, length us, event | category | flops | bytes accessed | tf_op | source)
XLA Modules:
  0.0 47.5 jit_solution(17112872047765915753)
XLA Ops:
  0.0 0.0 copy-start.1
  0.0 3.0 %local_plane.1 = (f32[64,8,128]{2,1,0:T(8,128)S(1)}, f32[48,8,128]{2,1,0:T(8,128)S(1)}, f32[30,8,128]{2,1,0:T(8,128)S(1)}, f32[23,8,128]{2,1,0:T(8,128)S(1)}, f32[10,8,128]{2,1,0:T(8,128)S(1)}) custom-call(s32[1]{0:T(128)} %bitcast.q_ref, s32[32,2,128]{2,1,0:T(2,128)} %constant.10.clone.table_hbm.table, f32[1,512]{1,0:T(1,128)} %bitcast.6, ...), custom_call_target="tpu_custom_call" | custom-call | tf_op jit(solution)/shard_map/local_plane/pallas_call | solution.py:186
  3.0 4.5 %collective-permute-start = (f32[48,8,128]{2,1,0:T(8,128)S(1)}, f32[48,8,128]{2,1,0:T(8,128)S(1)}, u32[]{:S(2)}, u32[]{:S(2)}) collective-permute-start(f32[48,8,128]{2,1,0:T(8,128)S(1)} %get-tuple-element.16), channel_id=1, source_target_pairs={{0,1},{1,2},{2,3},{3,4},{4,5},{5,6},{6,7},{8,9},{9,10},{10,11},{11... | collective-permute-start | bytes 589832 | tf_op jit(solution)/shard_map/ppermute | solution.py:422
  7.5 3.1 %collective-permute-start.1 = (f32[30,8,128]{2,1,0:T(8,128)S(1)}, f32[30,8,128]{2,1,0:T(8,128)S(1)}, u32[]{:S(2)}, u32[]{:S(2)}) collective-permute-start(f32[30,8,128]{2,1,0:T(8,128)S(1)} %get-tuple-element.17), channel_id=1, source_target_pairs={{0,2},{1,3},{2,4},{3,5},{4,6},{5,7},{8,10},{9,11},{10,12},{11,13},... | collective-permute-start | bytes 368648 | tf_op jit(solution)/shard_map/ppermute | solution.py:422
  10.6 3.4 %collective-permute-start.2 = (f32[23,8,128]{2,1,0:T(8,128)S(1)}, f32[23,8,128]{2,1,0:T(8,128)S(1)}, u32[]{:S(2)}, u32[]{:S(2)}) collective-permute-start(f32[23,8,128]{2,1,0:T(8,128)S(1)} %get-tuple-element.18), channel_id=1, source_target_pairs={{0,3},{1,4},{2,5},{3,6},{4,7},{8,11},{9,12},{10,13},{11,14},{12,15... | collective-permute-start | bytes 282632 | tf_op jit(solution)/shard_map/ppermute | solution.py:422
  14.1 1.3 %collective-permute-start.3 = (f32[10,8,128]{2,1,0:T(8,128)S(1)}, f32[10,8,128]{2,1,0:T(8,128)S(1)}, u32[]{:S(2)}, u32[]{:S(2)}) collective-permute-start(f32[10,8,128]{2,1,0:T(8,128)S(1)} %get-tuple-element.19), channel_id=1, source_target_pairs={{0,4},{1,5},{2,6},{3,7},{8,12},{9,13},{10,14},{11,15},{16,20},{17,... | collective-permute-start | bytes 122888 | tf_op jit(solution)/shard_map/ppermute | solution.py:422
  15.4 1.6 %collective-permute-done.3.r4 = f32[10,8,128]{2,1,0:T(8,128)S(1)} collective-permute-done((f32[10,8,128]{2,1,0:T(8,128)S(1)}, f32[10,8,128]{2,1,0:T(8,128)S(1)}, u32[]{:S(2)}, u32[]{:S(2)}) %collective-permute-start.3) | collective-permute-done | bytes 40992 | tf_op jit(solution)/shard_map/ppermute | solution.py:422
  17.0 0.0 collective-permute-done.2.r3
  17.0 0.0 collective-permute-done.1.r2
  17.0 0.0 collective-permute-done.r1
  17.0 0.0 copy-start
  17.0 0.7 %copy-done = s32[32,2,128]{2,1,0:T(2,128)S(1)} copy-done((s32[32,2,128]{2,1,0:T(2,128)S(1)}, s32[32,2,128]{2,1,0:T(2,128)}, u32[]{:S(2)}) %copy-start) | copy-done | bytes 32792
  17.7 0.9 %gather_shifted.1 = f32[512,128]{1,0:T(8,128)S(1)} custom-call(s32[1]{0:T(128)} %bitcast.q_ref, s32[32,2,128]{2,1,0:T(2,128)S(1)} %copy-done, f32[64,8,128]{2,1,0:T(8,128)S(1)} %get-tuple-element.15.o0, f32[48,8,128]{2,1,0:T(8,128)S(1)} %collective-permute-done.r1, f32[30,8,128]{2,1,0:T(8,128)S(1)} %collective-permute-done.1.r2, ...), custom_call_target="tpu_custom_call" | custom-call | tf_op jit(solution)/shard_map/gather_shifted/pallas_call | solution.py:237
  18.6 19.3 %all_to_all.11 = f32[32,16,128]{2,1,0:T(8,128)S(1)} all-to-all(f32[32,16,128]{2,1,0:T(8,128)S(1)} %bitcast.4), channel_id=1, replica_groups=mesh['chan'=32,'tm'=8] {'chan'}, dimensions={0} | all-to-all | bytes 524288 | tf_op jit(solution)/shard_map/all_to_all | solution.py:431
  37.9 0.7 %final_plane.1 = (f32[2,64,512]{2,1,0:T(8,128)S(1)}, f32[2,64,128]{2,1,0:T(8,128)S(1)}) custom-call(f32[512,128]{1,0:T(8,128)S(1)} %bitcast.5), custom_call_target="tpu_custom_call" | custom-call | tf_op jit(solution)/shard_map/final_plane/pallas_call | solution.py:279
  38.6 5.9 %collective-permute-start.4 = (f32[2,64,128]{2,1,0:T(8,128)S(1)}, f32[2,64,128]{2,1,0:T(8,128)S(1)}, u32[]{:S(2)}, u32[]{:S(2)}) collective-permute-start(f32[2,64,128]{2,1,0:T(8,128)S(1)} %get-tuple-element.21), channel_id=1, source_target_pairs={{0,1},{1,2},{2,3},{3,4},{4,5},{5,6},{6,7},{8,9},{9,10},{10,11},{11... | collective-permute-start | bytes 196616 | tf_op jit(solution)/shard_map/ppermute | solution.py:422
  44.5 0.0 copy-done.1
  44.5 1.9 %boxcars_later.1 = (f32[2,6,64,512]{3,2,1,0:T(8,128)}, bf16[256,768]{1,0:T(8,128)(2,1)S(1)}, f32[1,768]{1,0:T(1,128)S(1)}) custom-call(s32[6]{0:T(128)S(1)} %copy-done.1, f32[2,64,512]{2,1,0:T(8,128)S(1)} %get-tuple-element.20.main), custom_call_target="tpu_custom_call" | custom-call | flops 301989888 | bytes 2097152 | tf_op jit(solution)/shard_map/boxcars_later/pallas_call | solution.py:369
  46.4 0.0 collective-permute-done.4.tail
  46.4 1.0 %boxcars_first.1 = f32[2,6,64,512]{3,2,1,0:T(8,128)} custom-call(f32[2,64,512]{2,1,0:T(8,128)S(1)} %get-tuple-element.20.main, f32[2,64,128]{2,1,0:T(8,128)S(1)} %collective-permute-done.4.tail, bf16[256,768]{1,0:T(8,128)(2,1)S(1)} %get-tuple-element.22.bands, f32[1,768]{1,0:T(1,128)S(1)} %get-tuple-element.23.norms, ...), custom_call_target="tpu_custom_call", output_to_operand_aliasing={{}: (4, {})} | custom-call | tf_op jit(solution)/shard_map/boxcars_first/pallas_call | solution.py:398
Async XLA Ops:
  0.0 44.5 %copy-start.1 = (s32[6]{0:T(128)S(1)}, s32[6]{0:T(128)}, u32[]{:S(2)}) copy-start(s32[6]{0:T(128)} %widths.1) | copy-start | bytes 76
  3.0 14.0 %collective-permute-start = (f32[48,8,128]{2,1,0:T(8,128)S(1)}, f32[48,8,128]{2,1,0:T(8,128)S(1)}, u32[]{:S(2)}, u32[]{:S(2)}) collective-permute-start(f32[48,8,128]{2,1,0:T(8,128)S(1)} %get-tuple-element.16), channel_id=1, source_target_pairs={{0,1},{1,2},{2,3},{3,4},{4,5},{5,6},{6,7},{8,9},{9,10},{10,11},{11... | collective-permute-start | bytes 589832 | tf_op jit(solution)/shard_map/ppermute | solution.py:422
  7.5 9.5 %collective-permute-start.1 = (f32[30,8,128]{2,1,0:T(8,128)S(1)}, f32[30,8,128]{2,1,0:T(8,128)S(1)}, u32[]{:S(2)}, u32[]{:S(2)}) collective-permute-start(f32[30,8,128]{2,1,0:T(8,128)S(1)} %get-tuple-element.17), channel_id=1, source_target_pairs={{0,2},{1,3},{2,4},{3,5},{4,6},{5,7},{8,10},{9,11},{10,12},{11,13},... | collective-permute-start | bytes 368648 | tf_op jit(solution)/shard_map/ppermute | solution.py:422
  10.6 6.4 %collective-permute-start.2 = (f32[23,8,128]{2,1,0:T(8,128)S(1)}, f32[23,8,128]{2,1,0:T(8,128)S(1)}, u32[]{:S(2)}, u32[]{:S(2)}) collective-permute-start(f32[23,8,128]{2,1,0:T(8,128)S(1)} %get-tuple-element.18), channel_id=1, source_target_pairs={{0,3},{1,4},{2,5},{3,6},{4,7},{8,11},{9,12},{10,13},{11,14},{12,15... | collective-permute-start | bytes 282632 | tf_op jit(solution)/shard_map/ppermute | solution.py:422
  14.1 2.9 %collective-permute-start.3 = (f32[10,8,128]{2,1,0:T(8,128)S(1)}, f32[10,8,128]{2,1,0:T(8,128)S(1)}, u32[]{:S(2)}, u32[]{:S(2)}) collective-permute-start(f32[10,8,128]{2,1,0:T(8,128)S(1)} %get-tuple-element.19), channel_id=1, source_target_pairs={{0,4},{1,5},{2,6},{3,7},{8,12},{9,13},{10,14},{11,15},{16,20},{17,... | collective-permute-start | bytes 122888 | tf_op jit(solution)/shard_map/ppermute | solution.py:422
  17.0 0.8 %copy-start = (s32[32,2,128]{2,1,0:T(2,128)S(1)}, s32[32,2,128]{2,1,0:T(2,128)}, u32[]{:S(2)}) copy-start(s32[32,2,128]{2,1,0:T(2,128)} %constant.10.clone.table_hbm.table) | copy-start | bytes 98308
  38.6 7.9 %collective-permute-start.4 = (f32[2,64,128]{2,1,0:T(8,128)S(1)}, f32[2,64,128]{2,1,0:T(8,128)S(1)}, u32[]{:S(2)}, u32[]{:S(2)}) collective-permute-start(f32[2,64,128]{2,1,0:T(8,128)S(1)} %get-tuple-element.21), channel_id=1, source_target_pairs={{0,1},{1,2},{2,3},{3,4},{4,5},{5,6},{6,7},{8,9},{9,10},{10,11},{11... | collective-permute-start | bytes 196616 | tf_op jit(solution)/shard_map/ppermute | solution.py:422

commit v5 on v4

--- a/solution.py
+++ b/solution.py
@@ -21,49 +21,74 @@
 PER = SPAN // LANES
 
 
+def tails(a):
+    reach = [sum((i >> level) + 1 >> 1 for level in range(6)) for i in range(4 * a, 4 * a + 4)]
+    return max(reach[:2]), max(reach[2:])
+
+
+def tile_span(q, a):
+    delay = 4 * q * a
+    first, second = tails(a)
+    end = (delay & (LANES - 1)) + SPAN
+    if isinstance(q, int):
+        end += max(first, 2 * q + second)
+    else:
+        end += jnp.maximum(first, 2 * q + second)
+    return delay >> 7, (end + LANES - 1) >> 7
+
+
 def packing():
-    tail = [sum(((i >> level) + 1) // 2 for level in range(6)) for i in range(ROWS)]
-    units = {}
+    counts = np.zeros((PARTS, REACH), np.int32)
     for q in range(PARTS):
         for a in range(TILES):
-            delay = 4 * q * a
-            ends = [
-                delay % LANES + 2 * q * (r // 2) + SPAN + tail[4 * a + r] for r in range(4)
-            ]
-            units[q, a] = (delay // LANES, -(-max(ends) // LANES))
-    counts = np.zeros((PARTS, REACH), np.int32)
-    for (q, a), (first, number) in units.items():
-        for h in range(first, first + number):
-            counts[q, h // PER] += 1
-    buffers = np.tile(np.arange(REACH), (PARTS, 1))
-    last = REACH - 1
-    few = (counts[:, last] == 0) & (counts[:, last - 1] <= counts[:, last].max())
-    buffers[few, last - 1] = last
-    sizes = [0] * REACH
+            first, number = tile_span(q, a)
+            for h in range(first, first + number):
+                counts[q, h // PER] += 1
+    sizes = [64, 48, 30, 23, 10]
+    buffers = np.zeros((PARTS, REACH), np.int32)
     distances = np.zeros((PARTS, REACH), np.int32)
     for q in range(PARTS):
-        for k in range(REACH):
+        taken = {0}
+        for k in range(REACH - 1, 0, -1):
             if counts[q, k]:
-                sizes[buffers[q, k]] = max(sizes[buffers[q, k]], int(counts[q, k]))
-                distances[q, buffers[q, k]] = k
+                fits = [i for i in range(1, REACH) if i not in taken and sizes[i] >= counts[q, k]]
+                buffers[q, k] = fits[-1]
+                distances[q, fits[-1]] = k
+                taken.add(fits[-1])
     starts = [sum(sizes[:k]) for k in range(REACH)]
-    spare = sum(sizes)
-    table = np.full((PARTS, 2, LANES), spare, np.int32)
-    for q in range(PARTS):
-        free = list(starts)
-        for a in range(TILES):
-            first, number = units[q, a]
-            for i in range(number):
-                h = first + i
-                k = buffers[q, h // PER]
-                table[q, 0, a * UNITS + i] = free[k]
-                place = (a * PER + h % PER) * 2 + (i >= PER)
-                table[q, 1, place] = free[k]
-                free[k] += 1
-    return sizes, starts, spare, table, distances
-
-
-SIZES, STARTS, SPARE, TABLE, DISTANCES = packing()
+    return sizes, starts, sum(sizes), buffers, distances
+
+
+SIZES, STARTS, SPARE, BUFFERS, DISTANCES = packing()
+
+
+def first_slots(q, free):
+    for k in range(REACH):
+        slot = STARTS[BUFFERS[0, k]]
+        for band in range(1, PARTS):
+            if BUFFERS[band, k] != BUFFERS[band - 1, k]:
+                slot = jnp.where(q >= band, STARTS[BUFFERS[band, k]], slot)
+        free[k] = slot
+    free[REACH] = SPARE
+
+
+def unit_slots(q, a, free):
+    first, number = tile_span(q, a)
+    at, k = first & (PER - 1), first >> 2
+    here = jnp.minimum(PER - at, number)
+    rest = number - here
+    then = jnp.minimum(rest, PER)
+    p0, p1, p2 = free[k], free[k + 1], free[k + 2]
+    free[k] = p0 + here
+    free[k + 1] = p1 + then
+    free[k + 2] = p2 + rest - then
+    slots = [p0]
+    for i in range(1, PER):
+        slots.append(jnp.where(i < here, p0 + i, p1 + i - here))
+    slots.append(p1 + PER - here)
+    last = jnp.where(here > 1, p1 + PER + 1 - here, p2)
+    slots.append(jnp.where(number > PER + 1, last, SPARE))
+    return slots, at
 
 
 def split(x):
@@ -120,7 +145,6 @@
 
 def local_kernel(
     q_ref,
-    table_hbm,
     scale_hbm,
     x_hbm,
     o0,
@@ -128,7 +152,7 @@
     o2,
     o3,
     o4,
-    slots,
+    free,
     scale,
     x,
     one,
@@ -140,8 +164,6 @@
     q = q_ref[0]
     fetch_scale = pltpu.make_async_copy(scale_hbm, scale, sems.at[2 * BEAMS])
     fetch_scale.start()
-    fetch_slots = pltpu.make_async_copy(table_hbm.at[q], slots, sems.at[2 * BEAMS + 1])
-    fetch_slots.start()
     fetches = []
     for b in range(BEAMS):
         for h in range(2):
@@ -169,15 +191,16 @@
             for g in range(8)
         ]
         merge_rows(groups, one.at[b], two.at[b])
-    fetch_slots.wait()
+    first_slots(q, free)
     odd = lax.broadcasted_iota(jnp.int32, (8, UNITS * LANES), 0) & 2 != 0
     for a in range(TILES):
         rows = [take(two.at[b], 4 * a, 4, 0, WIDE // LANES) for b in range(BEAMS)]
         rows = jnp.concatenate([jnp.concatenate(rows, axis=0), blank], axis=1)
         rows = jnp.where(odd, pltpu.roll(rows, 2 * q, 1), rows)
         rows = pltpu.roll(rows, (4 * q * a) & (LANES - 1), 1)
-        for i in range(UNITS):
-            packed[slots[0, a * UNITS + i]] = rows[:, i * LANES : (i + 1) * LANES]
+        slots, _ = unit_slots(q, a, free)
+        for i, slot in enumerate(slots):
+            packed[slot] = rows[:, i * LANES : (i + 1) * LANES]
     for k, out in enumerate((o0, o1, o2, o3, o4)):
         out[...] = packed[pl.ds(STARTS[k], SIZES[k])]
 
@@ -189,41 +212,40 @@
             pl.BlockSpec(memory_space=pltpu.SMEM),
             pl.BlockSpec(memory_space=pltpu.HBM),
             pl.BlockSpec(memory_space=pltpu.HBM),
-            pl.BlockSpec(memory_space=pltpu.HBM),
         ],
         out_shape=[jax.ShapeDtypeStruct((n, 8, LANES), jnp.float32) for n in SIZES],
         scratch_shapes=[
-            pltpu.SMEM((2, LANES), jnp.int32),
+            pltpu.SMEM((REACH + 3,), jnp.int32),
             pltpu.VMEM((1, CHANS), jnp.float32),
             pltpu.VMEM((BEAMS, CHANS, SPAN), jnp.bfloat16),
             pltpu.VMEM((BEAMS, WIDE // LANES, ROWS, LANES), jnp.float32),
             pltpu.VMEM((BEAMS, WIDE // LANES, ROWS, LANES), jnp.float32),
             pltpu.VMEM((SPARE + 1, 8, LANES), jnp.float32),
-            pltpu.SemaphoreType.DMA((2 * BEAMS + 2,)),
+            pltpu.SemaphoreType.DMA((2 * BEAMS + 1,)),
         ],
         compiler_params=pltpu.CompilerParams(vmem_limit_bytes=24 << 20),
         name="local_plane",
     )(
         q,
-        pltpu.with_memory_space_constraint(TABLE, pltpu.HBM),
         pltpu.with_memory_space_constraint(scale, pltpu.HBM),
         pltpu.with_memory_space_constraint(x, pltpu.HBM),
     )
 
 
-def gather_kernel(q_ref, table, o0, r1, r2, r3, r4, out, slots, packed, held, sem):
-    fetch_slots = pltpu.make_async_copy(table.at[q_ref[0]], slots, sem)
-    fetch_slots.start()
+def gather_kernel(q_ref, o0, r1, r2, r3, r4, out, free, packed, held):
+    q = q_ref[0]
+    first_slots(q, free)
     for k, piece in enumerate((o0, r1, r2, r3, r4)):
         packed[pl.ds(STARTS[k], SIZES[k])] = piece[...]
     packed[SPARE] = jnp.zeros((8, LANES), jnp.float32)
-    fetch_slots.wait()
     for a in range(TILES):
-        for c in range(PER):
-            place = (a * PER + c) * 2
-            held[c, pl.ds(8 * a, 8), :] = (
-                packed[slots[1, place]] + packed[slots[1, place + 1]]
-            )
+        slots, at = unit_slots(q, a, free)
+        rows = pl.ds(8 * a, 8)
+        tiles = [(at + i) & (PER - 1) for i in range(PER)]
+        held[tiles[0], rows, :] = packed[slots[0]] + packed[slots[PER]]
+        held[tiles[1], rows, :] = packed[slots[1]] + packed[slots[PER + 1]]
+        held[tiles[2], rows, :] = packed[slots[2]]
+        held[tiles[3], rows, :] = packed[slots[3]]
     for c in range(PER):
         for r in range(8):
             b, m, i = r >> 2, r >> 1 & 1, r & 1
@@ -236,20 +258,16 @@
     vmem = pl.BlockSpec(memory_space=pltpu.VMEM)
     return pl.pallas_call(
         gather_kernel,
-        in_specs=[
-            pl.BlockSpec(memory_space=pltpu.SMEM),
-        ]
-        + [vmem] * (1 + REACH),
+        in_specs=[pl.BlockSpec(memory_space=pltpu.SMEM)] + [vmem] * REACH,
         out_shape=jax.ShapeDtypeStruct((PARTS * 16, LANES), jnp.float32),
         scratch_shapes=[
-            pltpu.SMEM((2, LANES), jnp.int32),
+            pltpu.SMEM((REACH + 3,), jnp.int32),
             pltpu.VMEM((SPARE + 1, 8, LANES), jnp.float32),
             pltpu.VMEM((PER, 8 * TILES, LANES), jnp.float32),
-            pltpu.SemaphoreType.DMA,
         ],
         compiler_params=pltpu.CompilerParams(vmem_limit_bytes=24 << 20),
         name="gather_shifted",
-    )(q, TABLE, *pieces)
+    )(q, *pieces)
 
 
 def final_kernel(x_ref, main, tail, one, two):
@@ -411,10 +429,9 @@
     )(main, tail, bands, norms, rest)
 
 
-def later(block, buffer):
+def later(block, distances):
     route = []
-    for part in range(PARTS):
-        distance = int(DISTANCES[PARTS - 1 - part, buffer])
+    for part, distance in enumerate(distances):
         if distance:
             for i in range(SEGMENTS - distance):
                 sender = part * SEGMENTS + i
@@ -426,11 +443,11 @@
     q = (PARTS - 1 - lax.axis_index("chan")).astype(jnp.int32).reshape(1)
     pieces = list(local_plane(intensity, channel_scale.reshape(1, CHANS), q))
     for k in range(REACH - 1, 0, -1):
-        pieces[k] = later(pieces[k], k)
+        pieces[k] = later(pieces[k], DISTANCES[::-1, k].tolist())
     lined = gather_shifted(pieces, q)
     lined = lax.all_to_all(lined, "chan", 0, 0, tiled=True)
     main, tail = final_plane(lined)
-    tail = later(tail, 1)
+    tail = later(tail, [1] * PARTS)
     rest, bands, norms = boxcars_later(main, box_widths)
     return boxcars_first(main, tail, bands, norms, rest)
 

time: 47.8 us -> 46.5 us (0.973)
  local copies, waits for them, and re-layouts: 0.76 us -> 0.01 us
    unnamed x4 -> x2, local copies, waits for them, and re-layouts: 0.76 us -> 0.01 us
where the time goes in v5:
time: 46.5 us; the launch traced here: 46.3 us
  blocking collectives  19.3 us (42%)
  starting transfers between devices  18.3 us (39%)
  Pallas kernels  7.04 us (15%)
  waiting for transfers between devices  1.61 us (3%)
    all_to_all x1, blocking collectives, per_device(): lined = lax.all_to_all(lined, 'chan', 0, 0, tiled=True)  19.3 us
    ppermute x5, starting transfers between devices, later(): return lax.ppermute(block, ('chan', 'tm'), route)  18.3 us
    pallas_call x1, Pallas kernels, local_plane(): pl.pallas_call(local_kernel, in_specs=[pl.BlockSpec(memory_space=pltpu.SM...  2.89 us
    pallas_call x1, Pallas kernels, boxcars_later(): pl.pallas_call(later_kernel, in_specs=[pl.BlockSpec(memory_space=pltpu.SM...  1.91 us
    ppermute x5, waiting for transfers between devices, later(): return lax.ppermute(block, ('chan', 'tm'), route)  1.61 us
    pallas_call x1, Pallas kernels, boxcars_first(): pl.pallas_call(first_kernel, in_specs=[pl.BlockSpec(memory_space=pltpu.VM...  1.03 us
  transfers between devices with their start and end apart: 5, of which 1 were waited for; matrix products, arithmetic and copies ran while one was open for 0% of the time, Pallas kernels for 4%

profile of v5, /device:TPU:1, one launch (start us, length us, event | category | flops | bytes accessed | tf_op | source)
XLA Modules:
  0.0 46.3 jit_solution(13924551210920692492)
XLA Ops:
  0.0 0.0 copy-start
  0.0 2.9 %local_plane.1 = (f32[64,8,128]{2,1,0:T(8,128)S(1)}, f32[48,8,128]{2,1,0:T(8,128)S(1)}, f32[30,8,128]{2,1,0:T(8,128)S(1)}, f32[23,8,128]{2,1,0:T(8,128)S(1)}, f32[10,8,128]{2,1,0:T(8,128)S(1)}) custom-call(s32[1]{0:T(128)} %bitcast.q_ref, f32[1,512]{1,0:T(1,128)} %bitcast.6, bf16[2,512,512]{2,1,0:T(8,128)(2,1)} %x_hbm.1), custom_call_target="tpu_custom_call" | custom-call | tf_op jit(solution)/shard_map/local_plane/pallas_call | solution.py:209
  2.9 4.5 %collective-permute-start = (f32[48,8,128]{2,1,0:T(8,128)S(1)}, f32[48,8,128]{2,1,0:T(8,128)S(1)}, u32[]{:S(2)}, u32[]{:S(2)}) collective-permute-start(f32[48,8,128]{2,1,0:T(8,128)S(1)} %get-tuple-element.16), channel_id=1, source_target_pairs={{0,1},{1,2},{2,3},{3,4},{4,5},{5,6},{6,7},{8,9},{9,10},{10,11},{11... | collective-permute-start | bytes 589832 | tf_op jit(solution)/shard_map/ppermute | solution.py:439
  7.4 3.1 %collective-permute-start.1 = (f32[30,8,128]{2,1,0:T(8,128)S(1)}, f32[30,8,128]{2,1,0:T(8,128)S(1)}, u32[]{:S(2)}, u32[]{:S(2)}) collective-permute-start(f32[30,8,128]{2,1,0:T(8,128)S(1)} %get-tuple-element.17), channel_id=1, source_target_pairs={{0,2},{1,3},{2,4},{3,5},{4,6},{5,7},{8,10},{9,11},{10,12},{11,13},... | collective-permute-start | bytes 368648 | tf_op jit(solution)/shard_map/ppermute | solution.py:439
  10.5 3.4 %collective-permute-start.2 = (f32[23,8,128]{2,1,0:T(8,128)S(1)}, f32[23,8,128]{2,1,0:T(8,128)S(1)}, u32[]{:S(2)}, u32[]{:S(2)}) collective-permute-start(f32[23,8,128]{2,1,0:T(8,128)S(1)} %get-tuple-element.18), channel_id=1, source_target_pairs={{0,3},{1,4},{2,5},{3,6},{4,7},{8,11},{9,12},{10,13},{11,14},{12,15... | collective-permute-start | bytes 282632 | tf_op jit(solution)/shard_map/ppermute | solution.py:439
  14.0 1.3 %collective-permute-start.3 = (f32[10,8,128]{2,1,0:T(8,128)S(1)}, f32[10,8,128]{2,1,0:T(8,128)S(1)}, u32[]{:S(2)}, u32[]{:S(2)}) collective-permute-start(f32[10,8,128]{2,1,0:T(8,128)S(1)} %get-tuple-element.19), channel_id=1, source_target_pairs={{0,4},{1,5},{2,6},{3,7},{8,12},{9,13},{10,14},{11,15},{16,20},{17,... | collective-permute-start | bytes 122888 | tf_op jit(solution)/shard_map/ppermute | solution.py:439
  15.3 1.6 %collective-permute-done.3.r4 = f32[10,8,128]{2,1,0:T(8,128)S(1)} collective-permute-done((f32[10,8,128]{2,1,0:T(8,128)S(1)}, f32[10,8,128]{2,1,0:T(8,128)S(1)}, u32[]{:S(2)}, u32[]{:S(2)}) %collective-permute-start.3) | collective-permute-done | bytes 40992 | tf_op jit(solution)/shard_map/ppermute | solution.py:439
  16.9 0.0 collective-permute-done.2.r3
  16.9 0.0 collective-permute-done.1.r2
  16.9 0.0 collective-permute-done.r1
  16.9 0.5 %gather_shifted.1 = f32[512,128]{1,0:T(8,128)S(1)} custom-call(s32[1]{0:T(128)} %bitcast.q_ref, f32[64,8,128]{2,1,0:T(8,128)S(1)} %get-tuple-element.15.o0, f32[48,8,128]{2,1,0:T(8,128)S(1)} %collective-permute-done.r1, f32[30,8,128]{2,1,0:T(8,128)S(1)} %collective-permute-done.1.r2, f32[23,8,128]{2,1,0:T(8,128)S(1)} %collective-permute-done.2.r3, ...), custom_call_target="tpu_custom_call" | custom-call | tf_op jit(solution)/shard_map/gather_shifted/pallas_call | solution.py:259
  17.4 19.3 %all_to_all.11 = f32[32,16,128]{2,1,0:T(8,128)S(1)} all-to-all(f32[32,16,128]{2,1,0:T(8,128)S(1)} %bitcast.4), channel_id=1, replica_groups=mesh['chan'=32,'tm'=8] {'chan'}, dimensions={0} | all-to-all | bytes 524288 | tf_op jit(solution)/shard_map/all_to_all | solution.py:448
  36.7 0.7 %final_plane.1 = (f32[2,64,512]{2,1,0:T(8,128)S(1)}, f32[2,64,128]{2,1,0:T(8,128)S(1)}) custom-call(f32[512,128]{1,0:T(8,128)S(1)} %bitcast.5), custom_call_target="tpu_custom_call" | custom-call | tf_op jit(solution)/shard_map/final_plane/pallas_call | solution.py:297
  37.4 5.9 %collective-permute-start.4 = (f32[2,64,128]{2,1,0:T(8,128)S(1)}, f32[2,64,128]{2,1,0:T(8,128)S(1)}, u32[]{:S(2)}, u32[]{:S(2)}) collective-permute-start(f32[2,64,128]{2,1,0:T(8,128)S(1)} %get-tuple-element.21), channel_id=1, source_target_pairs={{0,1},{1,2},{2,3},{3,4},{4,5},{5,6},{6,7},{8,9},{9,10},{10,11},{11... | collective-permute-start | bytes 196616 | tf_op jit(solution)/shard_map/ppermute | solution.py:439
  43.3 0.0 copy-done
  43.3 1.9 %boxcars_later.1 = (f32[2,6,64,512]{3,2,1,0:T(8,128)}, bf16[256,768]{1,0:T(8,128)(2,1)S(1)}, f32[1,768]{1,0:T(1,128)S(1)}) custom-call(s32[6]{0:T(128)S(1)} %copy-done, f32[2,64,512]{2,1,0:T(8,128)S(1)} %get-tuple-element.20.main), custom_call_target="tpu_custom_call" | custom-call | flops 301989888 | bytes 2097152 | tf_op jit(solution)/shard_map/boxcars_later/pallas_call | solution.py:387
  45.2 0.0 collective-permute-done.4.tail
  45.2 1.0 %boxcars_first.1 = f32[2,6,64,512]{3,2,1,0:T(8,128)} custom-call(f32[2,64,512]{2,1,0:T(8,128)S(1)} %get-tuple-element.20.main, f32[2,64,128]{2,1,0:T(8,128)S(1)} %collective-permute-done.4.tail, bf16[256,768]{1,0:T(8,128)(2,1)S(1)} %get-tuple-element.22.bands, f32[1,768]{1,0:T(1,128)S(1)} %get-tuple-element.23.norms, ...), custom_call_target="tpu_custom_call", output_to_operand_aliasing={{}: (4, {})} | custom-call | tf_op jit(solution)/shard_map/boxcars_first/pallas_call | solution.py:416
Async XLA Ops:
  0.0 43.3 %copy-start = (s32[6]{0:T(128)S(1)}, s32[6]{0:T(128)}, u32[]{:S(2)}) copy-start(s32[6]{0:T(128)} %widths.1) | copy-start | bytes 76
  2.9 14.0 %collective-permute-start = (f32[48,8,128]{2,1,0:T(8,128)S(1)}, f32[48,8,128]{2,1,0:T(8,128)S(1)}, u32[]{:S(2)}, u32[]{:S(2)}) collective-permute-start(f32[48,8,128]{2,1,0:T(8,128)S(1)} %get-tuple-element.16), channel_id=1, source_target_pairs={{0,1},{1,2},{2,3},{3,4},{4,5},{5,6},{6,7},{8,9},{9,10},{10,11},{11... | collective-permute-start | bytes 589832 | tf_op jit(solution)/shard_map/ppermute | solution.py:439
  7.4 9.5 %collective-permute-start.1 = (f32[30,8,128]{2,1,0:T(8,128)S(1)}, f32[30,8,128]{2,1,0:T(8,128)S(1)}, u32[]{:S(2)}, u32[]{:S(2)}) collective-permute-start(f32[30,8,128]{2,1,0:T(8,128)S(1)} %get-tuple-element.17), channel_id=1, source_target_pairs={{0,2},{1,3},{2,4},{3,5},{4,6},{5,7},{8,10},{9,11},{10,12},{11,13},... | collective-permute-start | bytes 368648 | tf_op jit(solution)/shard_map/ppermute | solution.py:439
  10.5 6.4 %collective-permute-start.2 = (f32[23,8,128]{2,1,0:T(8,128)S(1)}, f32[23,8,128]{2,1,0:T(8,128)S(1)}, u32[]{:S(2)}, u32[]{:S(2)}) collective-permute-start(f32[23,8,128]{2,1,0:T(8,128)S(1)} %get-tuple-element.18), channel_id=1, source_target_pairs={{0,3},{1,4},{2,5},{3,6},{4,7},{8,11},{9,12},{10,13},{11,14},{12,15... | collective-permute-start | bytes 282632 | tf_op jit(solution)/shard_map/ppermute | solution.py:439
  14.0 2.9 %collective-permute-start.3 = (f32[10,8,128]{2,1,0:T(8,128)S(1)}, f32[10,8,128]{2,1,0:T(8,128)S(1)}, u32[]{:S(2)}, u32[]{:S(2)}) collective-permute-start(f32[10,8,128]{2,1,0:T(8,128)S(1)} %get-tuple-element.19), channel_id=1, source_target_pairs={{0,4},{1,5},{2,6},{3,7},{8,12},{9,13},{10,14},{11,15},{16,20},{17,... | collective-permute-start | bytes 122888 | tf_op jit(solution)/shard_map/ppermute | solution.py:439
  37.4 7.9 %collective-permute-start.4 = (f32[2,64,128]{2,1,0:T(8,128)S(1)}, f32[2,64,128]{2,1,0:T(8,128)S(1)}, u32[]{:S(2)}, u32[]{:S(2)}) collective-permute-start(f32[2,64,128]{2,1,0:T(8,128)S(1)} %get-tuple-element.21), channel_id=1, source_target_pairs={{0,1},{1,2},{2,3},{3,4},{4,5},{5,6},{6,7},{8,9},{9,10},{10,11},{11... | collective-permute-start | bytes 196616 | tf_op jit(solution)/shard_map/ppermute | solution.py:439

commit v6 on v5

--- a/solution.py
+++ b/solution.py
@@ -44,17 +44,19 @@
             first, number = tile_span(q, a)
             for h in range(first, first + number):
                 counts[q, h // PER] += 1
-    sizes = [64, 48, 30, 23, 10]
+    sizes = [64, 48, 30, 10, 23]
     buffers = np.zeros((PARTS, REACH), np.int32)
     distances = np.zeros((PARTS, REACH), np.int32)
     for q in range(PARTS):
         taken = {0}
         for k in range(REACH - 1, 0, -1):
             if counts[q, k]:
-                fits = [i for i in range(1, REACH) if i not in taken and sizes[i] >= counts[q, k]]
-                buffers[q, k] = fits[-1]
-                distances[q, fits[-1]] = k
-                taken.add(fits[-1])
+                fits = [i for i in (3, 4, 2, 1) if i not in taken and sizes[i] >= counts[q, k]]
+                if q < 22 and 2 in fits:
+                    fits = [i for i in fits if i != 4]
+                buffers[q, k] = fits[0]
+                distances[q, fits[0]] = k
+                taken.add(fits[0])
     starts = [sum(sizes[:k]) for k in range(REACH)]
     return sizes, starts, sum(sizes), buffers, distances
 
@@ -121,26 +123,26 @@
     return jnp.concatenate(chunks, axis=1)
 
 
-def merge_rows(groups, one, two):
-    tiles = WIDE // LANES
-    while len(groups) > 1:
-        groups = merge_groups(groups)
+def merge_rows(groups, one, two, tiles):
+    while len(groups[0]) > 1:
+        groups = [merge_groups(beam) for beam in groups]
     for e in range(8):
-        put(one, e, 8, groups[0][e])
+        for b, beam in enumerate(groups):
+            put(one.at[b], e, 8, beam[0][e])
     source, target = one, two
     trials = 8
     while trials < ROWS:
         for base in range(0, ROWS, 2 * trials):
             for a in range(0, trials, 8):
-                upper = take(source, base + a, 8, 0, tiles)
-                lower = take(source, base + trials + a, 8, 0, tiles)
-                early = pltpu.roll(upper, a, 1, stride=1, stride_axis=0)
-                late = pltpu.roll(upper, a + 1, 1, stride=1, stride_axis=0)
-                put(target, base + 2 * a, 2, lower + early)
-                put(target, base + 2 * a + 1, 2, lower + late)
+                for b in range(BEAMS):
+                    upper = take(source.at[b], base + a, 8, 0, tiles)
+                    lower = take(source.at[b], base + trials + a, 8, 0, tiles)
+                    early = pltpu.roll(upper, a, 1, stride=1, stride_axis=0)
+                    late = pltpu.roll(upper, a + 1, 1, stride=1, stride_axis=0)
+                    put(target.at[b], base + 2 * a, 2, lower + early)
+                    put(target.at[b], base + 2 * a + 1, 2, lower + late)
         source, target = target, source
         trials *= 2
-    return source
 
 
 def local_kernel(
@@ -181,16 +183,19 @@
     weights = jnp.where(member, scale[...], 0.0)
     weights = jnp.concatenate(split(weights), axis=0)
     blank = jnp.zeros((8, LANES), jnp.float32)
+    for fetch in fetches:
+        fetch.wait()
+    groups = []
     for b in range(BEAMS):
-        fetches[2 * b].wait()
-        fetches[2 * b + 1].wait()
         base = jnp.dot(weights, x[b], preferred_element_type=jnp.float32)
         base = base[:ROWS] + base[ROWS:]
-        groups = [
-            [jnp.concatenate([base[8 * g : 8 * g + 8], blank], axis=1)]
-            for g in range(8)
-        ]
-        merge_rows(groups, one.at[b], two.at[b])
+        groups.append(
+            [
+                [jnp.concatenate([base[8 * g : 8 * g + 8], blank], axis=1)]
+                for g in range(8)
+            ]
+        )
+    merge_rows(groups, one, two, WIDE // LANES)
     first_slots(q, free)
     odd = lax.broadcasted_iota(jnp.int32, (8, UNITS * LANES), 0) & 2 != 0
     for a in range(TILES):
@@ -270,9 +275,9 @@
     )(q, *pieces)
 
 
-def final_kernel(x_ref, main, tail, one, two):
+def final_groups(x_ref, first, last):
     blank = jnp.zeros((8, LANES), jnp.float32)
-    lane = lax.broadcasted_iota(jnp.int32, (ROWS, LANES), 1)
+    beams = []
     for b in range(BEAMS):
         groups = []
         for g in range(4):
@@ -280,32 +285,31 @@
             for e in range(2):
                 chunks = [
                     x_ref[pl.ds(g * 16 + b * 8 + c * 2 + e, 8, stride=64), :]
-                    for c in range(SPAN // LANES)
+                    for c in range(first, last)
                 ]
                 trials.append(jnp.concatenate(chunks + [blank], axis=1))
             groups.append(trials)
-        plane = merge_rows(groups, one.at[b], two.at[b])
-        main[b] = take(plane, 0, ROWS, 0, SPAN // LANES)
-        tail[b] = jnp.where(
-            lane < LANES // 2,
-            plane[SPAN // LANES],
-            plane[SPAN // LANES - 1],
-        )
-
-
-def final_plane(x):
+        beams.append(groups)
+    return beams
+
+
+def tail_kernel(x_ref, tail, one, two):
+    merge_rows(final_groups(x_ref, PER - 1, PER), one, two, 2)
+    lane = lax.broadcasted_iota(jnp.int32, (ROWS, LANES), 1)
+    for b in range(BEAMS):
+        tail[b] = jnp.where(lane < LANES // 2, two[b, 1], two[b, 0])
+
+
+def final_tail(x):
     return pl.pallas_call(
-        final_kernel,
-        out_shape=[
-            jax.ShapeDtypeStruct((BEAMS, ROWS, SPAN), jnp.float32),
-            jax.ShapeDtypeStruct((BEAMS, ROWS, LANES), jnp.float32),
-        ],
+        tail_kernel,
+        out_shape=jax.ShapeDtypeStruct((BEAMS, ROWS, LANES), jnp.float32),
         scratch_shapes=[
-            pltpu.VMEM((BEAMS, WIDE // LANES, ROWS, LANES), jnp.float32),
-            pltpu.VMEM((BEAMS, WIDE // LANES, ROWS, LANES), jnp.float32),
+            pltpu.VMEM((BEAMS, 2, ROWS, LANES), jnp.float32),
+            pltpu.VMEM((BEAMS, 2, ROWS, LANES), jnp.float32),
         ],
         compiler_params=pltpu.CompilerParams(vmem_limit_bytes=24 << 20),
-        name="final_plane",
+        name="final_tail",
     )(x)
 
 
@@ -340,17 +344,22 @@
             ]
 
 
-def later_kernel(widths, main, out, bands_out, norms_out, held, sems):
+def later_kernel(
+    widths, x_ref, out, start, bands_out, norms_out, one, two, held, sems
+):
+    merge_rows(final_groups(x_ref, 0, PER), one, two, WIDE // LANES)
     bands = boxcar_bands(widths)
     norms = boxcar_norms(widths)
     bands_out[...] = bands
     norms_out[...] = norms
     parts = []
-    for c in range(SPAN // LANES):
-        tile = main[:, :, pl.ds(c * LANES, LANES)].reshape(BEAMS * ROWS, LANES)
+    for c in range(PER):
+        tile = jnp.concatenate([two[b, c] for b in range(BEAMS)], axis=0)
+        if c == 0:
+            start[...] = tile
         parts.append(jnp.concatenate(split(tile), axis=0))
     copies = []
-    for c in range(1, SPAN // LANES):
+    for c in range(1, PER):
         boxcar_tile(parts[c - 1], parts[c], bands, norms, held, c - 1)
         copies.append(
             pltpu.make_async_copy(
@@ -364,13 +373,12 @@
         copy.wait()
 
 
-def first_kernel(main, tail, bands, norms, rest, out, held, sem):
+def first_kernel(start, tail, bands, norms, rest, out, held, sem):
     del rest
     lane = lax.broadcasted_iota(jnp.int32, (BEAMS * ROWS, LANES), 1)
     edge = tail[...].reshape(BEAMS * ROWS, LANES)
     before = jnp.where(lane >= LANES // 2, edge, 0.0)
-    here = main[:, :, pl.ds(0, LANES)].reshape(BEAMS * ROWS, LANES)
-    here = here + jnp.where(lane < LANES // 2, edge, 0.0)
+    here = start[...] + jnp.where(lane < LANES // 2, edge, 0.0)
     before = jnp.concatenate(split(before), axis=0)
     here = jnp.concatenate(split(here), axis=0)
     boxcar_tile(before, here, bands[...], norms[...], held, 0)
@@ -382,25 +390,22 @@
 OUT = jax.ShapeDtypeStruct((BEAMS, NBOX, ROWS, SPAN), jnp.float32)
 
 
-def boxcars_later(main, widths):
+def boxcars_later(x, widths):
     lanes = SPAN - LANES
+    vmem = pl.BlockSpec(memory_space=pltpu.VMEM)
     return pl.pallas_call(
         later_kernel,
-        in_specs=[
-            pl.BlockSpec(memory_space=pltpu.SMEM),
-            pl.BlockSpec(memory_space=pltpu.VMEM),
-        ],
-        out_specs=[
-            pl.BlockSpec(memory_space=pltpu.HBM),
-            pl.BlockSpec(memory_space=pltpu.VMEM),
-            pl.BlockSpec(memory_space=pltpu.VMEM),
-        ],
+        in_specs=[pl.BlockSpec(memory_space=pltpu.SMEM), vmem],
+        out_specs=[pl.BlockSpec(memory_space=pltpu.HBM), vmem, vmem, vmem],
         out_shape=[
             OUT,
+            jax.ShapeDtypeStruct((BEAMS * ROWS, LANES), jnp.float32),
             jax.ShapeDtypeStruct((2 * LANES, NBOX * LANES), jnp.bfloat16),
             jax.ShapeDtypeStruct((1, NBOX * LANES), jnp.float32),
         ],
         scratch_shapes=[
+            pltpu.VMEM((BEAMS, WIDE // LANES, ROWS, LANES), jnp.float32),
+            pltpu.VMEM((BEAMS, WIDE // LANES, ROWS, LANES), jnp.float32),
             pltpu.VMEM((BEAMS, NBOX, ROWS, lanes), jnp.float32),
             pltpu.SemaphoreType.DMA((lanes // LANES,)),
         ],
@@ -409,10 +414,10 @@
             flops=2 * 256 * 256 * 768 * 3, bytes_accessed=2 << 20, transcendentals=0
         ),
         name="boxcars_later",
-    )(widths, main)
-
-
-def boxcars_first(main, tail, bands, norms, rest):
+    )(widths, x)
+
+
+def boxcars_first(start, tail, bands, norms, rest):
     return pl.pallas_call(
         first_kernel,
         in_specs=[pl.BlockSpec(memory_space=pltpu.VMEM)] * 4
@@ -426,7 +431,7 @@
         ],
         compiler_params=pltpu.CompilerParams(vmem_limit_bytes=24 << 20),
         name="boxcars_first",
-    )(main, tail, bands, norms, rest)
+    )(start, tail, bands, norms, rest)
 
 
 def later(block, distances):
@@ -446,10 +451,9 @@
         pieces[k] = later(pieces[k], DISTANCES[::-1, k].tolist())
     lined = gather_shifted(pieces, q)
     lined = lax.all_to_all(lined, "chan", 0, 0, tiled=True)
-    main, tail = final_plane(lined)
-    tail = later(tail, [1] * PARTS)
-    rest, bands, norms = boxcars_later(main, box_widths)
-    return boxcars_first(main, tail, bands, norms, rest)
+    tail = later(final_tail(lined), [1] * PARTS)
+    rest, start, bands, norms = boxcars_later(lined, box_widths)
+    return boxcars_first(start, tail, bands, norms, rest)
 
 
 def solution(mesh):

time: 46.5 us -> 46.3 us (level)
    pallas_call x1, Pallas kernels: 2.89 us -> 2.4 us  [local_plane(): pl.pallas_call(local_kernel, in_specs=[pl.BlockSpec(memory_space=pltpu.SM...]
    pallas_call x1, Pallas kernels: 1.91 us -> 2.39 us  [boxcars_later(): pl.pallas_call(later_kernel, in_specs=[pl.BlockSpec(memory_space=pltpu.SM...]
  transfers between devices with their start and end apart: 5 -> 5, of which waited for: 1 -> 1; matrix products, arithmetic and copies ran while one was open for 0% -> 0% of each run, Pallas kernels for 4% -> 5%
where the time goes in v6:
time: 46.3 us; the launch traced here: 46 us
  blocking collectives  19.3 us (42%)
  starting transfers between devices  18.3 us (40%)
  Pallas kernels  6.78 us (15%)
  waiting for transfers between devices  1.61 us (3%)
    all_to_all x1, blocking collectives, per_device(): lined = lax.all_to_all(lined, 'chan', 0, 0, tiled=True)  19.3 us
    ppermute x5, starting transfers between devices, later(): return lax.ppermute(block, ('chan', 'tm'), route)  18.3 us
    pallas_call x1, Pallas kernels, local_plane(): pl.pallas_call(local_kernel, in_specs=[pl.BlockSpec(memory_space=pltpu.SM...  2.4 us
    pallas_call x1, Pallas kernels, boxcars_later(): pl.pallas_call(later_kernel, in_specs=[pl.BlockSpec(memory_space=pltpu.SM...  2.39 us
    ppermute x5, waiting for transfers between devices, later(): return lax.ppermute(block, ('chan', 'tm'), route)  1.61 us
    pallas_call x1, Pallas kernels, boxcars_first(): pl.pallas_call(first_kernel, in_specs=[pl.BlockSpec(memory_space=pltpu.VM...  1.03 us
  transfers between devices with their start and end apart: 5, of which 1 were waited for; matrix products, arithmetic and copies ran while one was open for 0% of the time, Pallas kernels for 5%

profile of v6, /device:TPU:1, one launch (start us, length us, event | category | flops | bytes accessed | tf_op | source)
XLA Modules:
  0.0 46.0 jit_solution(9622819585056675391)
XLA Ops:
  0.0 0.0 copy-start
  0.0 2.4 %local_plane.1 = (f32[64,8,128]{2,1,0:T(8,128)S(1)}, f32[48,8,128]{2,1,0:T(8,128)S(1)}, f32[30,8,128]{2,1,0:T(8,128)S(1)}, f32[10,8,128]{2,1,0:T(8,128)S(1)}, f32[23,8,128]{2,1,0:T(8,128)S(1)}) custom-call(s32[1]{0:T(128)} %bitcast.q_ref, f32[1,512]{1,0:T(1,128)} %bitcast.7, bf16[2,512,512]{2,1,0:T(8,128)(2,1)} %x_hbm.1), custom_call_target="tpu_custom_call" | custom-call | tf_op jit(solution)/shard_map/local_plane/pallas_call | solution.py:214
  2.4 4.5 %collective-permute-start = (f32[48,8,128]{2,1,0:T(8,128)S(1)}, f32[48,8,128]{2,1,0:T(8,128)S(1)}, u32[]{:S(2)}, u32[]{:S(2)}) collective-permute-start(f32[48,8,128]{2,1,0:T(8,128)S(1)} %get-tuple-element.15), channel_id=1, source_target_pairs={{0,1},{1,2},{2,3},{3,4},{4,5},{5,6},{6,7},{8,9},{9,10},{10,11},{11... | collective-permute-start | bytes 589832 | tf_op jit(solution)/shard_map/ppermute | solution.py:444
  6.9 3.1 %collective-permute-start.1 = (f32[30,8,128]{2,1,0:T(8,128)S(1)}, f32[30,8,128]{2,1,0:T(8,128)S(1)}, u32[]{:S(2)}, u32[]{:S(2)}) collective-permute-start(f32[30,8,128]{2,1,0:T(8,128)S(1)} %get-tuple-element.16), channel_id=1, source_target_pairs={{0,2},{1,3},{2,4},{3,5},{4,6},{5,7},{8,10},{9,11},{10,12},{11,13},... | collective-permute-start | bytes 368648 | tf_op jit(solution)/shard_map/ppermute | solution.py:444
  10.1 3.4 %collective-permute-start.3 = (f32[23,8,128]{2,1,0:T(8,128)S(1)}, f32[23,8,128]{2,1,0:T(8,128)S(1)}, u32[]{:S(2)}, u32[]{:S(2)}) collective-permute-start(f32[23,8,128]{2,1,0:T(8,128)S(1)} %get-tuple-element.18), channel_id=1, source_target_pairs={{0,3},{1,4},{2,5},{3,6},{4,7},{8,11},{9,12},{10,13},{11,14},{12,15... | collective-permute-start | bytes 282632 | tf_op jit(solution)/shard_map/ppermute | solution.py:444
  13.5 1.3 %collective-permute-start.2 = (f32[10,8,128]{2,1,0:T(8,128)S(1)}, f32[10,8,128]{2,1,0:T(8,128)S(1)}, u32[]{:S(2)}, u32[]{:S(2)}) collective-permute-start(f32[10,8,128]{2,1,0:T(8,128)S(1)} %get-tuple-element.17), channel_id=1, source_target_pairs={{0,4},{1,5},{2,6},{3,7},{8,12},{9,13},{10,14},{11,15},{16,20},{17,... | collective-permute-start | bytes 122888 | tf_op jit(solution)/shard_map/ppermute | solution.py:444
  14.8 1.6 %collective-permute-done.2.r3 = f32[10,8,128]{2,1,0:T(8,128)S(1)} collective-permute-done((f32[10,8,128]{2,1,0:T(8,128)S(1)}, f32[10,8,128]{2,1,0:T(8,128)S(1)}, u32[]{:S(2)}, u32[]{:S(2)}) %collective-permute-start.2) | collective-permute-done | bytes 40992 | tf_op jit(solution)/shard_map/ppermute | solution.py:444
  16.4 0.0 collective-permute-done.3.r4
  16.4 0.0 collective-permute-done.1.r2
  16.4 0.0 collective-permute-done.r1
  16.4 0.5 %gather_shifted.1 = f32[512,128]{1,0:T(8,128)S(1)} custom-call(s32[1]{0:T(128)} %bitcast.q_ref, f32[64,8,128]{2,1,0:T(8,128)S(1)} %get-tuple-element.14.o0, f32[48,8,128]{2,1,0:T(8,128)S(1)} %collective-permute-done.r1, f32[30,8,128]{2,1,0:T(8,128)S(1)} %collective-permute-done.1.r2, f32[10,8,128]{2,1,0:T(8,128)S(1)} %collective-permute-done.2.r3, ...), custom_call_target="tpu_custom_call" | custom-call | tf_op jit(solution)/shard_map/gather_shifted/pallas_call | solution.py:264
  16.9 19.3 %all_to_all.11 = f32[32,16,128]{2,1,0:T(8,128)S(1)} all-to-all(f32[32,16,128]{2,1,0:T(8,128)S(1)} %bitcast.4), channel_id=1, replica_groups=mesh['chan'=32,'tm'=8] {'chan'}, dimensions={0} | all-to-all | bytes 524288 | tf_op jit(solution)/shard_map/all_to_all | solution.py:453
  36.2 0.5 final_tail.1
  36.7 5.9 %collective-permute-start.4 = (f32[2,64,128]{2,1,0:T(8,128)S(1)}, f32[2,64,128]{2,1,0:T(8,128)S(1)}, u32[]{:S(2)}, u32[]{:S(2)}) collective-permute-start(f32[2,64,128]{2,1,0:T(8,128)S(1)} %final_tail.1), channel_id=1, source_target_pairs={{0,1},{1,2},{2,3},{3,4},{4,5},{5,6},{6,7},{8,9},{9,10},{10,11},{11... | collective-permute-start | bytes 196616 | tf_op jit(solution)/shard_map/ppermute | solution.py:444
  42.6 0.0 copy-done
  42.6 2.4 %boxcars_later.1 = (f32[2,6,64,512]{3,2,1,0:T(8,128)}, f32[128,128]{1,0:T(8,128)S(1)}, bf16[256,768]{1,0:T(8,128)(2,1)S(1)}, f32[1,768]{1,0:T(1,128)S(1)}) custom-call(s32[6]{0:T(128)S(1)} %copy-done, f32[512,128]{1,0:T(8,128)S(1)} %bitcast.6), custom_call_target="tpu_custom_call" | custom-call | flops 301989888 | bytes 2097152 | tf_op jit(solution)/shard_map/boxcars_later/pallas_call | solution.py:396
  45.0 0.0 collective-permute-done.4.tail
  45.0 1.0 %boxcars_first.1 = f32[2,6,64,512]{3,2,1,0:T(8,128)} custom-call(f32[128,128]{1,0:T(8,128)S(1)} %get-tuple-element.19.start, f32[2,64,128]{2,1,0:T(8,128)S(1)} %collective-permute-done.4.tail, bf16[256,768]{1,0:T(8,128)(2,1)S(1)} %get-tuple-element.20.bands, f32[1,768]{1,0:T(1,128)S(1)} %get-tuple-element.21.norms, ...), custom_call_target="tpu_custom_call", output_to_operand_aliasing={{}: (4, {})} | custom-call | tf_op jit(solution)/shard_map/boxcars_first/pallas_call | solution.py:421
Async XLA Ops:
  0.0 42.6 %copy-start = (s32[6]{0:T(128)S(1)}, s32[6]{0:T(128)}, u32[]{:S(2)}) copy-start(s32[6]{0:T(128)} %widths.1) | copy-start | bytes 76
  2.4 14.0 %collective-permute-start = (f32[48,8,128]{2,1,0:T(8,128)S(1)}, f32[48,8,128]{2,1,0:T(8,128)S(1)}, u32[]{:S(2)}, u32[]{:S(2)}) collective-permute-start(f32[48,8,128]{2,1,0:T(8,128)S(1)} %get-tuple-element.15), channel_id=1, source_target_pairs={{0,1},{1,2},{2,3},{3,4},{4,5},{5,6},{6,7},{8,9},{9,10},{10,11},{11... | collective-permute-start | bytes 589832 | tf_op jit(solution)/shard_map/ppermute | solution.py:444
  6.9 9.5 %collective-permute-start.1 = (f32[30,8,128]{2,1,0:T(8,128)S(1)}, f32[30,8,128]{2,1,0:T(8,128)S(1)}, u32[]{:S(2)}, u32[]{:S(2)}) collective-permute-start(f32[30,8,128]{2,1,0:T(8,128)S(1)} %get-tuple-element.16), channel_id=1, source_target_pairs={{0,2},{1,3},{2,4},{3,5},{4,6},{5,7},{8,10},{9,11},{10,12},{11,13},... | collective-permute-start | bytes 368648 | tf_op jit(solution)/shard_map/ppermute | solution.py:444
  10.1 6.3 %collective-permute-start.3 = (f32[23,8,128]{2,1,0:T(8,128)S(1)}, f32[23,8,128]{2,1,0:T(8,128)S(1)}, u32[]{:S(2)}, u32[]{:S(2)}) collective-permute-start(f32[23,8,128]{2,1,0:T(8,128)S(1)} %get-tuple-element.18), channel_id=1, source_target_pairs={{0,3},{1,4},{2,5},{3,6},{4,7},{8,11},{9,12},{10,13},{11,14},{12,15... | collective-permute-start | bytes 282632 | tf_op jit(solution)/shard_map/ppermute | solution.py:444
  13.5 2.9 %collective-permute-start.2 = (f32[10,8,128]{2,1,0:T(8,128)S(1)}, f32[10,8,128]{2,1,0:T(8,128)S(1)}, u32[]{:S(2)}, u32[]{:S(2)}) collective-permute-start(f32[10,8,128]{2,1,0:T(8,128)S(1)} %get-tuple-element.17), channel_id=1, source_target_pairs={{0,4},{1,5},{2,6},{3,7},{8,12},{9,13},{10,14},{11,15},{16,20},{17,... | collective-permute-start | bytes 122888 | tf_op jit(solution)/shard_map/ppermute | solution.py:444
  36.7 8.3 %collective-permute-start.4 = (f32[2,64,128]{2,1,0:T(8,128)S(1)}, f32[2,64,128]{2,1,0:T(8,128)S(1)}, u32[]{:S(2)}, u32[]{:S(2)}) collective-permute-start(f32[2,64,128]{2,1,0:T(8,128)S(1)} %final_tail.1), channel_id=1, source_target_pairs={{0,1},{1,2},{2,3},{3,4},{4,5},{5,6},{6,7},{8,9},{9,10},{10,11},{11... | collective-permute-start | bytes 196616 | tf_op jit(solution)/shard_map/ppermute | solution.py:444

commit v7 on v6

--- a/solution.py
+++ b/solution.py
@@ -15,10 +15,11 @@
 WIDE = SPAN + 128
 NBOX = 6
 LANES = 128
-REACH = 5
+REACH = 6
 TILES = 16
 UNITS = 6
 PER = SPAN // LANES
+BLOCK = 24
 
 
 def tails(a):
@@ -29,31 +30,39 @@
 def tile_span(q, a):
     delay = 4 * q * a
     first, second = tails(a)
-    end = (delay & (LANES - 1)) + SPAN
-    if isinstance(q, int):
-        end += max(first, 2 * q + second)
-    else:
-        end += jnp.maximum(first, 2 * q + second)
-    return delay >> 7, (end + LANES - 1) >> 7
+    within = delay & (LANES - 1)
+    end = within + SPAN + (max if isinstance(q, int) else jnp.maximum)(first, 2 * q + second)
+    tile = delay >> 7
+    far = (tile & (PER - 1)) * LANES + end > 2 * SPAN - (2 * q + 63)
+    return tile, (end + LANES - 1) >> 7, far
+
+
+def group_shares(q, a, least=min):
+    tile, number, far = tile_span(q, a)
+    at = tile & (PER - 1)
+    here = PER - at
+    then = least(number - here, PER)
+    over = number - here - then
+    return tile >> 2, at, number, far, (here, 1 + then, over + far)
 
 
 def packing():
     counts = np.zeros((PARTS, REACH), np.int32)
     for q in range(PARTS):
         for a in range(TILES):
-            first, number = tile_span(q, a)
-            for h in range(first, first + number):
-                counts[q, h // PER] += 1
-    sizes = [64, 48, 30, 10, 23]
+            k, _, _, _, shares = group_shares(q, a)
+            for i, share in enumerate(shares):
+                if share:
+                    counts[q, k + i] += share
+    sizes = [64, 60, 38, 29, 15, 1]
     buffers = np.zeros((PARTS, REACH), np.int32)
     distances = np.zeros((PARTS, REACH), np.int32)
     for q in range(PARTS):
         taken = {0}
         for k in range(REACH - 1, 0, -1):
             if counts[q, k]:
-                fits = [i for i in (3, 4, 2, 1) if i not in taken and sizes[i] >= counts[q, k]]
-                if q < 22 and 2 in fits:
-                    fits = [i for i in fits if i != 4]
+                allowed = (k,) if q >= 22 else (4, 2, 1)
+                fits = [i for i in allowed if i not in taken and sizes[i] >= counts[q, k]]
                 buffers[q, k] = fits[0]
                 distances[q, fits[0]] = k
                 taken.add(fits[0])
@@ -71,26 +80,23 @@
             if BUFFERS[band, k] != BUFFERS[band - 1, k]:
                 slot = jnp.where(q >= band, STARTS[BUFFERS[band, k]], slot)
         free[k] = slot
-    free[REACH] = SPARE
 
 
 def unit_slots(q, a, free):
-    first, number = tile_span(q, a)
-    at, k = first & (PER - 1), first >> 2
-    here = jnp.minimum(PER - at, number)
-    rest = number - here
-    then = jnp.minimum(rest, PER)
+    k, at, number, far, shares = group_shares(q, a, jnp.minimum)
+    here = shares[0]
     p0, p1, p2 = free[k], free[k + 1], free[k + 2]
     free[k] = p0 + here
-    free[k + 1] = p1 + then
-    free[k + 2] = p2 + rest - then
+    free[k + 1] = p1 + shares[1]
+    free[k + 2] = p2 + shares[2]
     slots = [p0]
     for i in range(1, PER):
-        slots.append(jnp.where(i < here, p0 + i, p1 + i - here))
-    slots.append(p1 + PER - here)
-    last = jnp.where(here > 1, p1 + PER + 1 - here, p2)
+        slots.append(jnp.where(i < here, p0 + i, p1 + 1 + i - here))
+    slots.append(p1 + 1 + PER - here)
+    last = jnp.where(here > 1, p1 + PER + 2 - here, p2 + 1)
     slots.append(jnp.where(number > PER + 1, last, SPARE))
-    return slots, at
+    again = (p1, p0 + here - 1), (jnp.where(far, p2, SPARE), jnp.where(far, p1 + PER, SPARE))
+    return slots, at, again
 
 
 def split(x):
@@ -154,6 +160,7 @@
     o2,
     o3,
     o4,
+    o5,
     free,
     scale,
     x,
@@ -203,10 +210,12 @@
         rows = jnp.concatenate([jnp.concatenate(rows, axis=0), blank], axis=1)
         rows = jnp.where(odd, pltpu.roll(rows, 2 * q, 1), rows)
         rows = pltpu.roll(rows, (4 * q * a) & (LANES - 1), 1)
-        slots, _ = unit_slots(q, a, free)
+        slots, _, again = unit_slots(q, a, free)
         for i, slot in enumerate(slots):
             packed[slot] = rows[:, i * LANES : (i + 1) * LANES]
-    for k, out in enumerate((o0, o1, o2, o3, o4)):
+        for slot, origin in again:
+            packed[slot] = packed[origin]
+    for k, out in enumerate((o0, o1, o2, o3, o4, o5)):
         out[...] = packed[pl.ds(STARTS[k], SIZES[k])]
 
 
@@ -220,7 +229,7 @@
         ],
         out_shape=[jax.ShapeDtypeStruct((n, 8, LANES), jnp.float32) for n in SIZES],
         scratch_shapes=[
-            pltpu.SMEM((REACH + 3,), jnp.int32),
+            pltpu.SMEM((REACH + 2,), jnp.int32),
             pltpu.VMEM((1, CHANS), jnp.float32),
             pltpu.VMEM((BEAMS, CHANS, SPAN), jnp.bfloat16),
             pltpu.VMEM((BEAMS, WIDE // LANES, ROWS, LANES), jnp.float32),
@@ -237,24 +246,25 @@
     )
 
 
-def gather_kernel(q_ref, o0, r1, r2, r3, r4, out, free, packed, held):
+def gather_kernel(q_ref, o0, r1, r2, r3, r4, r5, out, free, packed, held):
     q = q_ref[0]
     first_slots(q, free)
-    for k, piece in enumerate((o0, r1, r2, r3, r4)):
+    for k, piece in enumerate((o0, r1, r2, r3, r4, r5)):
         packed[pl.ds(STARTS[k], SIZES[k])] = piece[...]
     packed[SPARE] = jnp.zeros((8, LANES), jnp.float32)
     for a in range(TILES):
-        slots, at = unit_slots(q, a, free)
+        slots, at, again = unit_slots(q, a, free)
         rows = pl.ds(8 * a, 8)
-        tiles = [(at + i) & (PER - 1) for i in range(PER)]
+        tiles = [1 + ((at + i) & (PER - 1)) for i in range(PER)]
+        held[0, rows, :] = packed[again[0][0]] + packed[again[1][0]]
         held[tiles[0], rows, :] = packed[slots[0]] + packed[slots[PER]]
         held[tiles[1], rows, :] = packed[slots[1]] + packed[slots[PER + 1]]
         held[tiles[2], rows, :] = packed[slots[2]]
         held[tiles[3], rows, :] = packed[slots[3]]
-    for c in range(PER):
+    for c in range(WIDE // LANES):
         for r in range(8):
             b, m, i = r >> 2, r >> 1 & 1, r & 1
-            out[pl.ds(m * 16 + b * 8 + c * 2 + i, TILES, stride=32), :] = held[
+            out[pl.ds(m * BLOCK + c * 4 + b * 2 + i, TILES, stride=2 * BLOCK), :] = held[
                 c, pl.ds(r, TILES, stride=8), :
             ]
 
@@ -264,19 +274,18 @@
     return pl.pallas_call(
         gather_kernel,
         in_specs=[pl.BlockSpec(memory_space=pltpu.SMEM)] + [vmem] * REACH,
-        out_shape=jax.ShapeDtypeStruct((PARTS * 16, LANES), jnp.float32),
+        out_shape=jax.ShapeDtypeStruct((PARTS * BLOCK, LANES), jnp.float32),
         scratch_shapes=[
-            pltpu.SMEM((REACH + 3,), jnp.int32),
+            pltpu.SMEM((REACH + 2,), jnp.int32),
             pltpu.VMEM((SPARE + 1, 8, LANES), jnp.float32),
-            pltpu.VMEM((PER, 8 * TILES, LANES), jnp.float32),
+            pltpu.VMEM((WIDE // LANES, 8 * TILES, LANES), jnp.float32),
         ],
         compiler_params=pltpu.CompilerParams(vmem_limit_bytes=24 << 20),
         name="gather_shifted",
     )(q, *pieces)
 
 
-def final_groups(x_ref, first, last):
-    blank = jnp.zeros((8, LANES), jnp.float32)
+def final_groups(x_ref):
     beams = []
     for b in range(BEAMS):
         groups = []
@@ -284,33 +293,13 @@
             trials = []
             for e in range(2):
                 chunks = [
-                    x_ref[pl.ds(g * 16 + b * 8 + c * 2 + e, 8, stride=64), :]
-                    for c in range(first, last)
+                    x_ref[pl.ds(g * BLOCK + c * 4 + b * 2 + e, 8, stride=4 * BLOCK), :]
+                    for c in range(WIDE // LANES)
                 ]
-                trials.append(jnp.concatenate(chunks + [blank], axis=1))
+                trials.append(jnp.concatenate(chunks, axis=1))
             groups.append(trials)
         beams.append(groups)
     return beams
-
-
-def tail_kernel(x_ref, tail, one, two):
-    merge_rows(final_groups(x_ref, PER - 1, PER), one, two, 2)
-    lane = lax.broadcasted_iota(jnp.int32, (ROWS, LANES), 1)
-    for b in range(BEAMS):
-        tail[b] = jnp.where(lane < LANES // 2, two[b, 1], two[b, 0])
-
-
-def final_tail(x):
-    return pl.pallas_call(
-        tail_kernel,
-        out_shape=jax.ShapeDtypeStruct((BEAMS, ROWS, LANES), jnp.float32),
-        scratch_shapes=[
-            pltpu.VMEM((BEAMS, 2, ROWS, LANES), jnp.float32),
-            pltpu.VMEM((BEAMS, 2, ROWS, LANES), jnp.float32),
-        ],
-        compiler_params=pltpu.CompilerParams(vmem_limit_bytes=24 << 20),
-        name="final_tail",
-    )(x)
 
 
 def boxcar_bands(widths):
@@ -344,28 +333,21 @@
             ]
 
 
-def later_kernel(
-    widths, x_ref, out, start, bands_out, norms_out, one, two, held, sems
-):
-    merge_rows(final_groups(x_ref, 0, PER), one, two, WIDE // LANES)
+def final_kernel(widths, x_ref, out, one, two, held, sems):
+    merge_rows(final_groups(x_ref), one, two, WIDE // LANES)
     bands = boxcar_bands(widths)
     norms = boxcar_norms(widths)
-    bands_out[...] = bands
-    norms_out[...] = norms
     parts = []
-    for c in range(PER):
+    for c in range(WIDE // LANES):
         tile = jnp.concatenate([two[b, c] for b in range(BEAMS)], axis=0)
-        if c == 0:
-            start[...] = tile
         parts.append(jnp.concatenate(split(tile), axis=0))
     copies = []
-    for c in range(1, PER):
-        boxcar_tile(parts[c - 1], parts[c], bands, norms, held, c - 1)
+    for c in range(PER):
+        boxcar_tile(parts[c], parts[c + 1], bands, norms, held, c)
+        lanes = pl.ds(c * LANES, LANES)
         copies.append(
             pltpu.make_async_copy(
-                held.at[:, :, :, pl.ds((c - 1) * LANES, LANES)],
-                out.at[:, :, :, pl.ds(c * LANES, LANES)],
-                sems.at[c - 1],
+                held.at[:, :, :, lanes], out.at[:, :, :, lanes], sems.at[c]
             )
         )
         copies[-1].start()
@@ -373,65 +355,24 @@
         copy.wait()
 
 
-def first_kernel(start, tail, bands, norms, rest, out, held, sem):
-    del rest
-    lane = lax.broadcasted_iota(jnp.int32, (BEAMS * ROWS, LANES), 1)
-    edge = tail[...].reshape(BEAMS * ROWS, LANES)
-    before = jnp.where(lane >= LANES // 2, edge, 0.0)
-    here = start[...] + jnp.where(lane < LANES // 2, edge, 0.0)
-    before = jnp.concatenate(split(before), axis=0)
-    here = jnp.concatenate(split(here), axis=0)
-    boxcar_tile(before, here, bands[...], norms[...], held, 0)
-    copy = pltpu.make_async_copy(held, out.at[:, :, :, pl.ds(0, LANES)], sem)
-    copy.start()
-    copy.wait()
-
-
-OUT = jax.ShapeDtypeStruct((BEAMS, NBOX, ROWS, SPAN), jnp.float32)
-
-
-def boxcars_later(x, widths):
-    lanes = SPAN - LANES
-    vmem = pl.BlockSpec(memory_space=pltpu.VMEM)
+def final_boxcars(x, widths):
     return pl.pallas_call(
-        later_kernel,
-        in_specs=[pl.BlockSpec(memory_space=pltpu.SMEM), vmem],
-        out_specs=[pl.BlockSpec(memory_space=pltpu.HBM), vmem, vmem, vmem],
-        out_shape=[
-            OUT,
-            jax.ShapeDtypeStruct((BEAMS * ROWS, LANES), jnp.float32),
-            jax.ShapeDtypeStruct((2 * LANES, NBOX * LANES), jnp.bfloat16),
-            jax.ShapeDtypeStruct((1, NBOX * LANES), jnp.float32),
+        final_kernel,
+        in_specs=[
+            pl.BlockSpec(memory_space=pltpu.SMEM),
+            pl.BlockSpec(memory_space=pltpu.VMEM),
         ],
+        out_specs=pl.BlockSpec(memory_space=pltpu.HBM),
+        out_shape=jax.ShapeDtypeStruct((BEAMS, NBOX, ROWS, SPAN), jnp.float32),
         scratch_shapes=[
             pltpu.VMEM((BEAMS, WIDE // LANES, ROWS, LANES), jnp.float32),
             pltpu.VMEM((BEAMS, WIDE // LANES, ROWS, LANES), jnp.float32),
-            pltpu.VMEM((BEAMS, NBOX, ROWS, lanes), jnp.float32),
-            pltpu.SemaphoreType.DMA((lanes // LANES,)),
+            pltpu.VMEM((BEAMS, NBOX, ROWS, SPAN), jnp.float32),
+            pltpu.SemaphoreType.DMA((PER,)),
         ],
         compiler_params=pltpu.CompilerParams(vmem_limit_bytes=24 << 20),
-        cost_estimate=pl.CostEstimate(
-            flops=2 * 256 * 256 * 768 * 3, bytes_accessed=2 << 20, transcendentals=0
-        ),
-        name="boxcars_later",
+        name="final_boxcars",
     )(widths, x)
-
-
-def boxcars_first(start, tail, bands, norms, rest):
-    return pl.pallas_call(
-        first_kernel,
-        in_specs=[pl.BlockSpec(memory_space=pltpu.VMEM)] * 4
-        + [pl.BlockSpec(memory_space=pltpu.HBM)],
-        out_specs=pl.BlockSpec(memory_space=pltpu.HBM),
-        out_shape=OUT,
-        input_output_aliases={4: 0},
-        scratch_shapes=[
-            pltpu.VMEM((BEAMS, NBOX, ROWS, LANES), jnp.float32),
-            pltpu.SemaphoreType.DMA,
-        ],
-        compiler_params=pltpu.CompilerParams(vmem_limit_bytes=24 << 20),
-        name="boxcars_first",
-    )(start, tail, bands, norms, rest)
 
 
 def later(block, distances):
@@ -451,9 +392,7 @@
         pieces[k] = later(pieces[k], DISTANCES[::-1, k].tolist())
     lined = gather_shifted(pieces, q)
     lined = lax.all_to_all(lined, "chan", 0, 0, tiled=True)
-    tail = later(final_tail(lined), [1] * PARTS)
-    rest, start, bands, norms = boxcars_later(lined, box_widths)
-    return boxcars_first(start, tail, bands, norms, rest)
+    return final_boxcars(lined, box_widths)
 
 
 def solution(mesh):

time: 46.3 us -> 43.5 us (0.940)
  the two profiles are of different devices: /device:TPU:1 before, /device:TPU:4 now
where the time goes in v7:
time: 43.5 us; the launch traced here: 43.2 us
  blocking collectives  22.3 us (51%)
  starting transfers between devices  8.9 us (20%)
  waiting for transfers between devices  6.31 us (15%)
  Pallas kernels  5.61 us (13%)
    all_to_all x1, blocking collectives, per_device(): lined = lax.all_to_all(lined, 'chan', 0, 0, tiled=True)  22.3 us
    ppermute x5, starting transfers between devices, later(): return lax.ppermute(block, ('chan', 'tm'), route)  8.9 us
    ppermute x5, waiting for transfers between devices, later(): return lax.ppermute(block, ('chan', 'tm'), route)  6.31 us
    pallas_call x1, Pallas kernels, final_boxcars(): pl.pallas_call(final_kernel, in_specs=[pl.BlockSpec(memory_space=pltpu.SM...  2.56 us
    pallas_call x1, Pallas kernels, local_plane(): pl.pallas_call(local_kernel, in_specs=[pl.BlockSpec(memory_space=pltpu.SM...  2.55 us
  transfers between devices with their start and end apart: 5, of which 1 were waited for; matrix products, arithmetic and copies ran while one was open for 0% of the time, Pallas kernels for 0%

profile of v7, /device:TPU:4, one launch (start us, length us, event | category | flops | bytes accessed | tf_op | source)
XLA Modules:
  0.0 43.2 jit_solution(15402130180133594431)
XLA Ops:
  0.0 0.0 copy-start
  0.0 2.5 %local_plane.1 = (f32[64,8,128]{2,1,0:T(8,128)S(1)}, f32[60,8,128]{2,1,0:T(8,128)S(1)}, f32[38,8,128]{2,1,0:T(8,128)S(1)}, f32[29,8,128]{2,1,0:T(8,128)S(1)}, f3...) custom-call(s32[1]{0:T(128)} %bitcast.q_ref, f32[1,512]{1,0:T(1,128)} %bitcast.6, bf16[2,512,512]{2,1,0:T(8,128)(2,1)} %x_hbm.1), custom_call_target="tpu_custom_call" | custom-call | tf_op jit(solution)/shard_map/local_plane/pallas_call | solution.py:223
  2.6 1.9 %collective-permute-start = (f32[60,8,128]{2,1,0:T(8,128)S(1)}, f32[60,8,128]{2,1,0:T(8,128)S(1)}, u32[]{:S(2)}, u32[]{:S(2)}) collective-permute-start(f32[60,8,128]{2,1,0:T(8,128)S(1)} %get-tuple-element.12), channel_id=1, source_target_pairs={{0,1},{1,2},{2,3},{3,4},{4,5},{5,6},{6,7},{8,9},{9,10},{10,11},{11... | collective-permute-start | bytes 737288 | tf_op jit(solution)/shard_map/ppermute | solution.py:385
  4.5 3.1 %collective-permute-start.1 = (f32[38,8,128]{2,1,0:T(8,128)S(1)}, f32[38,8,128]{2,1,0:T(8,128)S(1)}, u32[]{:S(2)}, u32[]{:S(2)}) collective-permute-start(f32[38,8,128]{2,1,0:T(8,128)S(1)} %get-tuple-element.13), channel_id=1, source_target_pairs={{0,2},{1,3},{2,4},{3,5},{4,6},{5,7},{8,10},{9,11},{10,12},{11,13},... | collective-permute-start | bytes 466952 | tf_op jit(solution)/shard_map/ppermute | solution.py:385
  7.6 1.9 %collective-permute-start.2 = (f32[29,8,128]{2,1,0:T(8,128)S(1)}, f32[29,8,128]{2,1,0:T(8,128)S(1)}, u32[]{:S(2)}, u32[]{:S(2)}) collective-permute-start(f32[29,8,128]{2,1,0:T(8,128)S(1)} %get-tuple-element.14), channel_id=1, source_target_pairs={{0,3},{1,4},{2,5},{3,6},{4,7},{8,11},{9,12},{10,13},{11,14},{12,15... | collective-permute-start | bytes 356360 | tf_op jit(solution)/shard_map/ppermute | solution.py:385
  9.5 1.3 %collective-permute-start.3 = (f32[15,8,128]{2,1,0:T(8,128)S(1)}, f32[15,8,128]{2,1,0:T(8,128)S(1)}, u32[]{:S(2)}, u32[]{:S(2)}) collective-permute-start(f32[15,8,128]{2,1,0:T(8,128)S(1)} %get-tuple-element.15), channel_id=1, source_target_pairs={{0,4},{1,5},{2,6},{3,7},{8,12},{9,13},{10,14},{11,15},{16,20},{17,... | collective-permute-start | bytes 184328 | tf_op jit(solution)/shard_map/ppermute | solution.py:385
  10.8 0.7 %collective-permute-start.4 = (f32[1,8,128]{2,1,0:T(8,128)S(1)}, f32[1,8,128]{2,1,0:T(8,128)S(1)}, u32[]{:S(2)}, u32[]{:S(2)}) collective-permute-start(f32[1,8,128]{2,1,0:T(8,128)S(1)} %get-tuple-element.16), channel_id=1, source_target_pairs={{0,5},{1,6},{2,7}} | collective-permute-start | bytes 12296 | tf_op jit(solution)/shard_map/ppermute | solution.py:385
  11.5 0.0 collective-permute-done.4.r5
  11.5 6.3 %collective-permute-done.3.r4 = f32[15,8,128]{2,1,0:T(8,128)S(1)} collective-permute-done((f32[15,8,128]{2,1,0:T(8,128)S(1)}, f32[15,8,128]{2,1,0:T(8,128)S(1)}, u32[]{:S(2)}, u32[]{:S(2)}) %collective-permute-start.3) | collective-permute-done | bytes 61472 | tf_op jit(solution)/shard_map/ppermute | solution.py:385
  17.8 0.0 collective-permute-done.2.r3
  17.8 0.0 collective-permute-done.1.r2
  17.8 0.0 collective-permute-done.r1
  17.8 0.5 %gather_shifted.1 = f32[768,128]{1,0:T(8,128)S(1)} custom-call(s32[1]{0:T(128)} %bitcast.q_ref, f32[64,8,128]{2,1,0:T(8,128)S(1)} %get-tuple-element.11.o0, f32[60,8,128]{2,1,0:T(8,128)S(1)} %collective-permute-done.r1, f32[38,8,128]{2,1,0:T(8,128)S(1)} %collective-permute-done.1.r2, f32[29,8,128]{2,1,0:T(8,128)S(1)} %collective-permute-done.2.r3, ...), custom_call_target="tpu_custom_call" | custom-call | tf_op jit(solution)/shard_map/gather_shifted/pallas_call | solution.py:274
  18.3 22.3 %all_to_all.11 = f32[32,24,128]{2,1,0:T(8,128)S(1)} all-to-all(f32[32,24,128]{2,1,0:T(8,128)S(1)} %bitcast.4), channel_id=1, replica_groups=mesh['chan'=32,'tm'=8] {'chan'}, dimensions={0} | all-to-all | bytes 786432 | tf_op jit(solution)/shard_map/all_to_all | solution.py:394
  40.6 0.0 copy-done
  40.6 2.6 %final_boxcars.1 = f32[2,6,64,512]{3,2,1,0:T(8,128)} custom-call(s32[6]{0:T(128)S(1)} %copy-done, f32[768,128]{1,0:T(8,128)S(1)} %bitcast.5), custom_call_target="tpu_custom_call" | custom-call | tf_op jit(solution)/shard_map/final_boxcars/pallas_call | solution.py:359
Async XLA Ops:
  0.0 40.6 %copy-start = (s32[6]{0:T(128)S(1)}, s32[6]{0:T(128)}, u32[]{:S(2)}) copy-start(s32[6]{0:T(128)} %widths.1) | copy-start | bytes 76
  2.6 15.3 %collective-permute-start = (f32[60,8,128]{2,1,0:T(8,128)S(1)}, f32[60,8,128]{2,1,0:T(8,128)S(1)}, u32[]{:S(2)}, u32[]{:S(2)}) collective-permute-start(f32[60,8,128]{2,1,0:T(8,128)S(1)} %get-tuple-element.12), channel_id=1, source_target_pairs={{0,1},{1,2},{2,3},{3,4},{4,5},{5,6},{6,7},{8,9},{9,10},{10,11},{11... | collective-permute-start | bytes 737288 | tf_op jit(solution)/shard_map/ppermute | solution.py:385
  4.5 13.3 %collective-permute-start.1 = (f32[38,8,128]{2,1,0:T(8,128)S(1)}, f32[38,8,128]{2,1,0:T(8,128)S(1)}, u32[]{:S(2)}, u32[]{:S(2)}) collective-permute-start(f32[38,8,128]{2,1,0:T(8,128)S(1)} %get-tuple-element.13), channel_id=1, source_target_pairs={{0,2},{1,3},{2,4},{3,5},{4,6},{5,7},{8,10},{9,11},{10,12},{11,13},... | collective-permute-start | bytes 466952 | tf_op jit(solution)/shard_map/ppermute | solution.py:385
  7.6 10.2 %collective-permute-start.2 = (f32[29,8,128]{2,1,0:T(8,128)S(1)}, f32[29,8,128]{2,1,0:T(8,128)S(1)}, u32[]{:S(2)}, u32[]{:S(2)}) collective-permute-start(f32[29,8,128]{2,1,0:T(8,128)S(1)} %get-tuple-element.14), channel_id=1, source_target_pairs={{0,3},{1,4},{2,5},{3,6},{4,7},{8,11},{9,12},{10,13},{11,14},{12,15... | collective-permute-start | bytes 356360 | tf_op jit(solution)/shard_map/ppermute | solution.py:385
  9.5 8.3 %collective-permute-start.3 = (f32[15,8,128]{2,1,0:T(8,128)S(1)}, f32[15,8,128]{2,1,0:T(8,128)S(1)}, u32[]{:S(2)}, u32[]{:S(2)}) collective-permute-start(f32[15,8,128]{2,1,0:T(8,128)S(1)} %get-tuple-element.15), channel_id=1, source_target_pairs={{0,4},{1,5},{2,6},{3,7},{8,12},{9,13},{10,14},{11,15},{16,20},{17,... | collective-permute-start | bytes 184328 | tf_op jit(solution)/shard_map/ppermute | solution.py:385
  10.8 0.7 %collective-permute-start.4 = (f32[1,8,128]{2,1,0:T(8,128)S(1)}, f32[1,8,128]{2,1,0:T(8,128)S(1)}, u32[]{:S(2)}, u32[]{:S(2)}) collective-permute-start(f32[1,8,128]{2,1,0:T(8,128)S(1)} %get-tuple-element.16), channel_id=1, source_target_pairs={{0,5},{1,6},{2,7}} | collective-permute-start | bytes 12296 | tf_op jit(solution)/shard_map/ppermute | solution.py:385

commit v8 on v7

--- a/solution.py
+++ b/solution.py
@@ -19,7 +19,7 @@
 TILES = 16
 UNITS = 6
 PER = SPAN // LANES
-BLOCK = 24
+BLOCK = 20
 
 
 def tails(a):
@@ -391,7 +391,9 @@
     for k in range(REACH - 1, 0, -1):
         pieces[k] = later(pieces[k], DISTANCES[::-1, k].tolist())
     lined = gather_shifted(pieces, q)
+    lined = lined.reshape(PARTS, 1, BLOCK * LANES)
     lined = lax.all_to_all(lined, "chan", 0, 0, tiled=True)
+    lined = lined.reshape(PARTS * BLOCK, LANES)
     return final_boxcars(lined, box_widths)
 
 

time: 43.5 us -> 42.4 us (0.975)
  blocking collectives: 22.3 us -> 21 us
    all_to_all x1, blocking collectives: 22.3 us -> 21 us  [per_device(): lined = lax.all_to_all(lined, 'chan', 0, 0, tiled=True)]
where the time goes in v8:
time: 42.4 us; the launch traced here: 41.8 us
  blocking collectives  21 us (50%)
  starting transfers between devices  8.9 us (21%)
  waiting for transfers between devices  6.31 us (15%)
  Pallas kernels  5.55 us (13%)
    all_to_all x1, blocking collectives, per_device(): lined = lax.all_to_all(lined, 'chan', 0, 0, tiled=True)  21 us
    ppermute x5, starting transfers between devices, later(): return lax.ppermute(block, ('chan', 'tm'), route)  8.9 us
    ppermute x5, waiting for transfers between devices, later(): return lax.ppermute(block, ('chan', 'tm'), route)  6.31 us
    pallas_call x1, Pallas kernels, local_plane(): pl.pallas_call(local_kernel, in_specs=[pl.BlockSpec(memory_space=pltpu.SM...  2.55 us
    pallas_call x1, Pallas kernels, final_boxcars(): pl.pallas_call(final_kernel, in_specs=[pl.BlockSpec(memory_space=pltpu.SM...  2.53 us
  transfers between devices with their start and end apart: 5, of which 1 were waited for; matrix products, arithmetic and copies ran while one was open for 0% of the time, Pallas kernels for 0%

profile of v8, /device:TPU:4, one launch (start us, length us, event | category | flops | bytes accessed | tf_op | source)
XLA Modules:
  0.0 41.8 jit_solution(10854665575683105125)
XLA Ops:
  0.0 0.0 copy-start
  0.0 2.5 %local_plane.1 = (f32[64,8,128]{2,1,0:T(8,128)S(1)}, f32[60,8,128]{2,1,0:T(8,128)S(1)}, f32[38,8,128]{2,1,0:T(8,128)S(1)}, f32[29,8,128]{2,1,0:T(8,128)S(1)}, f3...) custom-call(s32[1]{0:T(128)} %bitcast.q_ref, f32[1,512]{1,0:T(1,128)} %bitcast.6, bf16[2,512,512]{2,1,0:T(8,128)(2,1)} %x_hbm.1), custom_call_target="tpu_custom_call" | custom-call | tf_op jit(solution)/shard_map/local_plane/pallas_call | solution.py:223
  2.6 1.9 %collective-permute-start = (f32[60,8,128]{2,1,0:T(8,128)S(1)}, f32[60,8,128]{2,1,0:T(8,128)S(1)}, u32[]{:S(2)}, u32[]{:S(2)}) collective-permute-start(f32[60,8,128]{2,1,0:T(8,128)S(1)} %get-tuple-element.12), channel_id=1, source_target_pairs={{0,1},{1,2},{2,3},{3,4},{4,5},{5,6},{6,7},{8,9},{9,10},{10,11},{11... | collective-permute-start | bytes 737288 | tf_op jit(solution)/shard_map/ppermute | solution.py:385
  4.5 3.1 %collective-permute-start.1 = (f32[38,8,128]{2,1,0:T(8,128)S(1)}, f32[38,8,128]{2,1,0:T(8,128)S(1)}, u32[]{:S(2)}, u32[]{:S(2)}) collective-permute-start(f32[38,8,128]{2,1,0:T(8,128)S(1)} %get-tuple-element.13), channel_id=1, source_target_pairs={{0,2},{1,3},{2,4},{3,5},{4,6},{5,7},{8,10},{9,11},{10,12},{11,13},... | collective-permute-start | bytes 466952 | tf_op jit(solution)/shard_map/ppermute | solution.py:385
  7.6 1.9 %collective-permute-start.2 = (f32[29,8,128]{2,1,0:T(8,128)S(1)}, f32[29,8,128]{2,1,0:T(8,128)S(1)}, u32[]{:S(2)}, u32[]{:S(2)}) collective-permute-start(f32[29,8,128]{2,1,0:T(8,128)S(1)} %get-tuple-element.14), channel_id=1, source_target_pairs={{0,3},{1,4},{2,5},{3,6},{4,7},{8,11},{9,12},{10,13},{11,14},{12,15... | collective-permute-start | bytes 356360 | tf_op jit(solution)/shard_map/ppermute | solution.py:385
  9.5 1.3 %collective-permute-start.3 = (f32[15,8,128]{2,1,0:T(8,128)S(1)}, f32[15,8,128]{2,1,0:T(8,128)S(1)}, u32[]{:S(2)}, u32[]{:S(2)}) collective-permute-start(f32[15,8,128]{2,1,0:T(8,128)S(1)} %get-tuple-element.15), channel_id=1, source_target_pairs={{0,4},{1,5},{2,6},{3,7},{8,12},{9,13},{10,14},{11,15},{16,20},{17,... | collective-permute-start | bytes 184328 | tf_op jit(solution)/shard_map/ppermute | solution.py:385
  10.8 0.7 %collective-permute-start.4 = (f32[1,8,128]{2,1,0:T(8,128)S(1)}, f32[1,8,128]{2,1,0:T(8,128)S(1)}, u32[]{:S(2)}, u32[]{:S(2)}) collective-permute-start(f32[1,8,128]{2,1,0:T(8,128)S(1)} %get-tuple-element.16), channel_id=1, source_target_pairs={{0,5},{1,6},{2,7}} | collective-permute-start | bytes 12296 | tf_op jit(solution)/shard_map/ppermute | solution.py:385
  11.5 0.0 collective-permute-done.4.r5
  11.5 6.3 %collective-permute-done.3.r4 = f32[15,8,128]{2,1,0:T(8,128)S(1)} collective-permute-done((f32[15,8,128]{2,1,0:T(8,128)S(1)}, f32[15,8,128]{2,1,0:T(8,128)S(1)}, u32[]{:S(2)}, u32[]{:S(2)}) %collective-permute-start.3) | collective-permute-done | bytes 61472 | tf_op jit(solution)/shard_map/ppermute | solution.py:385
  17.8 0.0 collective-permute-done.2.r3
  17.8 0.0 collective-permute-done.1.r2
  17.8 0.0 collective-permute-done.r1
  17.8 0.5 %gather_shifted.1 = f32[640,128]{1,0:T(8,128)S(1)} custom-call(s32[1]{0:T(128)} %bitcast.q_ref, f32[64,8,128]{2,1,0:T(8,128)S(1)} %get-tuple-element.11.o0, f32[60,8,128]{2,1,0:T(8,128)S(1)} %collective-permute-done.r1, f32[38,8,128]{2,1,0:T(8,128)S(1)} %collective-permute-done.1.r2, f32[29,8,128]{2,1,0:T(8,128)S(1)} %collective-permute-done.2.r3, ...), custom_call_target="tpu_custom_call" | custom-call | tf_op jit(solution)/shard_map/gather_shifted/pallas_call | solution.py:274
  18.3 21.0 %all_to_all.5 = f32[32,1,2560]{2,1,0:T(1,128)S(1)} all-to-all(f32[32,1,2560]{2,1,0:T(1,128)S(1)} %bitcast.4), channel_id=1, replica_groups=mesh['chan'=32,'tm'=8] {'chan'}, dimensions={0} | all-to-all | bytes 655360 | tf_op jit(solution)/shard_map/all_to_all | solution.py:395
  39.3 0.0 copy-done
  39.3 2.5 %final_boxcars.1 = f32[2,6,64,512]{3,2,1,0:T(8,128)} custom-call(s32[6]{0:T(128)S(1)} %copy-done, f32[640,128]{1,0:T(8,128)S(1)} %bitcast.5), custom_call_target="tpu_custom_call" | custom-call | tf_op jit(solution)/shard_map/final_boxcars/pallas_call | solution.py:359
Async XLA Ops:
  0.0 39.3 %copy-start = (s32[6]{0:T(128)S(1)}, s32[6]{0:T(128)}, u32[]{:S(2)}) copy-start(s32[6]{0:T(128)} %widths.1) | copy-start | bytes 76
  2.6 15.3 %collective-permute-start = (f32[60,8,128]{2,1,0:T(8,128)S(1)}, f32[60,8,128]{2,1,0:T(8,128)S(1)}, u32[]{:S(2)}, u32[]{:S(2)}) collective-permute-start(f32[60,8,128]{2,1,0:T(8,128)S(1)} %get-tuple-element.12), channel_id=1, source_target_pairs={{0,1},{1,2},{2,3},{3,4},{4,5},{5,6},{6,7},{8,9},{9,10},{10,11},{11... | collective-permute-start | bytes 737288 | tf_op jit(solution)/shard_map/ppermute | solution.py:385
  4.5 13.3 %collective-permute-start.1 = (f32[38,8,128]{2,1,0:T(8,128)S(1)}, f32[38,8,128]{2,1,0:T(8,128)S(1)}, u32[]{:S(2)}, u32[]{:S(2)}) collective-permute-start(f32[38,8,128]{2,1,0:T(8,128)S(1)} %get-tuple-element.13), channel_id=1, source_target_pairs={{0,2},{1,3},{2,4},{3,5},{4,6},{5,7},{8,10},{9,11},{10,12},{11,13},... | collective-permute-start | bytes 466952 | tf_op jit(solution)/shard_map/ppermute | solution.py:385
  7.6 10.2 %collective-permute-start.2 = (f32[29,8,128]{2,1,0:T(8,128)S(1)}, f32[29,8,128]{2,1,0:T(8,128)S(1)}, u32[]{:S(2)}, u32[]{:S(2)}) collective-permute-start(f32[29,8,128]{2,1,0:T(8,128)S(1)} %get-tuple-element.14), channel_id=1, source_target_pairs={{0,3},{1,4},{2,5},{3,6},{4,7},{8,11},{9,12},{10,13},{11,14},{12,15... | collective-permute-start | bytes 356360 | tf_op jit(solution)/shard_map/ppermute | solution.py:385
  9.5 8.3 %collective-permute-start.3 = (f32[15,8,128]{2,1,0:T(8,128)S(1)}, f32[15,8,128]{2,1,0:T(8,128)S(1)}, u32[]{:S(2)}, u32[]{:S(2)}) collective-permute-start(f32[15,8,128]{2,1,0:T(8,128)S(1)} %get-tuple-element.15), channel_id=1, source_target_pairs={{0,4},{1,5},{2,6},{3,7},{8,12},{9,13},{10,14},{11,15},{16,20},{17,... | collective-permute-start | bytes 184328 | tf_op jit(solution)/shard_map/ppermute | solution.py:385
  10.8 0.7 %collective-permute-start.4 = (f32[1,8,128]{2,1,0:T(8,128)S(1)}, f32[1,8,128]{2,1,0:T(8,128)S(1)}, u32[]{:S(2)}, u32[]{:S(2)}) collective-permute-start(f32[1,8,128]{2,1,0:T(8,128)S(1)} %get-tuple-element.16), channel_id=1, source_target_pairs={{0,5},{1,6},{2,7}} | collective-permute-start | bytes 12296 | tf_op jit(solution)/shard_map/ppermute | solution.py:385

commit v9 on v8

--- a/solution.py
+++ b/solution.py
@@ -19,7 +19,8 @@
 TILES = 16
 UNITS = 6
 PER = SPAN // LANES
-BLOCK = 20
+BLOCK = 10
+TOP = 32000.0
 
 
 def tails(a):
@@ -103,6 +104,36 @@
     first = x.astype(jnp.bfloat16)
     second = (x - first.astype(jnp.float32)).astype(jnp.bfloat16)
     return first, second
+
+
+def exponent_of(largest):
+    return jnp.floor(64.0 * jnp.log2(jnp.maximum(largest, 1e-36))).astype(jnp.int32) + 2
+
+
+def largest_of(tiles):
+    top = jnp.abs(tiles[0])
+    for tile in tiles[1:]:
+        top = jnp.maximum(top, jnp.abs(tile))
+    top = jnp.max(jnp.max(top, axis=1, keepdims=True), axis=0, keepdims=True)
+    return jnp.broadcast_to(top, (8, LANES))
+
+
+def span_of(exponent):
+    return jnp.exp2(exponent.astype(jnp.float32) * (1.0 / 64.0))
+
+
+def code(x, inverse):
+    return jnp.round(x * inverse * TOP).astype(jnp.int32)
+
+
+def pair(high, low):
+    return (high << 16) | (low & 0xFFFF)
+
+
+def unpair(word, step):
+    high = (word >> 16).astype(jnp.float32) * step
+    low = ((word << 16) >> 16).astype(jnp.float32) * step
+    return high, low
 
 
 def roll(x, shift):
@@ -261,12 +292,21 @@
         held[tiles[1], rows, :] = packed[slots[1]] + packed[slots[PER + 1]]
         held[tiles[2], rows, :] = packed[slots[2]]
         held[tiles[3], rows, :] = packed[slots[3]]
-    for c in range(WIDE // LANES):
-        for r in range(8):
-            b, m, i = r >> 2, r >> 1 & 1, r & 1
-            out[pl.ds(m * BLOCK + c * 4 + b * 2 + i, TILES, stride=2 * BLOCK), :] = held[
-                c, pl.ds(r, TILES, stride=8), :
-            ]
+    tiles = WIDE // LANES
+    values = [held[c, pl.ds(8 * a, 8), :] for c in range(tiles) for a in range(TILES)]
+    exponent = exponent_of(largest_of(values))
+    inverse = 1.0 / span_of(exponent)[:1]
+    exponent = jnp.broadcast_to(exponent[:1], (TILES, LANES))
+    lane = lax.broadcasted_iota(jnp.int32, (TILES, LANES), 1)
+    for c in range(tiles):
+        for r in range(4):
+            high = code(held[c, pl.ds(r, TILES, stride=8), :], inverse)
+            low = code(held[c, pl.ds(4 + r, TILES, stride=8), :], inverse)
+            word = pair(high, low)
+            if c == 0:
+                word = jnp.where(lane == 0, exponent, word)
+            rows = pl.ds((r >> 1) * BLOCK + c * 2 + (r & 1), TILES, stride=2 * BLOCK)
+            out[rows, :] = word
 
 
 def gather_shifted(pieces, q):
@@ -274,7 +314,7 @@
     return pl.pallas_call(
         gather_kernel,
         in_specs=[pl.BlockSpec(memory_space=pltpu.SMEM)] + [vmem] * REACH,
-        out_shape=jax.ShapeDtypeStruct((PARTS * BLOCK, LANES), jnp.float32),
+        out_shape=jax.ShapeDtypeStruct((PARTS * BLOCK, LANES), jnp.int32),
         scratch_shapes=[
             pltpu.SMEM((REACH + 2,), jnp.int32),
             pltpu.VMEM((SPARE + 1, 8, LANES), jnp.float32),
@@ -286,19 +326,18 @@
 
 
 def final_groups(x_ref):
-    beams = []
-    for b in range(BEAMS):
-        groups = []
-        for g in range(4):
-            trials = []
-            for e in range(2):
-                chunks = [
-                    x_ref[pl.ds(g * BLOCK + c * 4 + b * 2 + e, 8, stride=4 * BLOCK), :]
-                    for c in range(WIDE // LANES)
-                ]
-                trials.append(jnp.concatenate(chunks, axis=1))
-            groups.append(trials)
-        beams.append(groups)
+    beams = [[[] for _ in range(4)] for _ in range(BEAMS)]
+    for g in range(4):
+        for e in range(2):
+            words = [
+                x_ref[pl.ds(g * BLOCK + c * 2 + e, 8, stride=4 * BLOCK), :]
+                for c in range(WIDE // LANES)
+            ]
+            step = jnp.broadcast_to(span_of(words[0][:, :1]) * (1.0 / TOP), (8, LANES))
+            chunks = [unpair(word, step) for word in words]
+            for b in range(BEAMS):
+                row = jnp.concatenate([chunk[b] for chunk in chunks], axis=1)
+                beams[b][g].append(row)
     return beams
 
 

time: 42.4 us -> 39.4 us (0.929)
  blocking collectives: 21 us -> 18 us
    all_to_all x1, blocking collectives: 21 us -> 18 us  [per_device(): lined = lax.all_to_all(lined, 'chan', 0, 0, tiled=True)]
where the time goes in v9:
time: 39.4 us; the launch traced here: 39 us
  blocking collectives  18 us (46%)
  starting transfers between devices  8.9 us (23%)
  waiting for transfers between devices  6.31 us (16%)
  Pallas kernels  5.71 us (14%)
    all_to_all x1, blocking collectives, per_device(): lined = lax.all_to_all(lined, 'chan', 0, 0, tiled=True)  18 us
    ppermute x5, starting transfers between devices, later(): return lax.ppermute(block, ('chan', 'tm'), route)  8.9 us
    ppermute x5, waiting for transfers between devices, later(): return lax.ppermute(block, ('chan', 'tm'), route)  6.31 us
    pallas_call x1, Pallas kernels, final_boxcars(): pl.pallas_call(final_kernel, in_specs=[pl.BlockSpec(memory_space=pltpu.SM...  2.58 us
    pallas_call x1, Pallas kernels, local_plane(): pl.pallas_call(local_kernel, in_specs=[pl.BlockSpec(memory_space=pltpu.SM...  2.55 us
  transfers between devices with their start and end apart: 5, of which 1 were waited for; matrix products, arithmetic and copies ran while one was open for 0% of the time, Pallas kernels for 0%

profile of v9, /device:TPU:4, one launch (start us, length us, event | category | flops | bytes accessed | tf_op | source)
XLA Modules:
  0.0 39.0 jit_solution(5796384024227688967)
XLA Ops:
  0.0 0.0 copy-start
  0.0 2.5 %local_plane.1 = (f32[64,8,128]{2,1,0:T(8,128)S(1)}, f32[60,8,128]{2,1,0:T(8,128)S(1)}, f32[38,8,128]{2,1,0:T(8,128)S(1)}, f32[29,8,128]{2,1,0:T(8,128)S(1)}, f3...) custom-call(s32[1]{0:T(128)} %bitcast.q_ref, f32[1,512]{1,0:T(1,128)} %bitcast.6, bf16[2,512,512]{2,1,0:T(8,128)(2,1)} %x_hbm.1), custom_call_target="tpu_custom_call" | custom-call | tf_op jit(solution)/shard_map/local_plane/pallas_call | solution.py:254
  2.6 1.9 %collective-permute-start = (f32[60,8,128]{2,1,0:T(8,128)S(1)}, f32[60,8,128]{2,1,0:T(8,128)S(1)}, u32[]{:S(2)}, u32[]{:S(2)}) collective-permute-start(f32[60,8,128]{2,1,0:T(8,128)S(1)} %get-tuple-element.12), channel_id=1, source_target_pairs={{0,1},{1,2},{2,3},{3,4},{4,5},{5,6},{6,7},{8,9},{9,10},{10,11},{11... | collective-permute-start | bytes 737288 | tf_op jit(solution)/shard_map/ppermute | solution.py:424
  4.5 3.1 %collective-permute-start.1 = (f32[38,8,128]{2,1,0:T(8,128)S(1)}, f32[38,8,128]{2,1,0:T(8,128)S(1)}, u32[]{:S(2)}, u32[]{:S(2)}) collective-permute-start(f32[38,8,128]{2,1,0:T(8,128)S(1)} %get-tuple-element.13), channel_id=1, source_target_pairs={{0,2},{1,3},{2,4},{3,5},{4,6},{5,7},{8,10},{9,11},{10,12},{11,13},... | collective-permute-start | bytes 466952 | tf_op jit(solution)/shard_map/ppermute | solution.py:424
  7.6 1.9 %collective-permute-start.2 = (f32[29,8,128]{2,1,0:T(8,128)S(1)}, f32[29,8,128]{2,1,0:T(8,128)S(1)}, u32[]{:S(2)}, u32[]{:S(2)}) collective-permute-start(f32[29,8,128]{2,1,0:T(8,128)S(1)} %get-tuple-element.14), channel_id=1, source_target_pairs={{0,3},{1,4},{2,5},{3,6},{4,7},{8,11},{9,12},{10,13},{11,14},{12,15... | collective-permute-start | bytes 356360 | tf_op jit(solution)/shard_map/ppermute | solution.py:424
  9.5 1.3 %collective-permute-start.3 = (f32[15,8,128]{2,1,0:T(8,128)S(1)}, f32[15,8,128]{2,1,0:T(8,128)S(1)}, u32[]{:S(2)}, u32[]{:S(2)}) collective-permute-start(f32[15,8,128]{2,1,0:T(8,128)S(1)} %get-tuple-element.15), channel_id=1, source_target_pairs={{0,4},{1,5},{2,6},{3,7},{8,12},{9,13},{10,14},{11,15},{16,20},{17,... | collective-permute-start | bytes 184328 | tf_op jit(solution)/shard_map/ppermute | solution.py:424
  10.8 0.7 %collective-permute-start.4 = (f32[1,8,128]{2,1,0:T(8,128)S(1)}, f32[1,8,128]{2,1,0:T(8,128)S(1)}, u32[]{:S(2)}, u32[]{:S(2)}) collective-permute-start(f32[1,8,128]{2,1,0:T(8,128)S(1)} %get-tuple-element.16), channel_id=1, source_target_pairs={{0,5},{1,6},{2,7}} | collective-permute-start | bytes 12296 | tf_op jit(solution)/shard_map/ppermute | solution.py:424
  11.5 0.0 collective-permute-done.4.r5
  11.5 6.3 %collective-permute-done.3.r4 = f32[15,8,128]{2,1,0:T(8,128)S(1)} collective-permute-done((f32[15,8,128]{2,1,0:T(8,128)S(1)}, f32[15,8,128]{2,1,0:T(8,128)S(1)}, u32[]{:S(2)}, u32[]{:S(2)}) %collective-permute-start.3) | collective-permute-done | bytes 61472 | tf_op jit(solution)/shard_map/ppermute | solution.py:424
  17.8 0.0 collective-permute-done.2.r3
  17.8 0.0 collective-permute-done.1.r2
  17.8 0.0 collective-permute-done.r1
  17.8 0.6 %gather_shifted.1 = s32[320,128]{1,0:T(8,128)S(1)} custom-call(s32[1]{0:T(128)} %bitcast.q_ref, f32[64,8,128]{2,1,0:T(8,128)S(1)} %get-tuple-element.11.o0, f32[60,8,128]{2,1,0:T(8,128)S(1)} %collective-permute-done.r1, f32[38,8,128]{2,1,0:T(8,128)S(1)} %collective-permute-done.1.r2, f32[29,8,128]{2,1,0:T(8,128)S(1)} %collective-permute-done.2.r3, ...), custom_call_target="tpu_custom_call" | custom-call | tf_op jit(solution)/shard_map/gather_shifted/pallas_call | solution.py:314
  18.4 18.0 %all_to_all.5 = s32[32,1,1280]{2,1,0:T(1,128)S(1)} all-to-all(s32[32,1,1280]{2,1,0:T(1,128)S(1)} %bitcast.4), channel_id=1, replica_groups=mesh['chan'=32,'tm'=8] {'chan'}, dimensions={0} | all-to-all | bytes 327680 | tf_op jit(solution)/shard_map/all_to_all | solution.py:434
  36.4 0.0 copy-done
  36.4 2.6 %final_boxcars.1 = f32[2,6,64,512]{3,2,1,0:T(8,128)} custom-call(s32[6]{0:T(128)S(1)} %copy-done, s32[320,128]{1,0:T(8,128)S(1)} %bitcast.5), custom_call_target="tpu_custom_call" | custom-call | tf_op jit(solution)/shard_map/final_boxcars/pallas_call | solution.py:398
Async XLA Ops:
  0.0 36.4 %copy-start = (s32[6]{0:T(128)S(1)}, s32[6]{0:T(128)}, u32[]{:S(2)}) copy-start(s32[6]{0:T(128)} %widths.1) | copy-start | bytes 76
  2.6 15.3 %collective-permute-start = (f32[60,8,128]{2,1,0:T(8,128)S(1)}, f32[60,8,128]{2,1,0:T(8,128)S(1)}, u32[]{:S(2)}, u32[]{:S(2)}) collective-permute-start(f32[60,8,128]{2,1,0:T(8,128)S(1)} %get-tuple-element.12), channel_id=1, source_target_pairs={{0,1},{1,2},{2,3},{3,4},{4,5},{5,6},{6,7},{8,9},{9,10},{10,11},{11... | collective-permute-start | bytes 737288 | tf_op jit(solution)/shard_map/ppermute | solution.py:424
  4.5 13.3 %collective-permute-start.1 = (f32[38,8,128]{2,1,0:T(8,128)S(1)}, f32[38,8,128]{2,1,0:T(8,128)S(1)}, u32[]{:S(2)}, u32[]{:S(2)}) collective-permute-start(f32[38,8,128]{2,1,0:T(8,128)S(1)} %get-tuple-element.13), channel_id=1, source_target_pairs={{0,2},{1,3},{2,4},{3,5},{4,6},{5,7},{8,10},{9,11},{10,12},{11,13},... | collective-permute-start | bytes 466952 | tf_op jit(solution)/shard_map/ppermute | solution.py:424
  7.6 10.2 %collective-permute-start.2 = (f32[29,8,128]{2,1,0:T(8,128)S(1)}, f32[29,8,128]{2,1,0:T(8,128)S(1)}, u32[]{:S(2)}, u32[]{:S(2)}) collective-permute-start(f32[29,8,128]{2,1,0:T(8,128)S(1)} %get-tuple-element.14), channel_id=1, source_target_pairs={{0,3},{1,4},{2,5},{3,6},{4,7},{8,11},{9,12},{10,13},{11,14},{12,15... | collective-permute-start | bytes 356360 | tf_op jit(solution)/shard_map/ppermute | solution.py:424
  9.5 8.3 %collective-permute-start.3 = (f32[15,8,128]{2,1,0:T(8,128)S(1)}, f32[15,8,128]{2,1,0:T(8,128)S(1)}, u32[]{:S(2)}, u32[]{:S(2)}) collective-permute-start(f32[15,8,128]{2,1,0:T(8,128)S(1)} %get-tuple-element.15), channel_id=1, source_target_pairs={{0,4},{1,5},{2,6},{3,7},{8,12},{9,13},{10,14},{11,15},{16,20},{17,... | collective-permute-start | bytes 184328 | tf_op jit(solution)/shard_map/ppermute | solution.py:424
  10.8 0.7 %collective-permute-start.4 = (f32[1,8,128]{2,1,0:T(8,128)S(1)}, f32[1,8,128]{2,1,0:T(8,128)S(1)}, u32[]{:S(2)}, u32[]{:S(2)}) collective-permute-start(f32[1,8,128]{2,1,0:T(8,128)S(1)} %get-tuple-element.16), channel_id=1, source_target_pairs={{0,5},{1,6},{2,7}} | collective-permute-start | bytes 12296 | tf_op jit(solution)/shard_map/ppermute | solution.py:424

commit v10 on v9

--- a/solution.py
+++ b/solution.py
@@ -55,7 +55,7 @@
             for i, share in enumerate(shares):
                 if share:
                     counts[q, k + i] += share
-    sizes = [64, 60, 38, 29, 15, 1]
+    sizes = [64, 60, 38, 30, 16, 2]
     buffers = np.zeros((PARTS, REACH), np.int32)
     distances = np.zeros((PARTS, REACH), np.int32)
     for q in range(PARTS):
@@ -246,8 +246,22 @@
             packed[slot] = rows[:, i * LANES : (i + 1) * LANES]
         for slot, origin in again:
             packed[slot] = packed[origin]
-    for k, out in enumerate((o0, o1, o2, o3, o4, o5)):
-        out[...] = packed[pl.ds(STARTS[k], SIZES[k])]
+    o0[...] = packed[pl.ds(0, SIZES[0])]
+    tiles = [
+        two[b, c, pl.ds(8 * a, 8), :]
+        for b in range(BEAMS)
+        for c in range(WIDE // LANES)
+        for a in range(8)
+    ]
+    exponent = exponent_of(largest_of(tiles))
+    inverse = 1.0 / span_of(exponent)
+    for k, out in enumerate((o1, o2, o3, o4, o5), 1):
+        words = SIZES[k] // 2
+        for t in range(words):
+            slot = STARTS[k] + 2 * t
+            high, low = code(packed[slot], inverse), code(packed[slot + 1], inverse)
+            out[t] = pair(high, low)
+        out[words] = exponent
 
 
 def local_plane(x, scale, q):
@@ -258,7 +272,8 @@
             pl.BlockSpec(memory_space=pltpu.HBM),
             pl.BlockSpec(memory_space=pltpu.HBM),
         ],
-        out_shape=[jax.ShapeDtypeStruct((n, 8, LANES), jnp.float32) for n in SIZES],
+        out_shape=[jax.ShapeDtypeStruct((SIZES[0], 8, LANES), jnp.float32)]
+        + [jax.ShapeDtypeStruct((n // 2 + 1, 8, LANES), jnp.int32) for n in SIZES[1:]],
         scratch_shapes=[
             pltpu.SMEM((REACH + 2,), jnp.int32),
             pltpu.VMEM((1, CHANS), jnp.float32),
@@ -280,8 +295,13 @@
 def gather_kernel(q_ref, o0, r1, r2, r3, r4, r5, out, free, packed, held):
     q = q_ref[0]
     first_slots(q, free)
-    for k, piece in enumerate((o0, r1, r2, r3, r4, r5)):
-        packed[pl.ds(STARTS[k], SIZES[k])] = piece[...]
+    packed[pl.ds(0, SIZES[0])] = o0[...]
+    for k, piece in enumerate((r1, r2, r3, r4, r5), 1):
+        words = SIZES[k] // 2
+        step = span_of(piece[words]) * (1.0 / TOP)
+        for t in range(words):
+            slot = STARTS[k] + 2 * t
+            packed[slot], packed[slot + 1] = unpair(piece[t], step)
     packed[SPARE] = jnp.zeros((8, LANES), jnp.float32)
     for a in range(TILES):
         slots, at, again = unit_slots(q, a, free)

time: 39.4 us -> 38.4 us (0.975)
  waiting for transfers between devices: 6.31 us -> 5.39 us
    ppermute x5, waiting for transfers between devices: 6.31 us -> 5.39 us  [later(): return lax.ppermute(block, ('chan', 'tm'), route)]
where the time goes in v10:
time: 38.4 us; the launch traced here: 38.2 us
  blocking collectives  18.1 us (47%)
  starting transfers between devices  8.9 us (23%)
  Pallas kernels  5.78 us (15%)
  waiting for transfers between devices  5.39 us (14%)
    all_to_all x1, blocking collectives, per_device(): lined = lax.all_to_all(lined, 'chan', 0, 0, tiled=True)  18.1 us
    ppermute x5, starting transfers between devices, later(): return lax.ppermute(block, ('chan', 'tm'), route)  8.9 us
    ppermute x5, waiting for transfers between devices, later(): return lax.ppermute(block, ('chan', 'tm'), route)  5.39 us
    pallas_call x1, Pallas kernels, local_plane(): pl.pallas_call(local_kernel, in_specs=[pl.BlockSpec(memory_space=pltpu.SM...  2.6 us
    pallas_call x1, Pallas kernels, final_boxcars(): pl.pallas_call(final_kernel, in_specs=[pl.BlockSpec(memory_space=pltpu.SM...  2.58 us
  transfers between devices with their start and end apart: 5, of which 1 were waited for; matrix products, arithmetic and copies ran while one was open for 0% of the time, Pallas kernels for 0%

profile of v10, /device:TPU:4, one launch (start us, length us, event | category | flops | bytes accessed | tf_op | source)
XLA Modules:
  0.0 38.2 jit_solution(4117536486403082716)
XLA Ops:
  0.0 0.0 copy-start
  0.0 2.6 %local_plane.1 = (f32[64,8,128]{2,1,0:T(8,128)S(1)}, s32[31,8,128]{2,1,0:T(8,128)S(1)}, s32[20,8,128]{2,1,0:T(8,128)S(1)}, s32[16,8,128]{2,1,0:T(8,128)S(1)}, s3...) custom-call(s32[1]{0:T(128)} %bitcast.q_ref, f32[1,512]{1,0:T(1,128)} %bitcast.6, bf16[2,512,512]{2,1,0:T(8,128)(2,1)} %x_hbm.1), custom_call_target="tpu_custom_call" | custom-call | tf_op jit(solution)/shard_map/local_plane/pallas_call | solution.py:268
  2.6 1.9 %collective-permute-start = (s32[31,8,128]{2,1,0:T(8,128)S(1)}, s32[31,8,128]{2,1,0:T(8,128)S(1)}, u32[]{:S(2)}, u32[]{:S(2)}) collective-permute-start(s32[31,8,128]{2,1,0:T(8,128)S(1)} %get-tuple-element.12), channel_id=1, source_target_pairs={{0,1},{1,2},{2,3},{3,4},{4,5},{5,6},{6,7},{8,9},{9,10},{10,11},{11... | collective-permute-start | bytes 380936 | tf_op jit(solution)/shard_map/ppermute | solution.py:444
  4.5 3.1 %collective-permute-start.1 = (s32[20,8,128]{2,1,0:T(8,128)S(1)}, s32[20,8,128]{2,1,0:T(8,128)S(1)}, u32[]{:S(2)}, u32[]{:S(2)}) collective-permute-start(s32[20,8,128]{2,1,0:T(8,128)S(1)} %get-tuple-element.13), channel_id=1, source_target_pairs={{0,2},{1,3},{2,4},{3,5},{4,6},{5,7},{8,10},{9,11},{10,12},{11,13},... | collective-permute-start | bytes 245768 | tf_op jit(solution)/shard_map/ppermute | solution.py:444
  7.7 1.9 %collective-permute-start.2 = (s32[16,8,128]{2,1,0:T(8,128)S(1)}, s32[16,8,128]{2,1,0:T(8,128)S(1)}, u32[]{:S(2)}, u32[]{:S(2)}) collective-permute-start(s32[16,8,128]{2,1,0:T(8,128)S(1)} %get-tuple-element.14), channel_id=1, source_target_pairs={{0,3},{1,4},{2,5},{3,6},{4,7},{8,11},{9,12},{10,13},{11,14},{12,15... | collective-permute-start | bytes 196616 | tf_op jit(solution)/shard_map/ppermute | solution.py:444
  9.6 1.3 %collective-permute-start.3 = (s32[9,8,128]{2,1,0:T(8,128)S(1)}, s32[9,8,128]{2,1,0:T(8,128)S(1)}, u32[]{:S(2)}, u32[]{:S(2)}) collective-permute-start(s32[9,8,128]{2,1,0:T(8,128)S(1)} %get-tuple-element.15), channel_id=1, source_target_pairs={{0,4},{1,5},{2,6},{3,7},{8,12},{9,13},{10,14},{11,15},{16,20},{17,... | collective-permute-start | bytes 110600 | tf_op jit(solution)/shard_map/ppermute | solution.py:444
  10.9 0.7 %collective-permute-start.4 = (s32[2,8,128]{2,1,0:T(8,128)S(1)}, s32[2,8,128]{2,1,0:T(8,128)S(1)}, u32[]{:S(2)}, u32[]{:S(2)}) collective-permute-start(s32[2,8,128]{2,1,0:T(8,128)S(1)} %get-tuple-element.16), channel_id=1, source_target_pairs={{0,5},{1,6},{2,7}} | collective-permute-start | bytes 24584 | tf_op jit(solution)/shard_map/ppermute | solution.py:444
  11.5 0.0 collective-permute-done.4.r5
  11.6 5.4 %collective-permute-done.3.r4 = s32[9,8,128]{2,1,0:T(8,128)S(1)} collective-permute-done((s32[9,8,128]{2,1,0:T(8,128)S(1)}, s32[9,8,128]{2,1,0:T(8,128)S(1)}, u32[]{:S(2)}, u32[]{:S(2)}) %collective-permute-start.3) | collective-permute-done | bytes 36896 | tf_op jit(solution)/shard_map/ppermute | solution.py:444
  16.9 0.0 collective-permute-done.2.r3
  16.9 0.0 collective-permute-done.1.r2
  16.9 0.0 collective-permute-done.r1
  16.9 0.6 %gather_shifted.1 = s32[320,128]{1,0:T(8,128)S(1)} custom-call(s32[1]{0:T(128)} %bitcast.q_ref, f32[64,8,128]{2,1,0:T(8,128)S(1)} %get-tuple-element.11.o0, s32[31,8,128]{2,1,0:T(8,128)S(1)} %collective-permute-done.r1, s32[20,8,128]{2,1,0:T(8,128)S(1)} %collective-permute-done.1.r2, s32[16,8,128]{2,1,0:T(8,128)S(1)} %collective-permute-done.2.r3, ...), custom_call_target="tpu_custom_call" | custom-call | tf_op jit(solution)/shard_map/gather_shifted/pallas_call | solution.py:334
  17.6 18.1 %all_to_all.5 = s32[32,1,1280]{2,1,0:T(1,128)S(1)} all-to-all(s32[32,1,1280]{2,1,0:T(1,128)S(1)} %bitcast.4), channel_id=1, replica_groups=mesh['chan'=32,'tm'=8] {'chan'}, dimensions={0} | all-to-all | bytes 327680 | tf_op jit(solution)/shard_map/all_to_all | solution.py:454
  35.6 0.0 copy-done
  35.6 2.6 %final_boxcars.1 = f32[2,6,64,512]{3,2,1,0:T(8,128)} custom-call(s32[6]{0:T(128)S(1)} %copy-done, s32[320,128]{1,0:T(8,128)S(1)} %bitcast.5), custom_call_target="tpu_custom_call" | custom-call | tf_op jit(solution)/shard_map/final_boxcars/pallas_call | solution.py:418
Async XLA Ops:
  0.0 35.6 %copy-start = (s32[6]{0:T(128)S(1)}, s32[6]{0:T(128)}, u32[]{:S(2)}) copy-start(s32[6]{0:T(128)} %widths.1) | copy-start | bytes 76
  2.6 14.3 %collective-permute-start = (s32[31,8,128]{2,1,0:T(8,128)S(1)}, s32[31,8,128]{2,1,0:T(8,128)S(1)}, u32[]{:S(2)}, u32[]{:S(2)}) collective-permute-start(s32[31,8,128]{2,1,0:T(8,128)S(1)} %get-tuple-element.12), channel_id=1, source_target_pairs={{0,1},{1,2},{2,3},{3,4},{4,5},{5,6},{6,7},{8,9},{9,10},{10,11},{11... | collective-permute-start | bytes 380936 | tf_op jit(solution)/shard_map/ppermute | solution.py:444
  4.5 12.4 %collective-permute-start.1 = (s32[20,8,128]{2,1,0:T(8,128)S(1)}, s32[20,8,128]{2,1,0:T(8,128)S(1)}, u32[]{:S(2)}, u32[]{:S(2)}) collective-permute-start(s32[20,8,128]{2,1,0:T(8,128)S(1)} %get-tuple-element.13), channel_id=1, source_target_pairs={{0,2},{1,3},{2,4},{3,5},{4,6},{5,7},{8,10},{9,11},{10,12},{11,13},... | collective-permute-start | bytes 245768 | tf_op jit(solution)/shard_map/ppermute | solution.py:444
  7.7 9.3 %collective-permute-start.2 = (s32[16,8,128]{2,1,0:T(8,128)S(1)}, s32[16,8,128]{2,1,0:T(8,128)S(1)}, u32[]{:S(2)}, u32[]{:S(2)}) collective-permute-start(s32[16,8,128]{2,1,0:T(8,128)S(1)} %get-tuple-element.14), channel_id=1, source_target_pairs={{0,3},{1,4},{2,5},{3,6},{4,7},{8,11},{9,12},{10,13},{11,14},{12,15... | collective-permute-start | bytes 196616 | tf_op jit(solution)/shard_map/ppermute | solution.py:444
  9.6 7.4 %collective-permute-start.3 = (s32[9,8,128]{2,1,0:T(8,128)S(1)}, s32[9,8,128]{2,1,0:T(8,128)S(1)}, u32[]{:S(2)}, u32[]{:S(2)}) collective-permute-start(s32[9,8,128]{2,1,0:T(8,128)S(1)} %get-tuple-element.15), channel_id=1, source_target_pairs={{0,4},{1,5},{2,6},{3,7},{8,12},{9,13},{10,14},{11,15},{16,20},{17,... | collective-permute-start | bytes 110600 | tf_op jit(solution)/shard_map/ppermute | solution.py:444
  10.9 0.7 %collective-permute-start.4 = (s32[2,8,128]{2,1,0:T(8,128)S(1)}, s32[2,8,128]{2,1,0:T(8,128)S(1)}, u32[]{:S(2)}, u32[]{:S(2)}) collective-permute-start(s32[2,8,128]{2,1,0:T(8,128)S(1)} %get-tuple-element.16), channel_id=1, source_target_pairs={{0,5},{1,6},{2,7}} | collective-permute-start | bytes 24584 | tf_op jit(solution)/shard_map/ppermute | solution.py:444

commit v11 on v10

--- a/solution.py
+++ b/solution.py
@@ -18,6 +18,7 @@
 REACH = 6
 TILES = 16
 UNITS = 6
+PLACES = UNITS + 4
 PER = SPAN // LANES
 BLOCK = 10
 TOP = 32000.0
@@ -193,6 +194,7 @@
     o4,
     o5,
     free,
+    places,
     scale,
     x,
     one,
@@ -217,14 +219,19 @@
     row = lax.broadcasted_iota(jnp.int32, (ROWS, CHANS), 0)
     col = lax.broadcasted_iota(jnp.int32, (ROWS, CHANS), 1)
     member = (row & 7) * 8 + (row >> 3) == col >> 3
+    first_slots(q, free)
+    for a in range(TILES):
+        slots, _, again = unit_slots(q, a, free)
+        for i, slot in enumerate(slots + [*again[0], *again[1]]):
+            places[a * PLACES + i] = slot
     fetch_scale.wait()
     weights = jnp.where(member, scale[...], 0.0)
     weights = jnp.concatenate(split(weights), axis=0)
     blank = jnp.zeros((8, LANES), jnp.float32)
-    for fetch in fetches:
-        fetch.wait()
     groups = []
     for b in range(BEAMS):
+        fetches[2 * b].wait()
+        fetches[2 * b + 1].wait()
         base = jnp.dot(weights, x[b], preferred_element_type=jnp.float32)
         base = base[:ROWS] + base[ROWS:]
         groups.append(
@@ -234,18 +241,17 @@
             ]
         )
     merge_rows(groups, one, two, WIDE // LANES)
-    first_slots(q, free)
     odd = lax.broadcasted_iota(jnp.int32, (8, UNITS * LANES), 0) & 2 != 0
     for a in range(TILES):
         rows = [take(two.at[b], 4 * a, 4, 0, WIDE // LANES) for b in range(BEAMS)]
         rows = jnp.concatenate([jnp.concatenate(rows, axis=0), blank], axis=1)
         rows = jnp.where(odd, pltpu.roll(rows, 2 * q, 1), rows)
         rows = pltpu.roll(rows, (4 * q * a) & (LANES - 1), 1)
-        slots, _, again = unit_slots(q, a, free)
-        for i, slot in enumerate(slots):
-            packed[slot] = rows[:, i * LANES : (i + 1) * LANES]
-        for slot, origin in again:
-            packed[slot] = packed[origin]
+        place = a * PLACES
+        for i in range(UNITS):
+            packed[places[place + i]] = rows[:, i * LANES : (i + 1) * LANES]
+        for i in (UNITS, UNITS + 2):
+            packed[places[place + i]] = packed[places[place + i + 1]]
     o0[...] = packed[pl.ds(0, SIZES[0])]
     tiles = [
         two[b, c, pl.ds(8 * a, 8), :]
@@ -276,6 +282,7 @@
         + [jax.ShapeDtypeStruct((n // 2 + 1, 8, LANES), jnp.int32) for n in SIZES[1:]],
         scratch_shapes=[
             pltpu.SMEM((REACH + 2,), jnp.int32),
+            pltpu.SMEM((TILES * PLACES,), jnp.int32),
             pltpu.VMEM((1, CHANS), jnp.float32),
             pltpu.VMEM((BEAMS, CHANS, SPAN), jnp.bfloat16),
             pltpu.VMEM((BEAMS, WIDE // LANES, ROWS, LANES), jnp.float32),
@@ -361,55 +368,59 @@
     return beams
 
 
-def boxcar_bands(widths):
+def boxcar_bands(widths, places):
     u = lax.broadcasted_iota(jnp.int32, (2 * LANES, LANES), 0)
     t = lax.broadcasted_iota(jnp.int32, (2 * LANES, LANES), 1)
     ago = t + LANES - u
     bands = []
-    for k in range(NBOX):
+    for k in places:
         inside = jnp.logical_and(ago >= 0, ago < widths[k])
         bands.append(jnp.where(inside, 1.0, 0.0).astype(jnp.bfloat16))
     return jnp.concatenate(bands, axis=1)
 
 
-def boxcar_norms(widths):
-    norms = []
-    for k in range(NBOX):
-        square = jnp.full((1, LANES), widths[k] * (CHANS * PARTS), jnp.int32)
-        norms.append(lax.rsqrt(square.astype(jnp.float32)))
-    return jnp.concatenate(norms, axis=1)
-
-
-def boxcar_tile(before, here, bands, norms, held, c):
-    window = jnp.concatenate([before, here], axis=1)
-    sums = jnp.dot(window, bands, preferred_element_type=jnp.float32)
-    rows = BEAMS * ROWS
-    sums = (sums[:rows] + sums[rows:]) * norms
-    for b in range(BEAMS):
-        for k in range(NBOX):
-            held[b, k, :, pl.ds(c * LANES, LANES)] = sums[
-                b * ROWS : (b + 1) * ROWS, k * LANES : (k + 1) * LANES
-            ]
+def boxcar_norm(width):
+    square = jnp.full((1, LANES), width * (CHANS * PARTS), jnp.int32)
+    return lax.rsqrt(square.astype(jnp.float32))
 
 
 def final_kernel(widths, x_ref, out, one, two, held, sems):
     merge_rows(final_groups(x_ref), one, two, WIDE // LANES)
-    bands = boxcar_bands(widths)
-    norms = boxcar_norms(widths)
+    rows = BEAMS * ROWS
+    copies = []
+
+    def send(k):
+        copies.append(pltpu.make_async_copy(held.at[:, k], out.at[:, k], sems.at[k]))
+        copies[-1].start()
+
+    norm = boxcar_norm(widths[0])
+    for b in range(BEAMS):
+        for c in range(PER):
+            held[b, 0, :, pl.ds(c * LANES, LANES)] = two[b, c + 1] * norm
+    send(0)
     parts = []
     for c in range(WIDE // LANES):
         tile = jnp.concatenate([two[b, c] for b in range(BEAMS)], axis=0)
-        parts.append(jnp.concatenate(split(tile), axis=0))
-    copies = []
-    for c in range(PER):
-        boxcar_tile(parts[c], parts[c + 1], bands, norms, held, c)
-        lanes = pl.ds(c * LANES, LANES)
-        copies.append(
-            pltpu.make_async_copy(
-                held.at[:, :, :, lanes], out.at[:, :, :, lanes], sems.at[c]
-            )
-        )
-        copies[-1].start()
+        parts.append(split(tile))
+    windows = [
+        jnp.concatenate([before[0], here[0], before[1], here[1]], axis=1)
+        for before, here in zip(parts, parts[1:])
+    ]
+    windows = jnp.concatenate(windows, axis=0)
+    for places in ((1, 2), (3, 4), (5,)):
+        bands = boxcar_bands(widths, places)
+        bands = jnp.concatenate([bands, bands], axis=0)
+        sums = jnp.dot(windows, bands, preferred_element_type=jnp.float32)
+        for i, k in enumerate(places):
+            norm = boxcar_norm(widths[k])
+            for c in range(PER):
+                term = sums[rows * c : rows * (c + 1), i * LANES : (i + 1) * LANES]
+                term = term * norm
+                for b in range(BEAMS):
+                    held[b, k, :, pl.ds(c * LANES, LANES)] = term[
+                        b * ROWS : (b + 1) * ROWS
+                    ]
+            send(k)
     for copy in copies:
         copy.wait()
 
@@ -427,7 +438,7 @@
             pltpu.VMEM((BEAMS, WIDE // LANES, ROWS, LANES), jnp.float32),
             pltpu.VMEM((BEAMS, WIDE // LANES, ROWS, LANES), jnp.float32),
             pltpu.VMEM((BEAMS, NBOX, ROWS, SPAN), jnp.float32),
-            pltpu.SemaphoreType.DMA((PER,)),
+            pltpu.SemaphoreType.DMA((NBOX,)),
         ],
         compiler_params=pltpu.CompilerParams(vmem_limit_bytes=24 << 20),
         name="final_boxcars",

time: 38.4 us -> 38.5 us (level)
  no operation moved by 1% of the time
where the time goes in v11:
time: 38.5 us; the launch traced here: 38.2 us
  blocking collectives  18.1 us (47%)
  starting transfers between devices  8.9 us (23%)
  Pallas kernels  5.82 us (15%)
  waiting for transfers between devices  5.39 us (14%)
    all_to_all x1, blocking collectives, per_device(): lined = lax.all_to_all(lined, 'chan', 0, 0, tiled=True)  18.1 us
    ppermute x5, starting transfers between devices, later(): return lax.ppermute(block, ('chan', 'tm'), route)  8.9 us
    ppermute x5, waiting for transfers between devices, later(): return lax.ppermute(block, ('chan', 'tm'), route)  5.39 us
    pallas_call x1, Pallas kernels, local_plane(): pl.pallas_call(local_kernel, in_specs=[pl.BlockSpec(memory_space=pltpu.SM...  2.61 us
    pallas_call x1, Pallas kernels, final_boxcars(): pl.pallas_call(final_kernel, in_specs=[pl.BlockSpec(memory_space=pltpu.SM...  2.61 us
  transfers between devices with their start and end apart: 5, of which 1 were waited for; matrix products, arithmetic and copies ran while one was open for 0% of the time, Pallas kernels for 0%

profile of v11, /device:TPU:4, one launch (start us, length us, event | category | flops | bytes accessed | tf_op | source)
XLA Modules:
  0.0 38.2 jit_solution(10485745852645633825)
XLA Ops:
  0.0 0.0 copy-start
  0.0 2.6 %local_plane.1 = (f32[64,8,128]{2,1,0:T(8,128)S(1)}, s32[31,8,128]{2,1,0:T(8,128)S(1)}, s32[20,8,128]{2,1,0:T(8,128)S(1)}, s32[16,8,128]{2,1,0:T(8,128)S(1)}, s3...) custom-call(s32[1]{0:T(128)} %bitcast.q_ref, f32[1,512]{1,0:T(1,128)} %bitcast.6, bf16[2,512,512]{2,1,0:T(8,128)(2,1)} %x_hbm.1), custom_call_target="tpu_custom_call" | custom-call | tf_op jit(solution)/shard_map/local_plane/pallas_call | solution.py:274
  2.6 1.9 %collective-permute-start = (s32[31,8,128]{2,1,0:T(8,128)S(1)}, s32[31,8,128]{2,1,0:T(8,128)S(1)}, u32[]{:S(2)}, u32[]{:S(2)}) collective-permute-start(s32[31,8,128]{2,1,0:T(8,128)S(1)} %get-tuple-element.12), channel_id=1, source_target_pairs={{0,1},{1,2},{2,3},{3,4},{4,5},{5,6},{6,7},{8,9},{9,10},{10,11},{11... | collective-permute-start | bytes 380936 | tf_op jit(solution)/shard_map/ppermute | solution.py:455
  4.6 3.1 %collective-permute-start.1 = (s32[20,8,128]{2,1,0:T(8,128)S(1)}, s32[20,8,128]{2,1,0:T(8,128)S(1)}, u32[]{:S(2)}, u32[]{:S(2)}) collective-permute-start(s32[20,8,128]{2,1,0:T(8,128)S(1)} %get-tuple-element.13), channel_id=1, source_target_pairs={{0,2},{1,3},{2,4},{3,5},{4,6},{5,7},{8,10},{9,11},{10,12},{11,13},... | collective-permute-start | bytes 245768 | tf_op jit(solution)/shard_map/ppermute | solution.py:455
  7.7 1.9 %collective-permute-start.2 = (s32[16,8,128]{2,1,0:T(8,128)S(1)}, s32[16,8,128]{2,1,0:T(8,128)S(1)}, u32[]{:S(2)}, u32[]{:S(2)}) collective-permute-start(s32[16,8,128]{2,1,0:T(8,128)S(1)} %get-tuple-element.14), channel_id=1, source_target_pairs={{0,3},{1,4},{2,5},{3,6},{4,7},{8,11},{9,12},{10,13},{11,14},{12,15... | collective-permute-start | bytes 196616 | tf_op jit(solution)/shard_map/ppermute | solution.py:455
  9.6 1.3 %collective-permute-start.3 = (s32[9,8,128]{2,1,0:T(8,128)S(1)}, s32[9,8,128]{2,1,0:T(8,128)S(1)}, u32[]{:S(2)}, u32[]{:S(2)}) collective-permute-start(s32[9,8,128]{2,1,0:T(8,128)S(1)} %get-tuple-element.15), channel_id=1, source_target_pairs={{0,4},{1,5},{2,6},{3,7},{8,12},{9,13},{10,14},{11,15},{16,20},{17,... | collective-permute-start | bytes 110600 | tf_op jit(solution)/shard_map/ppermute | solution.py:455
  10.9 0.7 %collective-permute-start.4 = (s32[2,8,128]{2,1,0:T(8,128)S(1)}, s32[2,8,128]{2,1,0:T(8,128)S(1)}, u32[]{:S(2)}, u32[]{:S(2)}) collective-permute-start(s32[2,8,128]{2,1,0:T(8,128)S(1)} %get-tuple-element.16), channel_id=1, source_target_pairs={{0,5},{1,6},{2,7}} | collective-permute-start | bytes 24584 | tf_op jit(solution)/shard_map/ppermute | solution.py:455
  11.6 0.0 collective-permute-done.4.r5
  11.6 5.4 %collective-permute-done.3.r4 = s32[9,8,128]{2,1,0:T(8,128)S(1)} collective-permute-done((s32[9,8,128]{2,1,0:T(8,128)S(1)}, s32[9,8,128]{2,1,0:T(8,128)S(1)}, u32[]{:S(2)}, u32[]{:S(2)}) %collective-permute-start.3) | collective-permute-done | bytes 36896 | tf_op jit(solution)/shard_map/ppermute | solution.py:455
  16.9 0.0 collective-permute-done.2.r3
  16.9 0.0 collective-permute-done.1.r2
  17.0 0.0 collective-permute-done.r1
  17.0 0.6 %gather_shifted.1 = s32[320,128]{1,0:T(8,128)S(1)} custom-call(s32[1]{0:T(128)} %bitcast.q_ref, f32[64,8,128]{2,1,0:T(8,128)S(1)} %get-tuple-element.11.o0, s32[31,8,128]{2,1,0:T(8,128)S(1)} %collective-permute-done.r1, s32[20,8,128]{2,1,0:T(8,128)S(1)} %collective-permute-done.1.r2, s32[16,8,128]{2,1,0:T(8,128)S(1)} %collective-permute-done.2.r3, ...), custom_call_target="tpu_custom_call" | custom-call | tf_op jit(solution)/shard_map/gather_shifted/pallas_call | solution.py:341
  17.6 18.1 %all_to_all.5 = s32[32,1,1280]{2,1,0:T(1,128)S(1)} all-to-all(s32[32,1,1280]{2,1,0:T(1,128)S(1)} %bitcast.4), channel_id=1, replica_groups=mesh['chan'=32,'tm'=8] {'chan'}, dimensions={0} | all-to-all | bytes 327680 | tf_op jit(solution)/shard_map/all_to_all | solution.py:465
  35.6 0.0 copy-done
  35.6 2.6 %final_boxcars.1 = f32[2,6,64,512]{3,2,1,0:T(8,128)} custom-call(s32[6]{0:T(128)S(1)} %copy-done, s32[320,128]{1,0:T(8,128)S(1)} %bitcast.5), custom_call_target="tpu_custom_call" | custom-call | tf_op jit(solution)/shard_map/final_boxcars/pallas_call | solution.py:429
Async XLA Ops:
  0.0 35.6 %copy-start = (s32[6]{0:T(128)S(1)}, s32[6]{0:T(128)}, u32[]{:S(2)}) copy-start(s32[6]{0:T(128)} %widths.1) | copy-start | bytes 76
  2.6 14.3 %collective-permute-start = (s32[31,8,128]{2,1,0:T(8,128)S(1)}, s32[31,8,128]{2,1,0:T(8,128)S(1)}, u32[]{:S(2)}, u32[]{:S(2)}) collective-permute-start(s32[31,8,128]{2,1,0:T(8,128)S(1)} %get-tuple-element.12), channel_id=1, source_target_pairs={{0,1},{1,2},{2,3},{3,4},{4,5},{5,6},{6,7},{8,9},{9,10},{10,11},{11... | collective-permute-start | bytes 380936 | tf_op jit(solution)/shard_map/ppermute | solution.py:455
  4.6 12.4 %collective-permute-start.1 = (s32[20,8,128]{2,1,0:T(8,128)S(1)}, s32[20,8,128]{2,1,0:T(8,128)S(1)}, u32[]{:S(2)}, u32[]{:S(2)}) collective-permute-start(s32[20,8,128]{2,1,0:T(8,128)S(1)} %get-tuple-element.13), channel_id=1, source_target_pairs={{0,2},{1,3},{2,4},{3,5},{4,6},{5,7},{8,10},{9,11},{10,12},{11,13},... | collective-permute-start | bytes 245768 | tf_op jit(solution)/shard_map/ppermute | solution.py:455
  7.7 9.3 %collective-permute-start.2 = (s32[16,8,128]{2,1,0:T(8,128)S(1)}, s32[16,8,128]{2,1,0:T(8,128)S(1)}, u32[]{:S(2)}, u32[]{:S(2)}) collective-permute-start(s32[16,8,128]{2,1,0:T(8,128)S(1)} %get-tuple-element.14), channel_id=1, source_target_pairs={{0,3},{1,4},{2,5},{3,6},{4,7},{8,11},{9,12},{10,13},{11,14},{12,15... | collective-permute-start | bytes 196616 | tf_op jit(solution)/shard_map/ppermute | solution.py:455
  9.6 7.4 %collective-permute-start.3 = (s32[9,8,128]{2,1,0:T(8,128)S(1)}, s32[9,8,128]{2,1,0:T(8,128)S(1)}, u32[]{:S(2)}, u32[]{:S(2)}) collective-permute-start(s32[9,8,128]{2,1,0:T(8,128)S(1)} %get-tuple-element.15), channel_id=1, source_target_pairs={{0,4},{1,5},{2,6},{3,7},{8,12},{9,13},{10,14},{11,15},{16,20},{17,... | collective-permute-start | bytes 110600 | tf_op jit(solution)/shard_map/ppermute | solution.py:455
  10.9 0.7 %collective-permute-start.4 = (s32[2,8,128]{2,1,0:T(8,128)S(1)}, s32[2,8,128]{2,1,0:T(8,128)S(1)}, u32[]{:S(2)}, u32[]{:S(2)}) collective-permute-start(s32[2,8,128]{2,1,0:T(8,128)S(1)} %get-tuple-element.16), channel_id=1, source_target_pairs={{0,5},{1,6},{2,7}} | collective-permute-start | bytes 24584 | tf_op jit(solution)/shard_map/ppermute | solution.py:455

commit v12 on v11

--- a/solution.py
+++ b/solution.py
@@ -184,7 +184,6 @@
 
 
 def local_kernel(
-    q_ref,
     scale_hbm,
     x_hbm,
     o0,
@@ -203,7 +202,7 @@
     sems,
 ):
     half = CHANS // 2
-    q = q_ref[0]
+    q = PARTS - 1 - lax.axis_index("chan")
     fetch_scale = pltpu.make_async_copy(scale_hbm, scale, sems.at[2 * BEAMS])
     fetch_scale.start()
     fetches = []
@@ -270,11 +269,10 @@
         out[words] = exponent
 
 
-def local_plane(x, scale, q):
+def local_plane(x, scale):
     return pl.pallas_call(
         local_kernel,
         in_specs=[
-            pl.BlockSpec(memory_space=pltpu.SMEM),
             pl.BlockSpec(memory_space=pltpu.HBM),
             pl.BlockSpec(memory_space=pltpu.HBM),
         ],
@@ -293,14 +291,13 @@
         compiler_params=pltpu.CompilerParams(vmem_limit_bytes=24 << 20),
         name="local_plane",
     )(
-        q,
         pltpu.with_memory_space_constraint(scale, pltpu.HBM),
         pltpu.with_memory_space_constraint(x, pltpu.HBM),
     )
 
 
-def gather_kernel(q_ref, o0, r1, r2, r3, r4, r5, out, free, packed, held):
-    q = q_ref[0]
+def gather_kernel(o0, r1, r2, r3, r4, r5, out, free, packed, held):
+    q = PARTS - 1 - lax.axis_index("chan")
     first_slots(q, free)
     packed[pl.ds(0, SIZES[0])] = o0[...]
     for k, piece in enumerate((r1, r2, r3, r4, r5), 1):
@@ -336,11 +333,11 @@
             out[rows, :] = word
 
 
-def gather_shifted(pieces, q):
+def gather_shifted(pieces):
     vmem = pl.BlockSpec(memory_space=pltpu.VMEM)
     return pl.pallas_call(
         gather_kernel,
-        in_specs=[pl.BlockSpec(memory_space=pltpu.SMEM)] + [vmem] * REACH,
+        in_specs=[vmem] * REACH,
         out_shape=jax.ShapeDtypeStruct((PARTS * BLOCK, LANES), jnp.int32),
         scratch_shapes=[
             pltpu.SMEM((REACH + 2,), jnp.int32),
@@ -349,7 +346,7 @@
         ],
         compiler_params=pltpu.CompilerParams(vmem_limit_bytes=24 << 20),
         name="gather_shifted",
-    )(q, *pieces)
+    )(*pieces)
 
 
 def final_groups(x_ref):
@@ -374,14 +371,13 @@
     ago = t + LANES - u
     bands = []
     for k in places:
-        inside = jnp.logical_and(ago >= 0, ago < widths[k])
+        inside = jnp.logical_and(ago >= 0, ago < widths[:, k : k + 1])
         bands.append(jnp.where(inside, 1.0, 0.0).astype(jnp.bfloat16))
     return jnp.concatenate(bands, axis=1)
 
 
 def boxcar_norm(width):
-    square = jnp.full((1, LANES), width * (CHANS * PARTS), jnp.int32)
-    return lax.rsqrt(square.astype(jnp.float32))
+    return lax.rsqrt((width * (CHANS * PARTS)).astype(jnp.float32))
 
 
 def final_kernel(widths, x_ref, out, one, two, held, sems):
@@ -393,7 +389,7 @@
         copies.append(pltpu.make_async_copy(held.at[:, k], out.at[:, k], sems.at[k]))
         copies[-1].start()
 
-    norm = boxcar_norm(widths[0])
+    norm = boxcar_norm(widths[:, :1])
     for b in range(BEAMS):
         for c in range(PER):
             held[b, 0, :, pl.ds(c * LANES, LANES)] = two[b, c + 1] * norm
@@ -412,7 +408,7 @@
         bands = jnp.concatenate([bands, bands], axis=0)
         sums = jnp.dot(windows, bands, preferred_element_type=jnp.float32)
         for i, k in enumerate(places):
-            norm = boxcar_norm(widths[k])
+            norm = boxcar_norm(widths[:, k : k + 1])
             for c in range(PER):
                 term = sums[rows * c : rows * (c + 1), i * LANES : (i + 1) * LANES]
                 term = term * norm
@@ -428,10 +424,7 @@
 def final_boxcars(x, widths):
     return pl.pallas_call(
         final_kernel,
-        in_specs=[
-            pl.BlockSpec(memory_space=pltpu.SMEM),
-            pl.BlockSpec(memory_space=pltpu.VMEM),
-        ],
+        in_specs=[pl.BlockSpec(memory_space=pltpu.VMEM)] * 2,
         out_specs=pl.BlockSpec(memory_space=pltpu.HBM),
         out_shape=jax.ShapeDtypeStruct((BEAMS, NBOX, ROWS, SPAN), jnp.float32),
         scratch_shapes=[
@@ -442,7 +435,7 @@
         ],
         compiler_params=pltpu.CompilerParams(vmem_limit_bytes=24 << 20),
         name="final_boxcars",
-    )(widths, x)
+    )(widths.reshape(1, NBOX), x)
 
 
 def later(block, distances):
@@ -456,11 +449,10 @@
 
 
 def per_device(intensity, channel_scale, box_widths):
-    q = (PARTS - 1 - lax.axis_index("chan")).astype(jnp.int32).reshape(1)
-    pieces = list(local_plane(intensity, channel_scale.reshape(1, CHANS), q))
+    pieces = list(local_plane(intensity, channel_scale.reshape(1, CHANS)))
     for k in range(REACH - 1, 0, -1):
         pieces[k] = later(pieces[k], DISTANCES[::-1, k].tolist())
-    lined = gather_shifted(pieces, q)
+    lined = gather_shifted(pieces)
     lined = lined.reshape(PARTS, 1, BLOCK * LANES)
     lined = lax.all_to_all(lined, "chan", 0, 0, tiled=True)
     lined = lined.reshape(PARTS * BLOCK, LANES)

time: 38.5 us -> 37.9 us (0.984)
  Pallas kernels: 5.82 us -> 5.3 us
    pallas_call x3, Pallas kernels: 5.82 us -> 5.3 us  [the longest x1 2.61 us: local_plane(): pl.pallas_call(local_kernel, in_specs=[pl.BlockSpec(memory_space=pltpu.HB...]
where the time goes in v12:
time: 37.9 us; the launch traced here: 37.7 us
  blocking collectives  18.1 us (48%)
  starting transfers between devices  8.9 us (23%)
  waiting for transfers between devices  5.39 us (14%)
  Pallas kernels  5.3 us (14%)
    all_to_all x1, blocking collectives, per_device(): lined = lax.all_to_all(lined, 'chan', 0, 0, tiled=True)  18.1 us
    ppermute x5, starting transfers between devices, later(): return lax.ppermute(block, ('chan', 'tm'), route)  8.9 us
    ppermute x5, waiting for transfers between devices, later(): return lax.ppermute(block, ('chan', 'tm'), route)  5.39 us
    pallas_call x1, Pallas kernels, local_plane(): pl.pallas_call(local_kernel, in_specs=[pl.BlockSpec(memory_space=pltpu.HB...  2.61 us
    pallas_call x1, Pallas kernels, final_boxcars(): pl.pallas_call(final_kernel, in_specs=[pl.BlockSpec(memory_space=pltpu.VM...  2.1 us
  transfers between devices with their start and end apart: 5, of which 1 were waited for; matrix products, arithmetic and copies ran while one was open for 0% of the time, Pallas kernels for 0%

profile of v12, /device:TPU:4, one launch (start us, length us, event | category | flops | bytes accessed | tf_op | source)
XLA Modules:
  0.0 37.7 jit_solution(18020494954615266803)
XLA Ops:
  0.0 0.0 copy-start
  0.0 2.6 %local_plane.1 = (f32[64,8,128]{2,1,0:T(8,128)S(1)}, s32[31,8,128]{2,1,0:T(8,128)S(1)}, s32[20,8,128]{2,1,0:T(8,128)S(1)}, s32[16,8,128]{2,1,0:T(8,128)S(1)}, s3...) custom-call(f32[1,512]{1,0:T(1,128)} %bitcast.7, bf16[2,512,512]{2,1,0:T(8,128)(2,1)} %x_hbm.1), custom_call_target="tpu_custom_call" | custom-call | tf_op jit(solution)/shard_map/local_plane/pallas_call | solution.py:273
  2.6 1.9 %collective-permute-start = (s32[31,8,128]{2,1,0:T(8,128)S(1)}, s32[31,8,128]{2,1,0:T(8,128)S(1)}, u32[]{:S(2)}, u32[]{:S(2)}) collective-permute-start(s32[31,8,128]{2,1,0:T(8,128)S(1)} %get-tuple-element.12), channel_id=1, source_target_pairs={{0,1},{1,2},{2,3},{3,4},{4,5},{5,6},{6,7},{8,9},{9,10},{10,11},{11... | collective-permute-start | bytes 380936 | tf_op jit(solution)/shard_map/ppermute | solution.py:448
  4.6 3.1 %collective-permute-start.1 = (s32[20,8,128]{2,1,0:T(8,128)S(1)}, s32[20,8,128]{2,1,0:T(8,128)S(1)}, u32[]{:S(2)}, u32[]{:S(2)}) collective-permute-start(s32[20,8,128]{2,1,0:T(8,128)S(1)} %get-tuple-element.13), channel_id=1, source_target_pairs={{0,2},{1,3},{2,4},{3,5},{4,6},{5,7},{8,10},{9,11},{10,12},{11,13},... | collective-permute-start | bytes 245768 | tf_op jit(solution)/shard_map/ppermute | solution.py:448
  7.7 1.9 %collective-permute-start.2 = (s32[16,8,128]{2,1,0:T(8,128)S(1)}, s32[16,8,128]{2,1,0:T(8,128)S(1)}, u32[]{:S(2)}, u32[]{:S(2)}) collective-permute-start(s32[16,8,128]{2,1,0:T(8,128)S(1)} %get-tuple-element.14), channel_id=1, source_target_pairs={{0,3},{1,4},{2,5},{3,6},{4,7},{8,11},{9,12},{10,13},{11,14},{12,15... | collective-permute-start | bytes 196616 | tf_op jit(solution)/shard_map/ppermute | solution.py:448
  9.6 1.3 %collective-permute-start.3 = (s32[9,8,128]{2,1,0:T(8,128)S(1)}, s32[9,8,128]{2,1,0:T(8,128)S(1)}, u32[]{:S(2)}, u32[]{:S(2)}) collective-permute-start(s32[9,8,128]{2,1,0:T(8,128)S(1)} %get-tuple-element.15), channel_id=1, source_target_pairs={{0,4},{1,5},{2,6},{3,7},{8,12},{9,13},{10,14},{11,15},{16,20},{17,... | collective-permute-start | bytes 110600 | tf_op jit(solution)/shard_map/ppermute | solution.py:448
  10.9 0.7 %collective-permute-start.4 = (s32[2,8,128]{2,1,0:T(8,128)S(1)}, s32[2,8,128]{2,1,0:T(8,128)S(1)}, u32[]{:S(2)}, u32[]{:S(2)}) collective-permute-start(s32[2,8,128]{2,1,0:T(8,128)S(1)} %get-tuple-element.16), channel_id=1, source_target_pairs={{0,5},{1,6},{2,7}} | collective-permute-start | bytes 24584 | tf_op jit(solution)/shard_map/ppermute | solution.py:448
  11.6 0.0 collective-permute-done.4.r5
  11.6 5.4 %collective-permute-done.3.r4 = s32[9,8,128]{2,1,0:T(8,128)S(1)} collective-permute-done((s32[9,8,128]{2,1,0:T(8,128)S(1)}, s32[9,8,128]{2,1,0:T(8,128)S(1)}, u32[]{:S(2)}, u32[]{:S(2)}) %collective-permute-start.3) | collective-permute-done | bytes 36896 | tf_op jit(solution)/shard_map/ppermute | solution.py:448
  16.9 0.0 collective-permute-done.2.r3
  16.9 0.0 collective-permute-done.1.r2
  17.0 0.0 collective-permute-done.r1
  17.0 0.6 %gather_shifted.1 = s32[320,128]{1,0:T(8,128)S(1)} custom-call(f32[64,8,128]{2,1,0:T(8,128)S(1)} %get-tuple-element.11.o0, s32[31,8,128]{2,1,0:T(8,128)S(1)} %collective-permute-done.r1, s32[20,8,128]{2,1,0:T(8,128)S(1)} %collective-permute-done.1.r2, s32[16,8,128]{2,1,0:T(8,128)S(1)} %collective-permute-done.2.r3, ...), custom_call_target="tpu_custom_call" | custom-call | tf_op jit(solution)/shard_map/gather_shifted/pallas_call | solution.py:338
  17.6 18.1 %all_to_all.5 = s32[32,1,1280]{2,1,0:T(1,128)S(1)} all-to-all(s32[32,1,1280]{2,1,0:T(1,128)S(1)} %bitcast.5), channel_id=1, replica_groups=mesh['chan'=32,'tm'=8] {'chan'}, dimensions={0} | all-to-all | bytes 327680 | tf_op jit(solution)/shard_map/all_to_all | solution.py:457
  35.6 0.0 copy-done
  35.6 2.1 %final_boxcars.1 = f32[2,6,64,512]{3,2,1,0:T(8,128)} custom-call(s32[1,6]{1,0:T(1,128)S(1)} %bitcast.6, s32[320,128]{1,0:T(8,128)S(1)} %bitcast.4), custom_call_target="tpu_custom_call" | custom-call | tf_op jit(solution)/shard_map/final_boxcars/pallas_call | solution.py:425
Async XLA Ops:
  0.0 35.6 %copy-start = (s32[6]{0:T(128)S(1)}, s32[6]{0:T(128)}, u32[]{:S(2)}) copy-start(s32[6]{0:T(128)} %param.5) | copy-start | bytes 76
  2.6 14.3 %collective-permute-start = (s32[31,8,128]{2,1,0:T(8,128)S(1)}, s32[31,8,128]{2,1,0:T(8,128)S(1)}, u32[]{:S(2)}, u32[]{:S(2)}) collective-permute-start(s32[31,8,128]{2,1,0:T(8,128)S(1)} %get-tuple-element.12), channel_id=1, source_target_pairs={{0,1},{1,2},{2,3},{3,4},{4,5},{5,6},{6,7},{8,9},{9,10},{10,11},{11... | collective-permute-start | bytes 380936 | tf_op jit(solution)/shard_map/ppermute | solution.py:448
  4.6 12.4 %collective-permute-start.1 = (s32[20,8,128]{2,1,0:T(8,128)S(1)}, s32[20,8,128]{2,1,0:T(8,128)S(1)}, u32[]{:S(2)}, u32[]{:S(2)}) collective-permute-start(s32[20,8,128]{2,1,0:T(8,128)S(1)} %get-tuple-element.13), channel_id=1, source_target_pairs={{0,2},{1,3},{2,4},{3,5},{4,6},{5,7},{8,10},{9,11},{10,12},{11,13},... | collective-permute-start | bytes 245768 | tf_op jit(solution)/shard_map/ppermute | solution.py:448
  7.7 9.3 %collective-permute-start.2 = (s32[16,8,128]{2,1,0:T(8,128)S(1)}, s32[16,8,128]{2,1,0:T(8,128)S(1)}, u32[]{:S(2)}, u32[]{:S(2)}) collective-permute-start(s32[16,8,128]{2,1,0:T(8,128)S(1)} %get-tuple-element.14), channel_id=1, source_target_pairs={{0,3},{1,4},{2,5},{3,6},{4,7},{8,11},{9,12},{10,13},{11,14},{12,15... | collective-permute-start | bytes 196616 | tf_op jit(solution)/shard_map/ppermute | solution.py:448
  9.6 7.4 %collective-permute-start.3 = (s32[9,8,128]{2,1,0:T(8,128)S(1)}, s32[9,8,128]{2,1,0:T(8,128)S(1)}, u32[]{:S(2)}, u32[]{:S(2)}) collective-permute-start(s32[9,8,128]{2,1,0:T(8,128)S(1)} %get-tuple-element.15), channel_id=1, source_target_pairs={{0,4},{1,5},{2,6},{3,7},{8,12},{9,13},{10,14},{11,15},{16,20},{17,... | collective-permute-start | bytes 110600 | tf_op jit(solution)/shard_map/ppermute | solution.py:448
  10.9 0.7 %collective-permute-start.4 = (s32[2,8,128]{2,1,0:T(8,128)S(1)}, s32[2,8,128]{2,1,0:T(8,128)S(1)}, u32[]{:S(2)}, u32[]{:S(2)}) collective-permute-start(s32[2,8,128]{2,1,0:T(8,128)S(1)} %get-tuple-element.16), channel_id=1, source_target_pairs={{0,5},{1,6},{2,7}} | collective-permute-start | bytes 24584 | tf_op jit(solution)/shard_map/ppermute | solution.py:448

commit v13 on v12

--- a/solution.py
+++ b/solution.py
@@ -20,6 +20,7 @@
 UNITS = 6
 PLACES = UNITS + 4
 PER = SPAN // LANES
+FRONT = PER
 BLOCK = 10
 TOP = 32000.0
 
@@ -63,7 +64,7 @@
         taken = {0}
         for k in range(REACH - 1, 0, -1):
             if counts[q, k]:
-                allowed = (k,) if q >= 22 else (4, 2, 1)
+                allowed = (k,) if q >= 22 or k == 3 else (4, 2, 1)
                 fits = [i for i in allowed if i not in taken and sizes[i] >= counts[q, k]]
                 buffers[q, k] = fits[0]
                 distances[q, fits[0]] = k
@@ -298,27 +299,34 @@
 
 def gather_kernel(o0, r1, r2, r3, r4, r5, out, free, packed, held):
     q = PARTS - 1 - lax.axis_index("chan")
+    tiles = WIDE // LANES
     first_slots(q, free)
-    packed[pl.ds(0, SIZES[0])] = o0[...]
+    packed[pl.ds(FRONT, SIZES[0])] = o0[...]
     for k, piece in enumerate((r1, r2, r3, r4, r5), 1):
         words = SIZES[k] // 2
         step = span_of(piece[words]) * (1.0 / TOP)
         for t in range(words):
-            slot = STARTS[k] + 2 * t
+            slot = FRONT + STARTS[k] + 2 * t
             packed[slot], packed[slot + 1] = unpair(piece[t], step)
-    packed[SPARE] = jnp.zeros((8, LANES), jnp.float32)
+    top = jnp.zeros((8, LANES), jnp.float32)
     for a in range(TILES):
-        slots, at, again = unit_slots(q, a, free)
-        rows = pl.ds(8 * a, 8)
-        tiles = [1 + ((at + i) & (PER - 1)) for i in range(PER)]
-        held[0, rows, :] = packed[again[0][0]] + packed[again[1][0]]
-        held[tiles[0], rows, :] = packed[slots[0]] + packed[slots[PER]]
-        held[tiles[1], rows, :] = packed[slots[1]] + packed[slots[PER + 1]]
-        held[tiles[2], rows, :] = packed[slots[2]]
-        held[tiles[3], rows, :] = packed[slots[3]]
-    tiles = WIDE // LANES
-    values = [held[c, pl.ds(8 * a, 8), :] for c in range(tiles) for a in range(TILES)]
-    exponent = exponent_of(largest_of(values))
+        k, at, _, _, (here, then, over) = group_shares(q, a, jnp.minimum)
+        p0, p1, p2 = free[k], free[k + 1], free[k + 2]
+        free[k] = p0 + here
+        free[k + 1] = p1 + then
+        free[k + 2] = p2 + over
+        end = packed[pl.ds(FRONT + p0 - at, PER)]
+        begin = packed[pl.ds(FRONT + p1, tiles)]
+        more = packed[pl.ds(FRONT + p2, 2)]
+        for c in range(tiles):
+            tile = jnp.where(c < then, begin[c], 0.0)
+            if c > 0:
+                tile = tile + jnp.where(c > at, end[c - 1], 0.0)
+            if c < 2:
+                tile = tile + jnp.where(c < over, more[c], 0.0)
+            held[c, pl.ds(8 * a, 8), :] = tile
+            top = jnp.maximum(top, jnp.abs(tile))
+    exponent = exponent_of(largest_of([top]))
     inverse = 1.0 / span_of(exponent)[:1]
     exponent = jnp.broadcast_to(exponent[:1], (TILES, LANES))
     lane = lax.broadcasted_iota(jnp.int32, (TILES, LANES), 1)
@@ -341,7 +349,7 @@
         out_shape=jax.ShapeDtypeStruct((PARTS * BLOCK, LANES), jnp.int32),
         scratch_shapes=[
             pltpu.SMEM((REACH + 2,), jnp.int32),
-            pltpu.VMEM((SPARE + 1, 8, LANES), jnp.float32),
+            pltpu.VMEM((FRONT + SPARE + WIDE // LANES, 8, LANES), jnp.float32),
             pltpu.VMEM((WIDE // LANES, 8 * TILES, LANES), jnp.float32),
         ],
         compiler_params=pltpu.CompilerParams(vmem_limit_bytes=24 << 20),

time: 37.9 us -> 37.9 us (level)
  no operation moved by 1% of the time
where the time goes in v13:
time: 37.9 us; the launch traced here: 37.6 us
  blocking collectives  18.1 us (48%)
  starting transfers between devices  8.9 us (23%)
  waiting for transfers between devices  5.39 us (14%)
  Pallas kernels  5.22 us (14%)
    all_to_all x1, blocking collectives, per_device(): lined = lax.all_to_all(lined, 'chan', 0, 0, tiled=True)  18.1 us
    ppermute x5, starting transfers between devices, later(): return lax.ppermute(block, ('chan', 'tm'), route)  8.9 us
    ppermute x5, waiting for transfers between devices, later(): return lax.ppermute(block, ('chan', 'tm'), route)  5.39 us
    pallas_call x1, Pallas kernels, local_plane(): pl.pallas_call(local_kernel, in_specs=[pl.BlockSpec(memory_space=pltpu.HB...  2.61 us
    pallas_call x1, Pallas kernels, final_boxcars(): pl.pallas_call(final_kernel, in_specs=[pl.BlockSpec(memory_space=pltpu.VM...  2.1 us
  transfers between devices with their start and end apart: 5, of which 1 were waited for; matrix products, arithmetic and copies ran while one was open for 0% of the time, Pallas kernels for 0%

profile of v13, /device:TPU:4, one launch (start us, length us, event | category | flops | bytes accessed | tf_op | source)
XLA Modules:
  0.0 37.6 jit_solution(8499686557674925396)
XLA Ops:
  0.0 0.0 copy-start
  0.0 2.6 %local_plane.1 = (f32[64,8,128]{2,1,0:T(8,128)S(1)}, s32[31,8,128]{2,1,0:T(8,128)S(1)}, s32[20,8,128]{2,1,0:T(8,128)S(1)}, s32[16,8,128]{2,1,0:T(8,128)S(1)}, s3...) custom-call(f32[1,512]{1,0:T(1,128)} %bitcast.7, bf16[2,512,512]{2,1,0:T(8,128)(2,1)} %x_hbm.1), custom_call_target="tpu_custom_call" | custom-call | tf_op jit(solution)/shard_map/local_plane/pallas_call | solution.py:274
  2.6 1.9 %collective-permute-start = (s32[31,8,128]{2,1,0:T(8,128)S(1)}, s32[31,8,128]{2,1,0:T(8,128)S(1)}, u32[]{:S(2)}, u32[]{:S(2)}) collective-permute-start(s32[31,8,128]{2,1,0:T(8,128)S(1)} %get-tuple-element.12), channel_id=1, source_target_pairs={{0,1},{1,2},{2,3},{3,4},{4,5},{5,6},{6,7},{8,9},{9,10},{10,11},{11... | collective-permute-start | bytes 380936 | tf_op jit(solution)/shard_map/ppermute | solution.py:456
  4.6 3.1 %collective-permute-start.1 = (s32[20,8,128]{2,1,0:T(8,128)S(1)}, s32[20,8,128]{2,1,0:T(8,128)S(1)}, u32[]{:S(2)}, u32[]{:S(2)}) collective-permute-start(s32[20,8,128]{2,1,0:T(8,128)S(1)} %get-tuple-element.13), channel_id=1, source_target_pairs={{0,2},{1,3},{2,4},{3,5},{4,6},{5,7},{8,10},{9,11},{10,12},{11,13},... | collective-permute-start | bytes 245768 | tf_op jit(solution)/shard_map/ppermute | solution.py:456
  7.7 1.9 %collective-permute-start.2 = (s32[16,8,128]{2,1,0:T(8,128)S(1)}, s32[16,8,128]{2,1,0:T(8,128)S(1)}, u32[]{:S(2)}, u32[]{:S(2)}) collective-permute-start(s32[16,8,128]{2,1,0:T(8,128)S(1)} %get-tuple-element.14), channel_id=1, source_target_pairs={{0,3},{1,4},{2,5},{3,6},{4,7},{8,11},{9,12},{10,13},{11,14},{12,15... | collective-permute-start | bytes 196616 | tf_op jit(solution)/shard_map/ppermute | solution.py:456
  9.6 1.3 %collective-permute-start.3 = (s32[9,8,128]{2,1,0:T(8,128)S(1)}, s32[9,8,128]{2,1,0:T(8,128)S(1)}, u32[]{:S(2)}, u32[]{:S(2)}) collective-permute-start(s32[9,8,128]{2,1,0:T(8,128)S(1)} %get-tuple-element.15), channel_id=1, source_target_pairs={{0,4},{1,5},{2,6},{3,7},{8,12},{9,13},{10,14},{11,15},{16,20},{17,... | collective-permute-start | bytes 110600 | tf_op jit(solution)/shard_map/ppermute | solution.py:456
  10.9 0.7 %collective-permute-start.4 = (s32[2,8,128]{2,1,0:T(8,128)S(1)}, s32[2,8,128]{2,1,0:T(8,128)S(1)}, u32[]{:S(2)}, u32[]{:S(2)}) collective-permute-start(s32[2,8,128]{2,1,0:T(8,128)S(1)} %get-tuple-element.16), channel_id=1, source_target_pairs={{0,5},{1,6},{2,7}} | collective-permute-start | bytes 24584 | tf_op jit(solution)/shard_map/ppermute | solution.py:456
  11.6 0.0 collective-permute-done.4.r5
  11.6 5.4 %collective-permute-done.3.r4 = s32[9,8,128]{2,1,0:T(8,128)S(1)} collective-permute-done((s32[9,8,128]{2,1,0:T(8,128)S(1)}, s32[9,8,128]{2,1,0:T(8,128)S(1)}, u32[]{:S(2)}, u32[]{:S(2)}) %collective-permute-start.3) | collective-permute-done | bytes 36896 | tf_op jit(solution)/shard_map/ppermute | solution.py:456
  16.9 0.0 collective-permute-done.2.r3
  16.9 0.0 collective-permute-done.1.r2
  17.0 0.0 collective-permute-done.r1
  17.0 0.5 %gather_shifted.1 = s32[320,128]{1,0:T(8,128)S(1)} custom-call(f32[64,8,128]{2,1,0:T(8,128)S(1)} %get-tuple-element.11.o0, s32[31,8,128]{2,1,0:T(8,128)S(1)} %collective-permute-done.r1, s32[20,8,128]{2,1,0:T(8,128)S(1)} %collective-permute-done.1.r2, s32[16,8,128]{2,1,0:T(8,128)S(1)} %collective-permute-done.2.r3, ...), custom_call_target="tpu_custom_call" | custom-call | tf_op jit(solution)/shard_map/gather_shifted/pallas_call | solution.py:346
  17.5 18.1 %all_to_all.5 = s32[32,1,1280]{2,1,0:T(1,128)S(1)} all-to-all(s32[32,1,1280]{2,1,0:T(1,128)S(1)} %bitcast.5), channel_id=1, replica_groups=mesh['chan'=32,'tm'=8] {'chan'}, dimensions={0} | all-to-all | bytes 327680 | tf_op jit(solution)/shard_map/all_to_all | solution.py:465
  35.5 0.0 copy-done
  35.5 2.1 %final_boxcars.1 = f32[2,6,64,512]{3,2,1,0:T(8,128)} custom-call(s32[1,6]{1,0:T(1,128)S(1)} %bitcast.6, s32[320,128]{1,0:T(8,128)S(1)} %bitcast.4), custom_call_target="tpu_custom_call" | custom-call | tf_op jit(solution)/shard_map/final_boxcars/pallas_call | solution.py:433
Async XLA Ops:
  0.0 35.5 %copy-start = (s32[6]{0:T(128)S(1)}, s32[6]{0:T(128)}, u32[]{:S(2)}) copy-start(s32[6]{0:T(128)} %param.5) | copy-start | bytes 76
  2.6 14.3 %collective-permute-start = (s32[31,8,128]{2,1,0:T(8,128)S(1)}, s32[31,8,128]{2,1,0:T(8,128)S(1)}, u32[]{:S(2)}, u32[]{:S(2)}) collective-permute-start(s32[31,8,128]{2,1,0:T(8,128)S(1)} %get-tuple-element.12), channel_id=1, source_target_pairs={{0,1},{1,2},{2,3},{3,4},{4,5},{5,6},{6,7},{8,9},{9,10},{10,11},{11... | collective-permute-start | bytes 380936 | tf_op jit(solution)/shard_map/ppermute | solution.py:456
  4.6 12.4 %collective-permute-start.1 = (s32[20,8,128]{2,1,0:T(8,128)S(1)}, s32[20,8,128]{2,1,0:T(8,128)S(1)}, u32[]{:S(2)}, u32[]{:S(2)}) collective-permute-start(s32[20,8,128]{2,1,0:T(8,128)S(1)} %get-tuple-element.13), channel_id=1, source_target_pairs={{0,2},{1,3},{2,4},{3,5},{4,6},{5,7},{8,10},{9,11},{10,12},{11,13},... | collective-permute-start | bytes 245768 | tf_op jit(solution)/shard_map/ppermute | solution.py:456
  7.7 9.3 %collective-permute-start.2 = (s32[16,8,128]{2,1,0:T(8,128)S(1)}, s32[16,8,128]{2,1,0:T(8,128)S(1)}, u32[]{:S(2)}, u32[]{:S(2)}) collective-permute-start(s32[16,8,128]{2,1,0:T(8,128)S(1)} %get-tuple-element.14), channel_id=1, source_target_pairs={{0,3},{1,4},{2,5},{3,6},{4,7},{8,11},{9,12},{10,13},{11,14},{12,15... | collective-permute-start | bytes 196616 | tf_op jit(solution)/shard_map/ppermute | solution.py:456
  9.6 7.4 %collective-permute-start.3 = (s32[9,8,128]{2,1,0:T(8,128)S(1)}, s32[9,8,128]{2,1,0:T(8,128)S(1)}, u32[]{:S(2)}, u32[]{:S(2)}) collective-permute-start(s32[9,8,128]{2,1,0:T(8,128)S(1)} %get-tuple-element.15), channel_id=1, source_target_pairs={{0,4},{1,5},{2,6},{3,7},{8,12},{9,13},{10,14},{11,15},{16,20},{17,... | collective-permute-start | bytes 110600 | tf_op jit(solution)/shard_map/ppermute | solution.py:456
  10.9 0.7 %collective-permute-start.4 = (s32[2,8,128]{2,1,0:T(8,128)S(1)}, s32[2,8,128]{2,1,0:T(8,128)S(1)}, u32[]{:S(2)}, u32[]{:S(2)}) collective-permute-start(s32[2,8,128]{2,1,0:T(8,128)S(1)} %get-tuple-element.16), channel_id=1, source_target_pairs={{0,5},{1,6},{2,7}} | collective-permute-start | bytes 24584 | tf_op jit(solution)/shard_map/ppermute | solution.py:456

commit v14 on v13

--- a/solution.py
+++ b/solution.py
@@ -132,9 +132,9 @@
     return (high << 16) | (low & 0xFFFF)
 
 
-def unpair(word, step):
-    high = (word >> 16).astype(jnp.float32) * step
-    low = ((word << 16) >> 16).astype(jnp.float32) * step
+def unpair(word, span):
+    high = (word >> 16).astype(jnp.float32) * (1.0 / TOP) * span
+    low = ((word << 16) >> 16).astype(jnp.float32) * (1.0 / TOP) * span
     return high, low
 
 
@@ -242,9 +242,12 @@
         )
     merge_rows(groups, one, two, WIDE // LANES)
     odd = lax.broadcasted_iota(jnp.int32, (8, UNITS * LANES), 0) & 2 != 0
+    top = jnp.zeros((8, LANES), jnp.float32)
     for a in range(TILES):
         rows = [take(two.at[b], 4 * a, 4, 0, WIDE // LANES) for b in range(BEAMS)]
         rows = jnp.concatenate([jnp.concatenate(rows, axis=0), blank], axis=1)
+        for c in range(WIDE // LANES):
+            top = jnp.maximum(top, jnp.abs(rows[:, c * LANES : (c + 1) * LANES]))
         rows = jnp.where(odd, pltpu.roll(rows, 2 * q, 1), rows)
         rows = pltpu.roll(rows, (4 * q * a) & (LANES - 1), 1)
         place = a * PLACES
@@ -253,13 +256,7 @@
         for i in (UNITS, UNITS + 2):
             packed[places[place + i]] = packed[places[place + i + 1]]
     o0[...] = packed[pl.ds(0, SIZES[0])]
-    tiles = [
-        two[b, c, pl.ds(8 * a, 8), :]
-        for b in range(BEAMS)
-        for c in range(WIDE // LANES)
-        for a in range(8)
-    ]
-    exponent = exponent_of(largest_of(tiles))
+    exponent = exponent_of(largest_of([top]))
     inverse = 1.0 / span_of(exponent)
     for k, out in enumerate((o1, o2, o3, o4, o5), 1):
         words = SIZES[k] // 2
@@ -304,10 +301,10 @@
     packed[pl.ds(FRONT, SIZES[0])] = o0[...]
     for k, piece in enumerate((r1, r2, r3, r4, r5), 1):
         words = SIZES[k] // 2
-        step = span_of(piece[words]) * (1.0 / TOP)
+        span = span_of(piece[words])
         for t in range(words):
             slot = FRONT + STARTS[k] + 2 * t
-            packed[slot], packed[slot + 1] = unpair(piece[t], step)
+            packed[slot], packed[slot + 1] = unpair(piece[t], span)
     top = jnp.zeros((8, LANES), jnp.float32)
     for a in range(TILES):
         k, at, _, _, (here, then, over) = group_shares(q, a, jnp.minimum)
@@ -365,8 +362,8 @@
                 x_ref[pl.ds(g * BLOCK + c * 2 + e, 8, stride=4 * BLOCK), :]
                 for c in range(WIDE // LANES)
             ]
-            step = jnp.broadcast_to(span_of(words[0][:, :1]) * (1.0 / TOP), (8, LANES))
-            chunks = [unpair(word, step) for word in words]
+            span = jnp.broadcast_to(span_of(words[0][:, :1]), (8, LANES))
+            chunks = [unpair(word, span) for word in words]
             for b in range(BEAMS):
                 row = jnp.concatenate([chunk[b] for chunk in chunks], axis=1)
                 beams[b][g].append(row)
@@ -410,16 +407,17 @@
         jnp.concatenate([before[0], here[0], before[1], here[1]], axis=1)
         for before, here in zip(parts, parts[1:])
     ]
-    windows = jnp.concatenate(windows, axis=0)
     for places in ((1, 2), (3, 4), (5,)):
         bands = boxcar_bands(widths, places)
         bands = jnp.concatenate([bands, bands], axis=0)
-        sums = jnp.dot(windows, bands, preferred_element_type=jnp.float32)
+        sums = [
+            jnp.dot(window, bands, preferred_element_type=jnp.float32)
+            for window in windows
+        ]
         for i, k in enumerate(places):
             norm = boxcar_norm(widths[:, k : k + 1])
             for c in range(PER):
-                term = sums[rows * c : rows * (c + 1), i * LANES : (i + 1) * LANES]
-                term = term * norm
+                term = sums[c][:, i * LANES : (i + 1) * LANES] * norm
                 for b in range(BEAMS):
                     held[b, k, :, pl.ds(c * LANES, LANES)] = term[
                         b * ROWS : (b + 1) * ROWS

time: 37.9 us -> 37.8 us (level)
  no operation moved by 1% of the time
where the time goes in v14:
time: 37.8 us; the launch traced here: 37.6 us
  blocking collectives  18.1 us (48%)
  starting transfers between devices  8.9 us (24%)
  waiting for transfers between devices  5.39 us (14%)
  Pallas kernels  5.15 us (14%)
    all_to_all x1, blocking collectives, per_device(): lined = lax.all_to_all(lined, 'chan', 0, 0, tiled=True)  18.1 us
    ppermute x5, starting transfers between devices, later(): return lax.ppermute(block, ('chan', 'tm'), route)  8.9 us
    ppermute x5, waiting for transfers between devices, later(): return lax.ppermute(block, ('chan', 'tm'), route)  5.39 us
    pallas_call x1, Pallas kernels, local_plane(): pl.pallas_call(local_kernel, in_specs=[pl.BlockSpec(memory_space=pltpu.HB...  2.61 us
    pallas_call x1, Pallas kernels, final_boxcars(): pl.pallas_call(final_kernel, in_specs=[pl.BlockSpec(memory_space=pltpu.VM...  2.02 us
  transfers between devices with their start and end apart: 5, of which 1 were waited for; matrix products, arithmetic and copies ran while one was open for 0% of the time, Pallas kernels for 0%

profile of v14, /device:TPU:4, one launch (start us, length us, event | category | flops | bytes accessed | tf_op | source)
XLA Modules:
  0.0 37.6 jit_solution(8461842075265099613)
XLA Ops:
  0.0 0.0 copy-start
  0.0 2.6 %local_plane.1 = (f32[64,8,128]{2,1,0:T(8,128)S(1)}, s32[31,8,128]{2,1,0:T(8,128)S(1)}, s32[20,8,128]{2,1,0:T(8,128)S(1)}, s32[16,8,128]{2,1,0:T(8,128)S(1)}, s3...) custom-call(f32[1,512]{1,0:T(1,128)} %bitcast.7, bf16[2,512,512]{2,1,0:T(8,128)(2,1)} %x_hbm.1), custom_call_target="tpu_custom_call" | custom-call | tf_op jit(solution)/shard_map/local_plane/pallas_call | solution.py:271
  2.6 1.9 %collective-permute-start = (s32[31,8,128]{2,1,0:T(8,128)S(1)}, s32[31,8,128]{2,1,0:T(8,128)S(1)}, u32[]{:S(2)}, u32[]{:S(2)}) collective-permute-start(s32[31,8,128]{2,1,0:T(8,128)S(1)} %get-tuple-element.12), channel_id=1, source_target_pairs={{0,1},{1,2},{2,3},{3,4},{4,5},{5,6},{6,7},{8,9},{9,10},{10,11},{11... | collective-permute-start | bytes 380936 | tf_op jit(solution)/shard_map/ppermute | solution.py:454
  4.6 3.1 %collective-permute-start.1 = (s32[20,8,128]{2,1,0:T(8,128)S(1)}, s32[20,8,128]{2,1,0:T(8,128)S(1)}, u32[]{:S(2)}, u32[]{:S(2)}) collective-permute-start(s32[20,8,128]{2,1,0:T(8,128)S(1)} %get-tuple-element.13), channel_id=1, source_target_pairs={{0,2},{1,3},{2,4},{3,5},{4,6},{5,7},{8,10},{9,11},{10,12},{11,13},... | collective-permute-start | bytes 245768 | tf_op jit(solution)/shard_map/ppermute | solution.py:454
  7.7 1.9 %collective-permute-start.2 = (s32[16,8,128]{2,1,0:T(8,128)S(1)}, s32[16,8,128]{2,1,0:T(8,128)S(1)}, u32[]{:S(2)}, u32[]{:S(2)}) collective-permute-start(s32[16,8,128]{2,1,0:T(8,128)S(1)} %get-tuple-element.14), channel_id=1, source_target_pairs={{0,3},{1,4},{2,5},{3,6},{4,7},{8,11},{9,12},{10,13},{11,14},{12,15... | collective-permute-start | bytes 196616 | tf_op jit(solution)/shard_map/ppermute | solution.py:454
  9.6 1.3 %collective-permute-start.3 = (s32[9,8,128]{2,1,0:T(8,128)S(1)}, s32[9,8,128]{2,1,0:T(8,128)S(1)}, u32[]{:S(2)}, u32[]{:S(2)}) collective-permute-start(s32[9,8,128]{2,1,0:T(8,128)S(1)} %get-tuple-element.15), channel_id=1, source_target_pairs={{0,4},{1,5},{2,6},{3,7},{8,12},{9,13},{10,14},{11,15},{16,20},{17,... | collective-permute-start | bytes 110600 | tf_op jit(solution)/shard_map/ppermute | solution.py:454
  10.9 0.7 %collective-permute-start.4 = (s32[2,8,128]{2,1,0:T(8,128)S(1)}, s32[2,8,128]{2,1,0:T(8,128)S(1)}, u32[]{:S(2)}, u32[]{:S(2)}) collective-permute-start(s32[2,8,128]{2,1,0:T(8,128)S(1)} %get-tuple-element.16), channel_id=1, source_target_pairs={{0,5},{1,6},{2,7}} | collective-permute-start | bytes 24584 | tf_op jit(solution)/shard_map/ppermute | solution.py:454
  11.6 0.0 collective-permute-done.4.r5
  11.6 5.4 %collective-permute-done.3.r4 = s32[9,8,128]{2,1,0:T(8,128)S(1)} collective-permute-done((s32[9,8,128]{2,1,0:T(8,128)S(1)}, s32[9,8,128]{2,1,0:T(8,128)S(1)}, u32[]{:S(2)}, u32[]{:S(2)}) %collective-permute-start.3) | collective-permute-done | bytes 36896 | tf_op jit(solution)/shard_map/ppermute | solution.py:454
  16.9 0.0 collective-permute-done.2.r3
  16.9 0.0 collective-permute-done.1.r2
  17.0 0.0 collective-permute-done.r1
  17.0 0.5 %gather_shifted.1 = s32[320,128]{1,0:T(8,128)S(1)} custom-call(f32[64,8,128]{2,1,0:T(8,128)S(1)} %get-tuple-element.11.o0, s32[31,8,128]{2,1,0:T(8,128)S(1)} %collective-permute-done.r1, s32[20,8,128]{2,1,0:T(8,128)S(1)} %collective-permute-done.1.r2, s32[16,8,128]{2,1,0:T(8,128)S(1)} %collective-permute-done.2.r3, ...), custom_call_target="tpu_custom_call" | custom-call | tf_op jit(solution)/shard_map/gather_shifted/pallas_call | solution.py:343
  17.5 18.1 %all_to_all.5 = s32[32,1,1280]{2,1,0:T(1,128)S(1)} all-to-all(s32[32,1,1280]{2,1,0:T(1,128)S(1)} %bitcast.5), channel_id=1, replica_groups=mesh['chan'=32,'tm'=8] {'chan'}, dimensions={0} | all-to-all | bytes 327680 | tf_op jit(solution)/shard_map/all_to_all | solution.py:463
  35.5 0.0 copy-done
  35.5 2.0 %final_boxcars.1 = f32[2,6,64,512]{3,2,1,0:T(8,128)} custom-call(s32[1,6]{1,0:T(1,128)S(1)} %bitcast.6, s32[320,128]{1,0:T(8,128)S(1)} %bitcast.4), custom_call_target="tpu_custom_call" | custom-call | tf_op jit(solution)/shard_map/final_boxcars/pallas_call | solution.py:431
Async XLA Ops:
  0.0 35.5 %copy-start = (s32[6]{0:T(128)S(1)}, s32[6]{0:T(128)}, u32[]{:S(2)}) copy-start(s32[6]{0:T(128)} %param.5) | copy-start | bytes 76
  2.6 14.3 %collective-permute-start = (s32[31,8,128]{2,1,0:T(8,128)S(1)}, s32[31,8,128]{2,1,0:T(8,128)S(1)}, u32[]{:S(2)}, u32[]{:S(2)}) collective-permute-start(s32[31,8,128]{2,1,0:T(8,128)S(1)} %get-tuple-element.12), channel_id=1, source_target_pairs={{0,1},{1,2},{2,3},{3,4},{4,5},{5,6},{6,7},{8,9},{9,10},{10,11},{11... | collective-permute-start | bytes 380936 | tf_op jit(solution)/shard_map/ppermute | solution.py:454
  4.6 12.4 %collective-permute-start.1 = (s32[20,8,128]{2,1,0:T(8,128)S(1)}, s32[20,8,128]{2,1,0:T(8,128)S(1)}, u32[]{:S(2)}, u32[]{:S(2)}) collective-permute-start(s32[20,8,128]{2,1,0:T(8,128)S(1)} %get-tuple-element.13), channel_id=1, source_target_pairs={{0,2},{1,3},{2,4},{3,5},{4,6},{5,7},{8,10},{9,11},{10,12},{11,13},... | collective-permute-start | bytes 245768 | tf_op jit(solution)/shard_map/ppermute | solution.py:454
  7.7 9.3 %collective-permute-start.2 = (s32[16,8,128]{2,1,0:T(8,128)S(1)}, s32[16,8,128]{2,1,0:T(8,128)S(1)}, u32[]{:S(2)}, u32[]{:S(2)}) collective-permute-start(s32[16,8,128]{2,1,0:T(8,128)S(1)} %get-tuple-element.14), channel_id=1, source_target_pairs={{0,3},{1,4},{2,5},{3,6},{4,7},{8,11},{9,12},{10,13},{11,14},{12,15... | collective-permute-start | bytes 196616 | tf_op jit(solution)/shard_map/ppermute | solution.py:454
  9.6 7.4 %collective-permute-start.3 = (s32[9,8,128]{2,1,0:T(8,128)S(1)}, s32[9,8,128]{2,1,0:T(8,128)S(1)}, u32[]{:S(2)}, u32[]{:S(2)}) collective-permute-start(s32[9,8,128]{2,1,0:T(8,128)S(1)} %get-tuple-element.15), channel_id=1, source_target_pairs={{0,4},{1,5},{2,6},{3,7},{8,12},{9,13},{10,14},{11,15},{16,20},{17,... | collective-permute-start | bytes 110600 | tf_op jit(solution)/shard_map/ppermute | solution.py:454
  10.9 0.7 %collective-permute-start.4 = (s32[2,8,128]{2,1,0:T(8,128)S(1)}, s32[2,8,128]{2,1,0:T(8,128)S(1)}, u32[]{:S(2)}, u32[]{:S(2)}) collective-permute-start(s32[2,8,128]{2,1,0:T(8,128)S(1)} %get-tuple-element.16), channel_id=1, source_target_pairs={{0,5},{1,6},{2,7}} | collective-permute-start | bytes 24584 | tf_op jit(solution)/shard_map/ppermute | solution.py:454

commit v15 on v14

--- a/solution.py
+++ b/solution.py
@@ -20,6 +20,7 @@
 UNITS = 6
 PLACES = UNITS + 4
 PER = SPAN // LANES
+FAR = 3
 FRONT = PER
 BLOCK = 10
 TOP = 32000.0
@@ -64,7 +65,7 @@
         taken = {0}
         for k in range(REACH - 1, 0, -1):
             if counts[q, k]:
-                allowed = (k,) if q >= 22 or k == 3 else (4, 2, 1)
+                allowed = (k,) if q >= 22 or k == 3 else (2, 1)
                 fits = [i for i in allowed if i not in taken and sizes[i] >= counts[q, k]]
                 buffers[q, k] = fits[0]
                 distances[q, fits[0]] = k
@@ -294,34 +295,63 @@
     )
 
 
-def gather_kernel(o0, r1, r2, r3, r4, r5, out, free, packed, held):
-    q = PARTS - 1 - lax.axis_index("chan")
-    tiles = WIDE // LANES
-    first_slots(q, free)
-    packed[pl.ds(FRONT, SIZES[0])] = o0[...]
-    for k, piece in enumerate((r1, r2, r3, r4, r5), 1):
+def unpack(pieces, first, packed):
+    for k, piece in enumerate(pieces, first):
         words = SIZES[k] // 2
         span = span_of(piece[words])
         for t in range(words):
             slot = FRONT + STARTS[k] + 2 * t
             packed[slot], packed[slot + 1] = unpair(piece[t], span)
+
+
+def window_tiles(q, a, free, packed, used):
+    k, at, _, _, (here, then, over) = group_shares(q, a, jnp.minimum)
+    p0, p1, p2 = free[k], free[k + 1], free[k + 2]
+    free[k] = p0 + here
+    free[k + 1] = p1 + then
+    free[k + 2] = p2 + over
+    end = packed[pl.ds(FRONT + p0 - at, PER)]
+    begin = packed[pl.ds(FRONT + p1, WIDE // LANES)]
+    more = packed[pl.ds(FRONT + p2, 2)]
+    at = jnp.where(used(p0), at, PER)
+    then = jnp.where(used(p1), then, 0)
+    over = jnp.where(used(p2), over, 0)
+    window = []
+    for c in range(WIDE // LANES):
+        tile = jnp.where(c < then, begin[c], 0.0)
+        if c > 0:
+            tile = tile + jnp.where(c > at, end[c - 1], 0.0)
+        if c < 2:
+            tile = tile + jnp.where(c < over, more[c], 0.0)
+        window.append(tile)
+    return window
+
+
+def near_kernel(o0, r1, r2, held, free, packed):
+    q = PARTS - 1 - lax.axis_index("chan")
+    first_slots(q, free)
+    packed[pl.ds(FRONT, SIZES[0])] = o0[...]
+    unpack((r1, r2), 1, packed)
+    for a in range(TILES):
+        window = window_tiles(q, a, free, packed, lambda p: p < STARTS[FAR])
+        for c, tile in enumerate(window):
+            held[c, pl.ds(8 * a, 8), :] = tile
+
+
+def far_kernel(near, r3, r4, r5, out, free, packed, held):
+    q = PARTS - 1 - lax.axis_index("chan")
+    tiles = WIDE // LANES
+    first_slots(q, free)
+    unpack((r3, r4, r5), FAR, packed)
     top = jnp.zeros((8, LANES), jnp.float32)
     for a in range(TILES):
-        k, at, _, _, (here, then, over) = group_shares(q, a, jnp.minimum)
-        p0, p1, p2 = free[k], free[k + 1], free[k + 2]
-        free[k] = p0 + here
-        free[k + 1] = p1 + then
-        free[k + 2] = p2 + over
-        end = packed[pl.ds(FRONT + p0 - at, PER)]
-        begin = packed[pl.ds(FRONT + p1, tiles)]
-        more = packed[pl.ds(FRONT + p2, 2)]
-        for c in range(tiles):
-            tile = jnp.where(c < then, begin[c], 0.0)
-            if c > 0:
-                tile = tile + jnp.where(c > at, end[c - 1], 0.0)
-            if c < 2:
-                tile = tile + jnp.where(c < over, more[c], 0.0)
-            held[c, pl.ds(8 * a, 8), :] = tile
+        rows = pl.ds(8 * a, 8)
+        window = [near[c, rows, :] for c in range(tiles)]
+        if 4 * (PARTS - 1) * a >= SPAN:
+            more = window_tiles(q, a, free, packed, lambda p: p >= STARTS[FAR])
+            window = [tile + part for tile, part in zip(window, more)]
+        for c, tile in enumerate(window):
+            held[c, rows, :] = tile
             top = jnp.maximum(top, jnp.abs(tile))
     exponent = exponent_of(largest_of([top]))
     inverse = 1.0 / span_of(exponent)[:1]
@@ -340,18 +370,31 @@
 
 def gather_shifted(pieces):
     vmem = pl.BlockSpec(memory_space=pltpu.VMEM)
+    windows = (WIDE // LANES, 8 * TILES, LANES)
+    slots = [
+        pltpu.SMEM((REACH + 2,), jnp.int32),
+        pltpu.VMEM((FRONT + SPARE + WIDE // LANES, 8, LANES), jnp.float32),
+    ]
+    params = pltpu.CompilerParams(vmem_limit_bytes=24 << 20)
+    near = pl.pallas_call(
+        near_kernel,
+        in_specs=[vmem] * FAR,
+        out_shape=jax.ShapeDtypeStruct(windows, jnp.float32),
+        scratch_shapes=slots,
+        compiler_params=params,
+        cost_estimate=pl.CostEstimate(
+            flops=1 << 22, bytes_accessed=4 << 20, transcendentals=0
+        ),
+        name="gather_near",
+    )(*pieces[:FAR])
     return pl.pallas_call(
-        gather_kernel,
-        in_specs=[vmem] * REACH,
+        far_kernel,
+        in_specs=[vmem] * (1 + REACH - FAR),
         out_shape=jax.ShapeDtypeStruct((PARTS * BLOCK, LANES), jnp.int32),
-        scratch_shapes=[
-            pltpu.SMEM((REACH + 2,), jnp.int32),
-            pltpu.VMEM((FRONT + SPARE + WIDE // LANES, 8, LANES), jnp.float32),
-            pltpu.VMEM((WIDE // LANES, 8 * TILES, LANES), jnp.float32),
-        ],
-        compiler_params=pltpu.CompilerParams(vmem_limit_bytes=24 << 20),
-        name="gather_shifted",
-    )(*pieces)
+        scratch_shapes=slots + [pltpu.VMEM(windows, jnp.float32)],
+        compiler_params=params,
+        name="gather_far",
+    )(near, *pieces[FAR:])
 
 
 def final_groups(x_ref):

time: 37.8 us -> 37.8 us (level)
  waiting for transfers between devices: 5.39 us -> 4.96 us
    ppermute x5, waiting for transfers between devices: 5.39 us -> 4.96 us  [later(): return lax.ppermute(block, ('chan', 'tm'), route)]
    pallas_call x1 -> x2, Pallas kernels: 0.51 us -> 0.82 us  [the longest x1 0.43 us: gather_shifted(): pl.pallas_call(far_kernel, in_specs=[vmem] * (1 + REACH - FAR), out_shape...]
  transfers between devices with their start and end apart: 5 -> 5, of which waited for: 1 -> 1; matrix products, arithmetic and copies ran while one was open for 0% -> 0% of each run, Pallas kernels for 0% -> 1%
where the time goes in v15:
time: 37.8 us; the launch traced here: 37.4 us
  blocking collectives  18.1 us (48%)
  starting transfers between devices  8.9 us (24%)
  Pallas kernels  5.44 us (14%)
  waiting for transfers between devices  4.96 us (13%)
    all_to_all x1, blocking collectives, per_device(): lined = lax.all_to_all(lined, 'chan', 0, 0, tiled=True)  18.1 us
    ppermute x5, starting transfers between devices, later(): return lax.ppermute(block, ('chan', 'tm'), route)  8.9 us
    ppermute x5, waiting for transfers between devices, later(): return lax.ppermute(block, ('chan', 'tm'), route)  4.96 us
    pallas_call x1, Pallas kernels, local_plane(): pl.pallas_call(local_kernel, in_specs=[pl.BlockSpec(memory_space=pltpu.HB...  2.61 us
    pallas_call x1, Pallas kernels, final_boxcars(): pl.pallas_call(final_kernel, in_specs=[pl.BlockSpec(memory_space=pltpu.VM...  2.01 us
  transfers between devices with their start and end apart: 5, of which 1 were waited for; matrix products, arithmetic and copies ran while one was open for 0% of the time, Pallas kernels for 1%

profile of v15, /device:TPU:4, one launch (start us, length us, event | category | flops | bytes accessed | tf_op | source)
XLA Modules:
  0.0 37.4 jit_solution(4682867539226861575)
XLA Ops:
  0.0 0.0 copy-start
  0.0 2.6 %local_plane.1 = (f32[64,8,128]{2,1,0:T(8,128)S(1)}, s32[31,8,128]{2,1,0:T(8,128)S(1)}, s32[20,8,128]{2,1,0:T(8,128)S(1)}, s32[16,8,128]{2,1,0:T(8,128)S(1)}, s3...) custom-call(f32[1,512]{1,0:T(1,128)} %bitcast.7, bf16[2,512,512]{2,1,0:T(8,128)(2,1)} %x_hbm.1), custom_call_target="tpu_custom_call" | custom-call | tf_op jit(solution)/shard_map/local_plane/pallas_call | solution.py:272
  2.6 1.9 %collective-permute-start = (s32[31,8,128]{2,1,0:T(8,128)S(1)}, s32[31,8,128]{2,1,0:T(8,128)S(1)}, u32[]{:S(2)}, u32[]{:S(2)}) collective-permute-start(s32[31,8,128]{2,1,0:T(8,128)S(1)} %get-tuple-element.12), channel_id=1, source_target_pairs={{0,1},{1,2},{2,3},{3,4},{4,5},{5,6},{6,7},{8,9},{9,10},{10,11},{11... | collective-permute-start | bytes 380936 | tf_op jit(solution)/shard_map/ppermute | solution.py:497
  4.6 3.1 %collective-permute-start.1 = (s32[20,8,128]{2,1,0:T(8,128)S(1)}, s32[20,8,128]{2,1,0:T(8,128)S(1)}, u32[]{:S(2)}, u32[]{:S(2)}) collective-permute-start(s32[20,8,128]{2,1,0:T(8,128)S(1)} %get-tuple-element.13), channel_id=1, source_target_pairs={{0,2},{1,3},{2,4},{3,5},{4,6},{5,7},{8,10},{9,11},{10,12},{11,13},... | collective-permute-start | bytes 245768 | tf_op jit(solution)/shard_map/ppermute | solution.py:497
  7.7 1.9 %collective-permute-start.2 = (s32[16,8,128]{2,1,0:T(8,128)S(1)}, s32[16,8,128]{2,1,0:T(8,128)S(1)}, u32[]{:S(2)}, u32[]{:S(2)}) collective-permute-start(s32[16,8,128]{2,1,0:T(8,128)S(1)} %get-tuple-element.14), channel_id=1, source_target_pairs={{0,3},{1,4},{2,5},{3,6},{4,7},{8,11},{9,12},{10,13},{11,14},{12,15... | collective-permute-start | bytes 196616 | tf_op jit(solution)/shard_map/ppermute | solution.py:497
  9.6 1.3 %collective-permute-start.3 = (s32[9,8,128]{2,1,0:T(8,128)S(1)}, s32[9,8,128]{2,1,0:T(8,128)S(1)}, u32[]{:S(2)}, u32[]{:S(2)}) collective-permute-start(s32[9,8,128]{2,1,0:T(8,128)S(1)} %get-tuple-element.15), channel_id=1, source_target_pairs={{0,4},{1,5},{2,6},{3,7},{8,12},{9,13},{10,14},{11,15},{16,20},{17,... | collective-permute-start | bytes 110600 | tf_op jit(solution)/shard_map/ppermute | solution.py:497
  10.9 0.7 %collective-permute-start.4 = (s32[2,8,128]{2,1,0:T(8,128)S(1)}, s32[2,8,128]{2,1,0:T(8,128)S(1)}, u32[]{:S(2)}, u32[]{:S(2)}) collective-permute-start(s32[2,8,128]{2,1,0:T(8,128)S(1)} %get-tuple-element.16), channel_id=1, source_target_pairs={{0,5},{1,6},{2,7}} | collective-permute-start | bytes 24584 | tf_op jit(solution)/shard_map/ppermute | solution.py:497
  11.6 0.0 collective-permute-done.1.r2
  11.6 0.0 collective-permute-done.r1
  11.6 0.4 %gather_near.1.near = f32[5,128,128]{2,1,0:T(8,128)S(1)} custom-call(f32[64,8,128]{2,1,0:T(8,128)S(1)} %get-tuple-element.11.o0, s32[31,8,128]{2,1,0:T(8,128)S(1)} %collective-permute-done.r1, s32[20,8,128]{2,1,0:T(8,128)S(1)} %collective-permute-done.1.r2), custom_call_target="tpu_custom_call" | custom-call | flops 4194304 | bytes 4194304 | tf_op jit(solution)/shard_map/gather_near/pallas_call | solution.py:379
  12.0 0.0 collective-permute-done.4.r5
  12.0 5.0 %collective-permute-done.3.r4 = s32[9,8,128]{2,1,0:T(8,128)S(1)} collective-permute-done((s32[9,8,128]{2,1,0:T(8,128)S(1)}, s32[9,8,128]{2,1,0:T(8,128)S(1)}, u32[]{:S(2)}, u32[]{:S(2)}) %collective-permute-start.3) | collective-permute-done | bytes 36896 | tf_op jit(solution)/shard_map/ppermute | solution.py:497
  16.9 0.0 collective-permute-done.2.r3
  16.9 0.4 %gather_far.1 = s32[320,128]{1,0:T(8,128)S(1)} custom-call(f32[5,128,128]{2,1,0:T(8,128)S(1)} %gather_near.1.near, s32[16,8,128]{2,1,0:T(8,128)S(1)} %collective-permute-done.2.r3, s32[9,8,128]{2,1,0:T(8,128)S(1)} %collective-permute-done.3.r4, s32[2,8,128]{2,1,0:T(8,128)S(1)} %collective-permute-done.4.r5), custom_call_target="tpu_custom_call" | custom-call | tf_op jit(solution)/shard_map/gather_far/pallas_call | solution.py:390
  17.4 18.1 %all_to_all.5 = s32[32,1,1280]{2,1,0:T(1,128)S(1)} all-to-all(s32[32,1,1280]{2,1,0:T(1,128)S(1)} %bitcast.4), channel_id=1, replica_groups=mesh['chan'=32,'tm'=8] {'chan'}, dimensions={0} | all-to-all | bytes 327680 | tf_op jit(solution)/shard_map/all_to_all | solution.py:506
  35.4 0.0 copy-done
  35.4 2.0 %final_boxcars.1 = f32[2,6,64,512]{3,2,1,0:T(8,128)} custom-call(s32[1,6]{1,0:T(1,128)S(1)} %bitcast.6, s32[320,128]{1,0:T(8,128)S(1)} %bitcast.5), custom_call_target="tpu_custom_call" | custom-call | tf_op jit(solution)/shard_map/final_boxcars/pallas_call | solution.py:474
Async XLA Ops:
  0.0 35.4 %copy-start = (s32[6]{0:T(128)S(1)}, s32[6]{0:T(128)}, u32[]{:S(2)}) copy-start(s32[6]{0:T(128)} %param.5) | copy-start | bytes 76
  2.6 8.9 %collective-permute-start = (s32[31,8,128]{2,1,0:T(8,128)S(1)}, s32[31,8,128]{2,1,0:T(8,128)S(1)}, u32[]{:S(2)}, u32[]{:S(2)}) collective-permute-start(s32[31,8,128]{2,1,0:T(8,128)S(1)} %get-tuple-element.12), channel_id=1, source_target_pairs={{0,1},{1,2},{2,3},{3,4},{4,5},{5,6},{6,7},{8,9},{9,10},{10,11},{11... | collective-permute-start | bytes 380936 | tf_op jit(solution)/shard_map/ppermute | solution.py:497
  4.6 7.0 %collective-permute-start.1 = (s32[20,8,128]{2,1,0:T(8,128)S(1)}, s32[20,8,128]{2,1,0:T(8,128)S(1)}, u32[]{:S(2)}, u32[]{:S(2)}) collective-permute-start(s32[20,8,128]{2,1,0:T(8,128)S(1)} %get-tuple-element.13), channel_id=1, source_target_pairs={{0,2},{1,3},{2,4},{3,5},{4,6},{5,7},{8,10},{9,11},{10,12},{11,13},... | collective-permute-start | bytes 245768 | tf_op jit(solution)/shard_map/ppermute | solution.py:497
  7.7 9.3 %collective-permute-start.2 = (s32[16,8,128]{2,1,0:T(8,128)S(1)}, s32[16,8,128]{2,1,0:T(8,128)S(1)}, u32[]{:S(2)}, u32[]{:S(2)}) collective-permute-start(s32[16,8,128]{2,1,0:T(8,128)S(1)} %get-tuple-element.14), channel_id=1, source_target_pairs={{0,3},{1,4},{2,5},{3,6},{4,7},{8,11},{9,12},{10,13},{11,14},{12,15... | collective-permute-start | bytes 196616 | tf_op jit(solution)/shard_map/ppermute | solution.py:497
  9.6 7.4 %collective-permute-start.3 = (s32[9,8,128]{2,1,0:T(8,128)S(1)}, s32[9,8,128]{2,1,0:T(8,128)S(1)}, u32[]{:S(2)}, u32[]{:S(2)}) collective-permute-start(s32[9,8,128]{2,1,0:T(8,128)S(1)} %get-tuple-element.15), channel_id=1, source_target_pairs={{0,4},{1,5},{2,6},{3,7},{8,12},{9,13},{10,14},{11,15},{16,20},{17,... | collective-permute-start | bytes 110600 | tf_op jit(solution)/shard_map/ppermute | solution.py:497
  10.9 1.1 %collective-permute-start.4 = (s32[2,8,128]{2,1,0:T(8,128)S(1)}, s32[2,8,128]{2,1,0:T(8,128)S(1)}, u32[]{:S(2)}, u32[]{:S(2)}) collective-permute-start(s32[2,8,128]{2,1,0:T(8,128)S(1)} %get-tuple-element.16), channel_id=1, source_target_pairs={{0,5},{1,6},{2,7}} | collective-permute-start | bytes 24584 | tf_op jit(solution)/shard_map/ppermute | solution.py:497

commit v16 on v15

--- a/solution.py
+++ b/solution.py
@@ -304,26 +304,25 @@
             packed[slot], packed[slot + 1] = unpair(piece[t], span)
 
 
-def window_tiles(q, a, free, packed, used):
-    k, at, _, _, (here, then, over) = group_shares(q, a, jnp.minimum)
-    p0, p1, p2 = free[k], free[k + 1], free[k + 2]
-    free[k] = p0 + here
-    free[k + 1] = p1 + then
-    free[k + 2] = p2 + over
-    end = packed[pl.ds(FRONT + p0 - at, PER)]
-    begin = packed[pl.ds(FRONT + p1, WIDE // LANES)]
-    more = packed[pl.ds(FRONT + p2, 2)]
-    at = jnp.where(used(p0), at, PER)
-    then = jnp.where(used(p1), then, 0)
-    over = jnp.where(used(p2), over, 0)
-    window = []
-    for c in range(WIDE // LANES):
-        tile = jnp.where(c < then, begin[c], 0.0)
-        if c > 0:
-            tile = tile + jnp.where(c > at, end[c - 1], 0.0)
-        if c < 2:
-            tile = tile + jnp.where(c < over, more[c], 0.0)
-        window.append(tile)
+def window_tiles(q, a, free, packed, used, least=0):
+    k, at, _, _, shares = group_shares(q, a, jnp.minimum)
+    most = 4 * (PARTS - 1) * a // SPAN
+    window = [None] * (WIDE // LANES)
+    for i, (first, count) in enumerate(((1, PER), (0, WIDE // LANES), (0, 2))):
+        if most + i < least:
+            continue
+        p = free[k + i]
+        free[k + i] = p + shares[i]
+        if i == 0:
+            block = packed[pl.ds(FRONT + p - at, count)]
+            after = jnp.where(used(p), at, PER)
+        else:
+            block = packed[pl.ds(FRONT + p, count)]
+            before = jnp.where(used(p), shares[i], 0)
+        for c in range(first, first + count):
+            inside = c > after if i == 0 else c < before
+            tile = jnp.where(inside, block[c - first], 0.0)
+            window[c] = tile if window[c] is None else window[c] + tile
     return window
 
 
@@ -348,8 +347,11 @@
         rows = pl.ds(8 * a, 8)
         window = [near[c, rows, :] for c in range(tiles)]
         if 4 * (PARTS - 1) * a >= SPAN:
-            more = window_tiles(q, a, free, packed, lambda p: p >= STARTS[FAR])
-            window = [tile + part for tile, part in zip(window, more)]
+            more = window_tiles(q, a, free, packed, lambda p: p >= STARTS[FAR], FAR)
+            window = [
+                tile if part is None else tile + part
+                for tile, part in zip(window, more)
+            ]
         for c, tile in enumerate(window):
             held[c, rows, :] = tile
             top = jnp.maximum(top, jnp.abs(tile))

time: 37.8 us -> 37.7 us (level)
  no operation moved by 1% of the time
where the time goes in v16:
time: 37.7 us; the launch traced here: 37.4 us
  blocking collectives  18.1 us (48%)
  starting transfers between devices  8.9 us (24%)
  Pallas kernels  5.38 us (14%)
  waiting for transfers between devices  4.96 us (13%)
    all_to_all x1, blocking collectives, per_device(): lined = lax.all_to_all(lined, 'chan', 0, 0, tiled=True)  18.1 us
    ppermute x5, starting transfers between devices, later(): return lax.ppermute(block, ('chan', 'tm'), route)  8.9 us
    ppermute x5, waiting for transfers between devices, later(): return lax.ppermute(block, ('chan', 'tm'), route)  4.96 us
    pallas_call x1, Pallas kernels, local_plane(): pl.pallas_call(local_kernel, in_specs=[pl.BlockSpec(memory_space=pltpu.HB...  2.61 us
    pallas_call x1, Pallas kernels, final_boxcars(): pl.pallas_call(final_kernel, in_specs=[pl.BlockSpec(memory_space=pltpu.VM...  2.01 us
  transfers between devices with their start and end apart: 5, of which 1 were waited for; matrix products, arithmetic and copies ran while one was open for 0% of the time, Pallas kernels for 1%

profile of v16, /device:TPU:4, one launch (start us, length us, event | category | flops | bytes accessed | tf_op | source)
XLA Modules:
  0.0 37.4 jit_solution(7391891567099556681)
XLA Ops:
  0.0 0.0 copy-start
  0.0 2.6 %local_plane.1 = (f32[64,8,128]{2,1,0:T(8,128)S(1)}, s32[31,8,128]{2,1,0:T(8,128)S(1)}, s32[20,8,128]{2,1,0:T(8,128)S(1)}, s32[16,8,128]{2,1,0:T(8,128)S(1)}, s3...) custom-call(f32[1,512]{1,0:T(1,128)} %bitcast.7, bf16[2,512,512]{2,1,0:T(8,128)(2,1)} %x_hbm.1), custom_call_target="tpu_custom_call" | custom-call | tf_op jit(solution)/shard_map/local_plane/pallas_call | solution.py:272
  2.6 1.9 %collective-permute-start = (s32[31,8,128]{2,1,0:T(8,128)S(1)}, s32[31,8,128]{2,1,0:T(8,128)S(1)}, u32[]{:S(2)}, u32[]{:S(2)}) collective-permute-start(s32[31,8,128]{2,1,0:T(8,128)S(1)} %get-tuple-element.12), channel_id=1, source_target_pairs={{0,1},{1,2},{2,3},{3,4},{4,5},{5,6},{6,7},{8,9},{9,10},{10,11},{11... | collective-permute-start | bytes 380936 | tf_op jit(solution)/shard_map/ppermute | solution.py:499
  4.6 3.1 %collective-permute-start.1 = (s32[20,8,128]{2,1,0:T(8,128)S(1)}, s32[20,8,128]{2,1,0:T(8,128)S(1)}, u32[]{:S(2)}, u32[]{:S(2)}) collective-permute-start(s32[20,8,128]{2,1,0:T(8,128)S(1)} %get-tuple-element.13), channel_id=1, source_target_pairs={{0,2},{1,3},{2,4},{3,5},{4,6},{5,7},{8,10},{9,11},{10,12},{11,13},... | collective-permute-start | bytes 245768 | tf_op jit(solution)/shard_map/ppermute | solution.py:499
  7.7 1.9 %collective-permute-start.2 = (s32[16,8,128]{2,1,0:T(8,128)S(1)}, s32[16,8,128]{2,1,0:T(8,128)S(1)}, u32[]{:S(2)}, u32[]{:S(2)}) collective-permute-start(s32[16,8,128]{2,1,0:T(8,128)S(1)} %get-tuple-element.14), channel_id=1, source_target_pairs={{0,3},{1,4},{2,5},{3,6},{4,7},{8,11},{9,12},{10,13},{11,14},{12,15... | collective-permute-start | bytes 196616 | tf_op jit(solution)/shard_map/ppermute | solution.py:499
  9.6 1.3 %collective-permute-start.3 = (s32[9,8,128]{2,1,0:T(8,128)S(1)}, s32[9,8,128]{2,1,0:T(8,128)S(1)}, u32[]{:S(2)}, u32[]{:S(2)}) collective-permute-start(s32[9,8,128]{2,1,0:T(8,128)S(1)} %get-tuple-element.15), channel_id=1, source_target_pairs={{0,4},{1,5},{2,6},{3,7},{8,12},{9,13},{10,14},{11,15},{16,20},{17,... | collective-permute-start | bytes 110600 | tf_op jit(solution)/shard_map/ppermute | solution.py:499
  10.9 0.7 %collective-permute-start.4 = (s32[2,8,128]{2,1,0:T(8,128)S(1)}, s32[2,8,128]{2,1,0:T(8,128)S(1)}, u32[]{:S(2)}, u32[]{:S(2)}) collective-permute-start(s32[2,8,128]{2,1,0:T(8,128)S(1)} %get-tuple-element.16), channel_id=1, source_target_pairs={{0,5},{1,6},{2,7}} | collective-permute-start | bytes 24584 | tf_op jit(solution)/shard_map/ppermute | solution.py:499
  11.6 0.0 collective-permute-done.1.r2
  11.6 0.0 collective-permute-done.r1
  11.6 0.4 %gather_near.1.near = f32[5,128,128]{2,1,0:T(8,128)S(1)} custom-call(f32[64,8,128]{2,1,0:T(8,128)S(1)} %get-tuple-element.11.o0, s32[31,8,128]{2,1,0:T(8,128)S(1)} %collective-permute-done.r1, s32[20,8,128]{2,1,0:T(8,128)S(1)} %collective-permute-done.1.r2), custom_call_target="tpu_custom_call" | custom-call | flops 4194304 | bytes 4194304 | tf_op jit(solution)/shard_map/gather_near/pallas_call | solution.py:381
  12.0 0.0 collective-permute-done.4.r5
  12.0 5.0 %collective-permute-done.3.r4 = s32[9,8,128]{2,1,0:T(8,128)S(1)} collective-permute-done((s32[9,8,128]{2,1,0:T(8,128)S(1)}, s32[9,8,128]{2,1,0:T(8,128)S(1)}, u32[]{:S(2)}, u32[]{:S(2)}) %collective-permute-start.3) | collective-permute-done | bytes 36896 | tf_op jit(solution)/shard_map/ppermute | solution.py:499
  16.9 0.0 collective-permute-done.2.r3
  16.9 0.4 gather_far.1
  17.3 18.1 %all_to_all.5 = s32[32,1,1280]{2,1,0:T(1,128)S(1)} all-to-all(s32[32,1,1280]{2,1,0:T(1,128)S(1)} %bitcast.4), channel_id=1, replica_groups=mesh['chan'=32,'tm'=8] {'chan'}, dimensions={0} | all-to-all | bytes 327680 | tf_op jit(solution)/shard_map/all_to_all | solution.py:508
  35.4 0.0 copy-done
  35.4 2.0 %final_boxcars.1 = f32[2,6,64,512]{3,2,1,0:T(8,128)} custom-call(s32[1,6]{1,0:T(1,128)S(1)} %bitcast.6, s32[320,128]{1,0:T(8,128)S(1)} %bitcast.5), custom_call_target="tpu_custom_call" | custom-call | tf_op jit(solution)/shard_map/final_boxcars/pallas_call | solution.py:476
Async XLA Ops:
  0.0 35.4 %copy-start = (s32[6]{0:T(128)S(1)}, s32[6]{0:T(128)}, u32[]{:S(2)}) copy-start(s32[6]{0:T(128)} %param.5) | copy-start | bytes 76
  2.6 8.9 %collective-permute-start = (s32[31,8,128]{2,1,0:T(8,128)S(1)}, s32[31,8,128]{2,1,0:T(8,128)S(1)}, u32[]{:S(2)}, u32[]{:S(2)}) collective-permute-start(s32[31,8,128]{2,1,0:T(8,128)S(1)} %get-tuple-element.12), channel_id=1, source_target_pairs={{0,1},{1,2},{2,3},{3,4},{4,5},{5,6},{6,7},{8,9},{9,10},{10,11},{11... | collective-permute-start | bytes 380936 | tf_op jit(solution)/shard_map/ppermute | solution.py:499
  4.6 7.0 %collective-permute-start.1 = (s32[20,8,128]{2,1,0:T(8,128)S(1)}, s32[20,8,128]{2,1,0:T(8,128)S(1)}, u32[]{:S(2)}, u32[]{:S(2)}) collective-permute-start(s32[20,8,128]{2,1,0:T(8,128)S(1)} %get-tuple-element.13), channel_id=1, source_target_pairs={{0,2},{1,3},{2,4},{3,5},{4,6},{5,7},{8,10},{9,11},{10,12},{11,13},... | collective-permute-start | bytes 245768 | tf_op jit(solution)/shard_map/ppermute | solution.py:499
  7.7 9.3 %collective-permute-start.2 = (s32[16,8,128]{2,1,0:T(8,128)S(1)}, s32[16,8,128]{2,1,0:T(8,128)S(1)}, u32[]{:S(2)}, u32[]{:S(2)}) collective-permute-start(s32[16,8,128]{2,1,0:T(8,128)S(1)} %get-tuple-element.14), channel_id=1, source_target_pairs={{0,3},{1,4},{2,5},{3,6},{4,7},{8,11},{9,12},{10,13},{11,14},{12,15... | collective-permute-start | bytes 196616 | tf_op jit(solution)/shard_map/ppermute | solution.py:499
  9.6 7.4 %collective-permute-start.3 = (s32[9,8,128]{2,1,0:T(8,128)S(1)}, s32[9,8,128]{2,1,0:T(8,128)S(1)}, u32[]{:S(2)}, u32[]{:S(2)}) collective-permute-start(s32[9,8,128]{2,1,0:T(8,128)S(1)} %get-tuple-element.15), channel_id=1, source_target_pairs={{0,4},{1,5},{2,6},{3,7},{8,12},{9,13},{10,14},{11,15},{16,20},{17,... | collective-permute-start | bytes 110600 | tf_op jit(solution)/shard_map/ppermute | solution.py:499
  10.9 1.1 %collective-permute-start.4 = (s32[2,8,128]{2,1,0:T(8,128)S(1)}, s32[2,8,128]{2,1,0:T(8,128)S(1)}, u32[]{:S(2)}, u32[]{:S(2)}) collective-permute-start(s32[2,8,128]{2,1,0:T(8,128)S(1)} %get-tuple-element.16), channel_id=1, source_target_pairs={{0,5},{1,6},{2,7}} | collective-permute-start | bytes 24584 | tf_op jit(solution)/shard_map/ppermute | solution.py:499
